TPU v7x, 32 devices: a whole 2x2x4 slice. The times are simulated.
32 devices in a mesh: dp: 8 (over z, y), tensor: 4 (over x, core).
Axes of the slice: x: 2, y: 2, z: 4, core: 2. Of those that a mesh axis runs over, the one named last changes fastest.
Arguments:
- policy_rows: bfloat16 [4096, 2048], P('dp'), may hold values from -6 to 6
- frozen_rows: bfloat16 [4096, 2048], P('dp'), may hold values from -6 to 6
- next_tokens: int32 [8, 256], replicated, may hold values from 0 to 50303
- desirable: int32 [8], replicated, may hold values 0 or 1
- answer_len: int32 [8], replicated, may hold values from 64 to 256, as said below
- partner: int32 [8], replicated, may hold values from 0 to 7, each once
- norms_copy: bfloat16 [4, 2048], P(None, 'dp')
- attend_in_copy: bfloat16 [3, 2048, 2048], P(None, 'dp', 'tensor'), may hold values from -0.125 to 0.125
- attend_out_copy: bfloat16 [2048, 2048], P('tensor', 'dp'), may hold values from -2 to 2
- expand_copy: bfloat16 [2048, 8192], P('dp', 'tensor'), may hold values from -0.125 to 0.125
- contract_copy: bfloat16 [8192, 2048], P('tensor', 'dp'), may hold values from -0.0625 to 0.0625
- norms_master: float32 [4, 2048], P(None, 'dp')
- attend_in_master: float32 [3, 2048, 2048], P(None, 'dp', 'tensor'), may hold values from -0.125 to 0.125
- attend_out_master: float32 [2048, 2048], P('tensor', 'dp'), may hold values from -2 to 2
- expand_master: float32 [2048, 8192], P('dp', 'tensor'), may hold values from -0.125 to 0.125
- contract_master: float32 [8192, 2048], P('tensor', 'dp'), may hold values from -0.0625 to 0.0625
- norms_first: float32 [4, 2048], P(None, 'dp'), may hold values from -0.015625 to 0.015625
- attend_in_first: float32 [3, 2048, 2048], P(None, 'dp', 'tensor'), may hold values from -0.0068359375 to 0.0068359375
- attend_out_first: float32 [2048, 2048], P('tensor', 'dp'), may hold values from -0.0008544922 to 0.0008544922
- expand_first: float32 [2048, 8192], P('dp', 'tensor'), may hold values from -0.0008544922 to 0.0008544922
- contract_first: float32 [8192, 2048], P('tensor', 'dp'), may hold values from -0.001953125 to 0.001953125
- norms_second: float32 [4, 2048], P(None, 'dp'), may hold values from 5.4931643e-06 to 2.166748e-05
- attend_in_second: float32 [3, 2048, 2048], P(None, 'dp', 'tensor'), may hold values from 8.087158e-07 to 3.2043456e-06
- attend_out_second: float32 [2048, 2048], P('tensor', 'dp'), may hold values from 2.4414062e-09 to 9.765625e-09
- expand_second: float32 [2048, 8192], P('dp', 'tensor'), may hold values from 1.953125e-09 to 7.8125e-09
- contract_second: float32 [8192, 2048], P('tensor', 'dp'), may hold values from 1.2207031e-08 to 4.8828124e-08
- frozen_norms: float32 [4, 2048], replicated
- frozen_in: bfloat16 [3, 2048, 2048], P(None, None, 'tensor'), may hold values from -0.125 to 0.125
- frozen_out: bfloat16 [2048, 2048], P('tensor'), may hold values from -2 to 2
- frozen_expand: bfloat16 [2048, 8192], P(None, 'tensor'), may hold values from -0.125 to 0.125
- frozen_contract: bfloat16 [8192, 2048], P('tensor'), may hold values from -0.0625 to 0.0625
- vocab_table: bfloat16 [2048, 50304], P(None, 'tensor')
Outputs:
- mixed: bfloat16 [4096, 2048], P('dp')
- input_grad: float32 [4096, 2048], P('dp')
- loss: float32 [1], replicated
- norms_next: float32 [4, 2048], P(None, 'dp')
- attend_in_next: float32 [3, 2048, 2048], P(None, 'dp', 'tensor')
- attend_out_next: float32 [2048, 2048], P('tensor', 'dp')
- expand_next: float32 [2048, 8192], P('dp', 'tensor')
- contract_next: float32 [8192, 2048], P('tensor', 'dp')
- norms_first_next: float32 [4, 2048], P(None, 'dp')
- attend_in_first_next: float32 [3, 2048, 2048], P(None, 'dp', 'tensor')
- attend_out_first_next: float32 [2048, 2048], P('tensor', 'dp')
- expand_first_next: float32 [2048, 8192], P('dp', 'tensor')
- contract_first_next: float32 [8192, 2048], P('tensor', 'dp')
- norms_second_next: float32 [4, 2048], P(None, 'dp')
- attend_in_second_next: float32 [3, 2048, 2048], P(None, 'dp', 'tensor')
- attend_out_second_next: float32 [2048, 2048], P('tensor', 'dp')
- expand_second_next: float32 [2048, 8192], P('dp', 'tensor')
- contract_second_next: float32 [8192, 2048], P('tensor', 'dp')
Inputs may be any that keep to these rules, and one draw needn't show every extreme that they name: 1 marks a desirable completion, 0 an undesirable one. `answer_len`: one example has 256 tokens in its completion and another 256 // 4. `partner`: a permutation of the examples.
All inputs are finite; a program needn't handle non-finite values.
Results may differ from a plain program's by a relative error of at most 0.02.
Values may be sent and summed in bfloat16 or wider, within the bound.
A program may use at most 384 MiB of HBM per device.

v0:
```python
import jax
import jax.numpy as jnp
from jax import lax
from jax.sharding import PartitionSpec as P

D = 2048
HD = 128
ROT = 32
HALF = 256
STEP = 10


NORM_EPSILON = 1e-05
KTO_BETA = 2.0
ADAM_ONE = 0.9
ADAM_TWO = 0.95
ADAM_EPSILON = 1e-08
DECAY_RATE = 0.1
NORM_RATE = 0.3
ROPE_BASE = 10000.0
MASKED = -1e30


def shortened(x):
    return jax.tree.map(lambda a: a.astype(jnp.bfloat16) if a.dtype == jnp.float32 else a, x)


def joined(value, axis, join):
    pieces = jax.tree.map(lambda part: lax.all_gather(part, axis), value)
    head = jax.tree.map(lambda part: part[0], pieces)
    tail = jax.tree.map(lambda part: part[1:], pieces)
    total, _ = lax.scan(lambda total, slab: (join(total, slab), None), head, tail)
    return total


def normalize(values):
    centre = jnp.mean(values, axis=-1, keepdims=True)
    centred = values - centre
    inverse_scale = lax.rsqrt(jnp.mean(centred * centred, axis=-1, keepdims=True) + NORM_EPSILON)
    return (centred * inverse_scale, inverse_scale)


def normalize_back(upstream, unit, inverse_scale):
    return inverse_scale * (
        upstream
        - jnp.mean(upstream, axis=-1, keepdims=True)
        - unit * jnp.mean(upstream * unit, axis=-1, keepdims=True)
    )


def layout(half):
    position_index = jnp.arange(3 * half, dtype=jnp.int32)
    place = jnp.where(position_index < 2 * half, position_index, position_index - half)
    group = jnp.where(position_index < half, 0, jnp.where(position_index < 2 * half, 1, 2))
    allowed = (place[None, :] <= place[:, None]) & (
        (group[None, :] == 0) | (group[None, :] == group[:, None])
    )
    freqs = ROPE_BASE ** (-jnp.arange(ROT // 2, dtype=jnp.float32) * 2.0 / ROT)
    angles = place.astype(jnp.float32)[:, None] * freqs[None, :]
    return (allowed, jnp.cos(angles)[:, None, :], jnp.sin(angles)[:, None, :])


def rotate(heads, cosines, sines):
    first = heads[..., : ROT // 2]
    second = heads[..., ROT // 2 : ROT]
    return jnp.concatenate(
        [first * cosines - second * sines, second * cosines + first * sines, heads[..., ROT:]],
        axis=-1,
    )


def rotate_back(upstream, cosines, sines):
    first = upstream[..., : ROT // 2]
    second = upstream[..., ROT // 2 : ROT]
    return jnp.concatenate(
        [first * cosines + second * sines, second * cosines - first * sines, upstream[..., ROT:]],
        axis=-1,
    )


def block_part(rows_full, norms, attend_in, attend_out, expand, contract, allowed, cosines, sines):
    count = rows_full.shape[0]
    heads = attend_in.shape[2] // HD
    unit, inverse_scale = normalize(rows_full)
    first_in = (unit * norms[0] + norms[1]).astype(jnp.bfloat16)
    second_in = (unit * norms[2] + norms[3]).astype(jnp.bfloat16)

    def project(which):
        return jnp.dot(first_in, attend_in[which], preferred_element_type=jnp.float32).reshape(
            count, heads, HD
        )

    query = rotate(project(0), cosines, sines).astype(jnp.bfloat16)
    keys = rotate(project(1), cosines, sines).astype(jnp.bfloat16)
    values = project(2).astype(jnp.bfloat16)
    scores = jnp.einsum("qhd,khd->hqk", query, keys, preferred_element_type=jnp.float32) * HD ** (
        -0.5
    )
    scores = jnp.where(allowed[None], scores, MASKED)
    peak = jnp.max(scores, axis=-1, keepdims=True)
    raised = jnp.exp(scores - peak)
    total = jnp.sum(raised, axis=-1, keepdims=True)
    chance = (raised / total).astype(jnp.bfloat16)
    log_total = peak + jnp.log(total)
    attended = (
        jnp.einsum("hqk,khd->qhd", chance, values, preferred_element_type=jnp.float32)
        .reshape(count, heads * HD)
        .astype(jnp.bfloat16)
    )
    hidden_pre = jnp.dot(second_in, expand, preferred_element_type=jnp.float32)
    hidden_in = jax.nn.gelu(hidden_pre, approximate=False).astype(jnp.bfloat16)
    partial_value = jnp.dot(attended, attend_out, preferred_element_type=jnp.float32) + jnp.dot(
        hidden_in, contract, preferred_element_type=jnp.float32
    )
    return (
        partial_value,
        (
            unit,
            inverse_scale,
            first_in,
            second_in,
            query,
            keys,
            values,
            log_total,
            attended,
            hidden_pre,
            hidden_in,
        ),
    )


def block_back(upstream, kept, attend_in, attend_out, expand, contract, allowed, cosines, sines):
    (
        unit,
        inverse_scale,
        first_in,
        second_in,
        query,
        keys,
        values,
        log_total,
        attended,
        hidden_pre,
        hidden_in,
    ) = kept
    count = upstream.shape[0]
    heads = attend_in.shape[2] // HD
    scale = HD ** (-0.5)
    branch_low = upstream.astype(jnp.bfloat16)
    back_hidden = jnp.einsum("rd,fd->rf", branch_low, contract, preferred_element_type=jnp.float32)
    grad_contract = jnp.einsum(
        "rf,rd->fd", hidden_in, branch_low, preferred_element_type=jnp.float32
    )
    unused, gelu_pull = jax.vjp(lambda inner: jax.nn.gelu(inner, approximate=False), hidden_pre)
    back_expand = gelu_pull(back_hidden)[0].astype(jnp.bfloat16)
    grad_expand = jnp.einsum(
        "rd,rf->df", second_in, back_expand, preferred_element_type=jnp.float32
    )
    back_second = jnp.einsum("rf,df->rd", back_expand, expand, preferred_element_type=jnp.float32)
    back_attended = (
        jnp.einsum("rd,ed->re", branch_low, attend_out, preferred_element_type=jnp.float32)
        .astype(jnp.bfloat16)
        .reshape(count, heads, HD)
    )
    grad_attend_out = jnp.einsum(
        "re,rd->ed", attended, branch_low, preferred_element_type=jnp.float32
    )
    scores = jnp.einsum("qhd,khd->hqk", query, keys, preferred_element_type=jnp.float32) * scale
    scores = jnp.where(allowed[None], scores, MASKED)
    chance = jnp.exp(scores - log_total)
    chance_low = chance.astype(jnp.bfloat16)
    back_chance = jnp.einsum(
        "qhd,khd->hqk", back_attended, values, preferred_element_type=jnp.float32
    )
    back_values = jnp.einsum(
        "hqk,qhd->khd", chance_low, back_attended, preferred_element_type=jnp.float32
    )
    back_scores = (
        chance * (back_chance - jnp.sum(chance * back_chance, axis=-1, keepdims=True))
    ).astype(jnp.bfloat16)
    back_query = (
        jnp.einsum("hqk,khd->qhd", back_scores, keys, preferred_element_type=jnp.float32) * scale
    )
    back_keys = (
        jnp.einsum("hqk,qhd->khd", back_scores, query, preferred_element_type=jnp.float32) * scale
    )
    lowered = (
        rotate_back(back_query, cosines, sines).astype(jnp.bfloat16).reshape(count, heads * HD),
        rotate_back(back_keys, cosines, sines).astype(jnp.bfloat16).reshape(count, heads * HD),
        back_values.astype(jnp.bfloat16).reshape(count, heads * HD),
    )
    grad_attend_in = jnp.stack(
        [
            jnp.einsum("rd,re->de", first_in, piece, preferred_element_type=jnp.float32)
            for piece in lowered
        ]
    )
    back_first = jnp.einsum(
        "re,de->rd", lowered[0], attend_in[0], preferred_element_type=jnp.float32
    )
    back_first = back_first + jnp.einsum(
        "re,de->rd", lowered[1], attend_in[1], preferred_element_type=jnp.float32
    )
    back_first = back_first + jnp.einsum(
        "re,de->rd", lowered[2], attend_in[2], preferred_element_type=jnp.float32
    )
    return (back_first, back_second, grad_attend_in, grad_attend_out, grad_expand, grad_contract)


def head_part(out_rows, table, local_targets):
    unit, inverse_scale = normalize(out_rows)
    unit_low = unit.astype(jnp.bfloat16)
    logits = jnp.dot(unit_low, table, preferred_element_type=jnp.float32)
    peak = jnp.max(logits, axis=-1)
    total = jnp.sum(jnp.exp(logits - peak[:, None]), axis=-1)
    target_hit = jnp.arange(table.shape[1], dtype=jnp.int32)[None, :] == local_targets[:, None]
    picked = jnp.sum(jnp.where(target_hit, logits, 0.0), axis=-1)
    return ((peak, total, picked), (unit, inverse_scale, logits, target_hit))


def combine_stats(first, second):
    peak = jnp.maximum(first[0], second[0])
    total = first[1] * jnp.exp(first[0] - peak) + second[1] * jnp.exp(second[0] - peak)
    return (peak, total, first[2] + second[2])


def bring_pairs(policy_tail, frozen_tail, partner, groups):
    width = policy_tail.shape[1]
    spread = (
        lax.all_to_all(
            policy_tail.reshape(groups, -1, width), "dp", split_axis=0, concat_axis=0, tiled=True
        ),
        lax.all_to_all(
            frozen_tail.reshape(groups, -1, width), "dp", split_axis=0, concat_axis=0, tiled=True
        ),
    )
    landed = (
        lax.all_to_all(
            jnp.take(spread[0], partner, axis=0), "dp", split_axis=0, concat_axis=0, tiled=True
        ),
        lax.all_to_all(
            jnp.take(spread[1], partner, axis=0), "dp", split_axis=0, concat_axis=0, tiled=True
        ),
    )
    return (landed[0].reshape(-1, width), landed[1].reshape(-1, width))


def return_pairs(borrowed_back, inverse, groups):
    width = borrowed_back.shape[1]
    spread = lax.all_to_all(
        borrowed_back.reshape(groups, -1, width).astype(jnp.bfloat16),
        "dp",
        split_axis=0,
        concat_axis=0,
        tiled=True,
    ).astype(jnp.float32)
    landed = lax.all_to_all(
        shortened(jnp.take(spread, inverse, axis=0)), "dp", split_axis=0, concat_axis=0, tiled=True
    )
    return landed.reshape(-1, width)


def adamw_step(master, first, second, gradient, rate, decay):
    new_first = ADAM_ONE * first + (1.0 - ADAM_ONE) * gradient
    new_second = ADAM_TWO * second + (1.0 - ADAM_TWO) * gradient * gradient
    ratio = (
        new_first
        / (1.0 - ADAM_ONE**STEP)
        / (jnp.sqrt(new_second / (1.0 - ADAM_TWO**STEP)) + ADAM_EPSILON)
    )
    return (master - rate * (ratio + decay * master), new_first, new_second)


def per_device(
    policy_rows,
    frozen_rows,
    next_tokens,
    desirable,
    answer_len,
    partner,
    norms_copy,
    attend_in_copy,
    attend_out_copy,
    expand_copy,
    contract_copy,
    norms_master,
    attend_in_master,
    attend_out_master,
    expand_master,
    contract_master,
    norms_first,
    attend_in_first,
    attend_out_first,
    expand_first,
    contract_first,
    norms_second,
    attend_in_second,
    attend_out_second,
    expand_second,
    contract_second,
    frozen_norms,
    frozen_in,
    frozen_out,
    frozen_expand,
    frozen_contract,
    vocab_table,
):
    groups = lax.axis_size("dp")
    own_index = lax.axis_index("dp")
    half = policy_rows.shape[0] // 2
    width = policy_rows.shape[1]
    inverse = jnp.zeros_like(partner).at[partner].set(jnp.arange(groups, dtype=jnp.int32))
    other_index = partner[own_index]
    norms_all, attend_in, attend_out, expand, contract = (
        lax.all_gather(norms_copy, "dp", axis=1, tiled=True),
        lax.all_gather(attend_in_copy, "dp", axis=1, tiled=True),
        lax.all_gather(attend_out_copy, "dp", axis=1, tiled=True),
        lax.all_gather(expand_copy, "dp", axis=0, tiled=True),
        lax.all_gather(contract_copy, "dp", axis=1, tiled=True),
    )
    norms_full = norms_all.astype(jnp.float32)
    other_policy, other_frozen = bring_pairs(
        policy_rows[half:], frozen_rows[half:], partner, groups
    )
    allowed, cosines, sines = layout(half)
    policy_work = jnp.concatenate([policy_rows, other_policy], axis=0).astype(jnp.float32)
    frozen_work = jnp.concatenate([frozen_rows, other_frozen], axis=0).astype(jnp.float32)
    policy_part, kept = block_part(
        policy_work, norms_full, attend_in, attend_out, expand, contract, allowed, cosines, sines
    )
    frozen_part, unused = block_part(
        frozen_work,
        frozen_norms,
        frozen_in,
        frozen_out,
        frozen_expand,
        frozen_contract,
        allowed,
        cosines,
        sines,
    )
    policy_branch, frozen_branch = (
        lax.psum(policy_part.astype(jnp.bfloat16), "tensor").astype(jnp.float32),
        lax.psum(frozen_part.astype(jnp.bfloat16), "tensor").astype(jnp.float32),
    )
    policy_out = policy_work + policy_branch
    frozen_result = frozen_work + frozen_branch
    vocab_local = vocab_table.shape[1]
    targets = (
        jnp.concatenate([next_tokens[own_index], next_tokens[other_index]])
        - lax.axis_index("tensor") * vocab_local
    )
    policy_stats, head_kept = head_part(policy_out[half:], vocab_table, targets)
    frozen_stats, unused_head = head_part(frozen_result[half:], vocab_table, targets)
    peak, total, picked = joined(
        (
            jnp.stack([policy_stats[0], frozen_stats[0]]),
            jnp.stack([policy_stats[1], frozen_stats[1]]),
            jnp.stack([policy_stats[2], frozen_stats[2]]),
        ),
        "tensor",
        combine_stats,
    )
    log_chance = picked - peak - jnp.log(total)
    steps = jnp.arange(half, dtype=jnp.int32)
    own_count = answer_len[own_index]
    other_count = answer_len[other_index]
    own_live = (steps < own_count).astype(jnp.float32)
    other_live = (steps < other_count).astype(jnp.float32)
    own_total = own_count.astype(jnp.float32)
    other_total = other_count.astype(jnp.float32)
    own_mean = jnp.sum(log_chance[:, :half] * own_live, axis=1) / own_total
    other_mean = jnp.sum(log_chance[:, half:] * other_live, axis=1) / other_total
    reward = own_mean[0] - own_mean[1]
    drift = lax.psum(other_mean[0] - other_mean[1], "dp") / groups
    penalty = jax.nn.softplus(drift)
    sign = (2 * desirable[own_index] - 1).astype(jnp.float32)
    settled = jax.nn.sigmoid(KTO_BETA * sign * (reward - penalty))
    slope = KTO_BETA * sign * settled * (1.0 - settled)
    slope_total, loss_total = lax.psum((slope, 1.0 - settled), "dp")
    pull = slope_total * jax.nn.sigmoid(drift) / groups
    row_weight = jnp.concatenate([-slope * own_live / own_total, pull * other_live / other_total])
    unit_out, inverse_out, logits, target_hit = head_kept
    softmax_part = jnp.exp(logits - peak[0][:, None]) / total[0][:, None]
    back_logits = (row_weight[:, None] * (target_hit.astype(jnp.float32) - softmax_part)).astype(
        jnp.bfloat16
    )
    back_unit = lax.psum(
        jnp.einsum(
            "sv,dv->sd", back_logits, vocab_table, preferred_element_type=jnp.float32
        ).astype(jnp.bfloat16),
        "tensor",
    ).astype(jnp.float32)
    back_out = jnp.concatenate(
        [jnp.zeros((half, width), jnp.float32), normalize_back(back_unit, unit_out, inverse_out)],
        axis=0,
    )
    back_first, back_second, grad_attend_in, grad_attend_out, grad_expand, grad_contract = (
        block_back(back_out, kept, attend_in, attend_out, expand, contract, allowed, cosines, sines)
    )
    back_first, back_second = (
        lax.psum(back_first.astype(jnp.bfloat16), "tensor").astype(jnp.float32),
        lax.psum(back_second.astype(jnp.bfloat16), "tensor").astype(jnp.float32),
    )
    unit_rows, inverse_scale = (kept[0], kept[1])
    grad_norms = jnp.stack(
        [
            jnp.sum(back_first * unit_rows, axis=0),
            jnp.sum(back_first, axis=0),
            jnp.sum(back_second * unit_rows, axis=0),
            jnp.sum(back_second, axis=0),
        ]
    )
    back_work = back_out + normalize_back(
        back_first * norms_full[0] + back_second * norms_full[2], unit_rows, inverse_scale
    )
    returned = return_pairs(back_work[2 * half :], inverse, groups)
    input_grad = jnp.concatenate([back_work[:half], back_work[half : 2 * half] + returned], axis=0)
    summed = (
        lax.psum_scatter(
            grad_norms.astype(jnp.bfloat16), "dp", scatter_dimension=1, tiled=True
        ).astype(jnp.float32),
        lax.psum_scatter(
            grad_attend_in.astype(jnp.bfloat16), "dp", scatter_dimension=1, tiled=True
        ).astype(jnp.float32),
        lax.psum_scatter(
            grad_attend_out.astype(jnp.bfloat16), "dp", scatter_dimension=1, tiled=True
        ).astype(jnp.float32),
        lax.psum_scatter(
            grad_expand.astype(jnp.bfloat16), "dp", scatter_dimension=0, tiled=True
        ).astype(jnp.float32),
        lax.psum_scatter(
            grad_contract.astype(jnp.bfloat16), "dp", scatter_dimension=1, tiled=True
        ).astype(jnp.float32),
    )
    matrix_rate = 0.5 * D ** (-0.5)
    out_rate = 0.5 * max(D // HALF, 1) ** (-0.5)
    masters = (norms_master, attend_in_master, attend_out_master, expand_master, contract_master)
    firsts = (norms_first, attend_in_first, attend_out_first, expand_first, contract_first)
    seconds = (norms_second, attend_in_second, attend_out_second, expand_second, contract_second)
    rates = (NORM_RATE, matrix_rate, out_rate, matrix_rate, matrix_rate)
    decays = (0.0, DECAY_RATE, DECAY_RATE, DECAY_RATE, DECAY_RATE)
    updated = [
        adamw_step(master, first, second, gradient, rate, decay)
        for master, first, second, gradient, rate, decay in zip(
            masters, firsts, seconds, summed, rates, decays
        )
    ]
    return (
        policy_out[: 2 * half].astype(jnp.bfloat16),
        input_grad,
        jnp.reshape(loss_total, (1,)),
        updated[0][0],
        updated[1][0],
        updated[2][0],
        updated[3][0],
        updated[4][0],
        updated[0][1],
        updated[1][1],
        updated[2][1],
        updated[3][1],
        updated[4][1],
        updated[0][2],
        updated[1][2],
        updated[2][2],
        updated[3][2],
        updated[4][2],
    )


def solution(mesh):
    return jax.shard_map(
        per_device,
        mesh=mesh,
        in_specs=(
            P("dp", None),
            P("dp", None),
            P(),
            P(),
            P(),
            P(),
            P(None, "dp"),
            P(None, "dp", "tensor"),
            P("tensor", "dp"),
            P("dp", "tensor"),
            P("tensor", "dp"),
            P(None, "dp"),
            P(None, "dp", "tensor"),
            P("tensor", "dp"),
            P("dp", "tensor"),
            P("tensor", "dp"),
            P(None, "dp"),
            P(None, "dp", "tensor"),
            P("tensor", "dp"),
            P("dp", "tensor"),
            P("tensor", "dp"),
            P(None, "dp"),
            P(None, "dp", "tensor"),
            P("tensor", "dp"),
            P("dp", "tensor"),
            P("tensor", "dp"),
            P(),
            P(None, None, "tensor"),
            P("tensor", None),
            P(None, "tensor"),
            P("tensor", None),
            P(None, "tensor"),
        ),
        out_specs=(
            P("dp", None),
            P("dp", None),
            P(),
            P(None, "dp"),
            P(None, "dp", "tensor"),
            P("tensor", "dp"),
            P("dp", "tensor"),
            P("tensor", "dp"),
            P(None, "dp"),
            P(None, "dp", "tensor"),
            P("tensor", "dp"),
            P("dp", "tensor"),
            P("tensor", "dp"),
            P(None, "dp"),
            P(None, "dp", "tensor"),
            P("tensor", "dp"),
            P("dp", "tensor"),
            P("tensor", "dp"),
        ),
        check_vma=False,
    )
```

profile of v0, /device:TPU:0, one launch (start us, length us, event | category | flops | bytes accessed | tf_op | source)
XLA Modules:
  0.0 1673.4 jit_solution(10166293399012540041)
XLA Ops:
  11.7 7.3 all-to-all-start
  21.4 45.9 %all-to-all-done = bf16[8,32,2048]{2,1,0:T(8,128)(2,1)S(1)} async-done(((bf16[8,32,2048]{2,1,0:T(8,128)(2,1)}), bf16[8,32,2048]{2,1,0:T(8,128)(2,1)S(1)}, u32[]{:S(2)}, u32[]{:S(2)}) %all-to-all-start) | async-done | bytes 1048608 | tf_op jit(solution)/shard_map/all_to_all | solution.py:231
  67.3 5.0 all-to-all-start.2
  74.7 50.9 %all-to-all-done.2 = bf16[8,32,2048]{2,1,0:T(8,128)(2,1)} async-done(((bf16[8,32,2048]{2,1,0:T(8,128)(2,1)}), bf16[8,32,2048]{2,1,0:T(8,128)(2,1)}, u32[]{:S(2)}, u32[]{:S(2)}) %all-to-all-start.2) | async-done | bytes 1048608 | tf_op jit(solution)/shard_map/all_to_all | solution.py:234
  131.2 4.4 all-to-all-start.1
  136.2 5.7 slice_bitcast_fusion.2
  141.9 3.9 copy.74
  145.8 3.9 copy.73
  149.7 40.3 %all_gather.33 = bf16[4,2048]{1,0:T(4,128)(2,1)S(1)} all-gather(bf16[4,256]{1,0:T(4,128)(2,1)S(1)} %copy-done.71), channel_id=1, replica_groups=mesh['dp'=8,'tensor'=4] {'dp'}, dimensions={1}, use_global_device_ids=true | all-gather | bytes 18432 | tf_op jit(solution)/shard_map/all_gather | solution.py:316
  191.9 4.2 all-to-all-start.3
  201.6 37.1 %all-to-all-done.3 = bf16[8,32,2048]{2,1,0:T(8,128)(2,1)} async-done(((bf16[8,32,2048]{2,1,0:T(8,128)(2,1)}), bf16[8,32,2048]{2,1,0:T(8,128)(2,1)}, u32[]{:S(2)}, u32[]{:S(2)}) %all-to-all-start.3) | async-done | bytes 1048608 | tf_op jit(solution)/shard_map/all_to_all | solution.py:242
  257.5 32.0 %fusion.55 = f32[768,2048]{1,0:T(8,128)} fusion(bf16[2048,2048]{1,0:T(8,128)(2,1)} %param.66, bf16[2048,2048]{1,0:T(8,128)(2,1)} %param.65, f32[2048]{0:T(1024)S(1)} %bitcast.235, f32[2048]{0:T(1024)S(1)} %bitcast.236, f32[768]{0:T(1024)S(1)} %add_rsqrt_fusion, f32[768]{0:T(1024)S(1)} %broadcast_multiply_fusion.2, bf16[256,2048]{1,0:T(8,128)(2,1)} %bitcast.25, ...), kind=kOutput, calls=%fused_computation.127 | convolution fusion | flops 13001293824 | bytes 26236928 | tf_op jit(solution)/shard_map/dot_general | solution.py:112
  289.5 6.0 slice_bitcast_fusion.4
  295.5 3.9 copy.68
  299.4 3.9 copy.67
  303.3 4.5 fusion.59
  312.0 4.1 copy.66
  316.1 4.5 fusion.135
  329.3 9.1 fusion.232
  338.4 10.2 fusion.139
  348.6 6.6 add_convert_fusion.2
  355.2 27.1 %multiply_convert_fusion.3 = (bf16[768,2048]{1,0:T(8,128)(2,1)}, f32[768,2048]{1,0:T(8,128)}, f32[768,2048]{1,0:T(8,128)}) fusion(bf16[2048,2048]{1,0:T(8,128)(2,1)} %all-gather.15.cloned.1.call-done, f32[2048]{0:T(1024)S(1)} %bitcast.227, f32[2048]{0:T(1024)S(1)} %bitcast.215, f32[768]{0:T(1024)S(1)} %add_rsqrt_fusion.1, ...), kind=kOutput, calls=%fused_computation.88 | convolution fusion | flops 6558842880 | bytes 27285504 | tf_op jit(solution)/shard_map/dot_general | solution.py:110
  382.4 59.3 %all-gather.17.cloned.1.call-done = bf16[2048,2048]{1,0:T(8,128)(2,1)} async-done(((bf16[2048,256]{1,0:T(8,128)(2,1)}), bf16[2048,2048]{1,0:T(8,128)(2,1)}) %all-gather.17.cloned.1.call-update) | async-done | bytes 8388624 | tf_op jit(solution)/shard_map/all_gather | solution.py:320
  441.7 11.9 fusion.235
  453.5 39.3 %all-gather.13.cloned.1.call-done = bf16[512,2048]{1,0:T(8,128)(2,1)} async-done(((bf16[512,256]{1,0:T(8,128)(2,1)}), bf16[512,2048]{1,0:T(8,128)(2,1)}) %all-gather.13.cloned.1.call-update) | async-done | bytes 2097168 | tf_op jit(solution)/shard_map/all_gather | solution.py:318
  492.9 6.9 add_convert_fusion.5
  508.2 4.7 fusion.204
  513.0 105.0 %all-reduce.12.cloned.1.call-done = (bf16[768,2048]{1,0:T(8,128)(2,1)}, bf16[768,2048]{1,0:T(8,128)(2,1)}) async-done(((bf16[768,2048]{1,0:T(8,128)(2,1)}, bf16[768,2048]{1,0:T(8,128)(2,1)}), (bf16[768,2048]{1,0:T(8,128)(2,1)}, bf16[768,2048]{1,0:T(8,128)(2,1)})) %all-reduce.12.cloned.1.call-update) | async-done | bytes 6291472 | tf_op jit(solution)/shard_map/psum | solution.py:344
  630.1 37.0 %fusion.233 = (f32[512]{0:T(512)S(1)}, f32[512,12576]{0,1:T(8,128)}) fusion(bf16[2048,12576]{0,1:T(8,128)(2,1)} %param.67, f32[512]{0:T(512)S(1)} %add_rsqrt_fusion.2, f32[512]{0:T(512)S(1)} %broadcast_multiply_fusion.6, bf16[768,2048]{1,0:T(8,128)(2,1)} %get-tuple-element.94, f32[768,2048]{1,0:T(8,128)} %fusion.204), kind=kOutput, calls=%fused_computation.377 | convolution fusion | flops 26385465344 | bytes 83564544 | tf_op jit(solution)/shard_map/dot_general | solution.py:214
  667.0 36.3 %fusion.234 = (f32[512]{0:T(512)S(1)}, f32[512,12576]{0,1:T(8,128)}) fusion(bf16[2048,12576]{0,1:T(8,128)(2,1)} %param.67, f32[768,2048]{1,0:T(8,128)} %copy-done.3, f32[512]{0:T(512)S(1)} %add_rsqrt_fusion.3, f32[512]{0:T(512)S(1)} %broadcast_multiply_fusion.7), kind=kOutput, calls=%fused_computation.378 | convolution fusion | flops 26383368192 | bytes 81467392 | tf_op jit(solution)/shard_map/dot_general | solution.py:214
  703.4 19.6 %select_reduce_fusion.1 = (f32[512]{0:T(512)S(1)}, f32[512]{0:T(512)S(1)}, f32[512]{0:T(512)S(1)}, f32[512]{0:T(512)S(1)}) fusion(f32[512,12576]{0,1:T(8,128)} %get-tuple-element.171, s32[512]{0:T(512)S(1)} %add_subtract_fusion, f32[512]{0:T(512)S(1)} %get-tuple-element.170, f32[512,12576]{0,1:T(8,128)} %get-tuple-element.169, f32[512]{0:T(512)S(1)} %get-tuple-element.168), kind=kLoop, calls=%fused_computation.13 | loop fusion | flops 57948160 | bytes 51525632 | tf_op jit(solution)/shard_map/reduce_sum | solution.py:218
  723.0 5.2 all-gather.5
  728.2 5.2 all-gather.4
  733.4 5.2 all-gather.3
  740.8 22.5 %psum.58 = f32[]{:T(128)} all-reduce(f32[]{:T(128)} %bitcast.57), channel_id=1, replica_groups=mesh['dp'=8,'tensor'=4] {'dp'}, use_global_device_ids=true, to_apply=%region_24.26 | all-reduce | flops 1 | bytes 8 | tf_op jit(solution)/shard_map/psum | solution.py:376
  766.7 18.3 %all-reduce.1 = (f32[]{:T(128)}, f32[1]{0:T(128)}) all-reduce(f32[]{:T(128)S(6)} %mul.856, f32[1]{0:T(128)} %bitcast.69), channel_id=1, replica_groups=mesh['dp'=8,'tensor'=4] {'dp'}, use_global_device_ids=true, to_apply=%region_25.27 | all-reduce | flops 2 | bytes 16 | tf_op jit(solution)/shard_map/psum | solution.py:381
  786.4 37.9 %fusion.103 = bf16[512,2048]{1,0:T(8,128)(2,1)} fusion(bf16[2048,12576]{0,1:T(8,128)(2,1)} %param.67, f32[512,12576]{0,1:T(8,128)} %get-tuple-element.171, f32[512]{0:T(512)S(1)} %bitcast.240, f32[512]{0:T(512)S(1)} %bitcast.239, f32[512]{0:T(512)S(1)} %pad_maximum_fusion.23, s32[512]{0:T(512)S(1)} %add_subtract_fusion), kind=kOutput, calls=%fused_computation.178 | convolution fusion | flops 26419904512 | bytes 79372288 | tf_op jit(solution)/shard_map/sv,dv->sd/dot_general | solution.py:390
  824.4 49.4 %all-reduce.8.cloned.1.call-done = bf16[512,2048]{1,0:T(8,128)(2,1)} async-done(((bf16[512,2048]{1,0:T(8,128)(2,1)}), bf16[512,2048]{1,0:T(8,128)(2,1)}) %all-reduce.8.cloned.1.call-update) | async-done | bytes 2097168 | tf_op jit(solution)/shard_map/psum | solution.py:389
  873.8 4.5 convert_reduce_fusion.1
  887.3 4.6 multiply_reduce_fusion
  891.9 10.3 multiply_convert_fusion.2
  902.3 4.3 multiply_bitcast_fusion
  909.1 4.5 fusion.118
  913.6 4.5 fusion.120
  918.2 15.5 add_convert_fusion
  933.7 12.0 convolution_convert_fusion.2
  945.7 5.4 add_convert_fusion.1
  951.2 120.0 %all-reduce.10.cloned.1.call-done = (bf16[768,2048]{1,0:T(8,128)(2,1)}, bf16[768,2048]{1,0:T(8,128)(2,1)}) async-done(((bf16[768,2048]{1,0:T(8,128)(2,1)}, bf16[768,2048]{1,0:T(8,128)(2,1)}), (bf16[768,2048]{1,0:T(8,128)(2,1)}, bf16[768,2048]{1,0:T(8,128)(2,1)})) %all-reduce.10.cloned.1.call-update) | async-done | bytes 6291472 | tf_op jit(solution)/shard_map/psum | solution.py:404
  1071.2 7.7 fusion.51
  1084.9 5.5 convolution_convert_fusion.3
  1090.5 4.1 fusion.106
  1102.3 11.6 convolution_convert_fusion.1
  1114.0 11.6 convolution_convert_fusion
  1125.6 6.1 pad_add_fusion
  1135.6 5.6 all-to-all-start.4
  1142.0 31.2 %all-to-all-done.4 = bf16[8,32,2048]{2,1,0:T(8,128)(2,1)S(1)} async-done(((bf16[8,32,2048]{2,1,0:T(8,128)(2,1)}), bf16[8,32,2048]{2,1,0:T(8,128)(2,1)S(1)}, u32[]{:S(2)}, u32[]{:S(2)}) %all-to-all-start.4) | async-done | bytes 1048608 | tf_op jit(solution)/shard_map/all_to_all | solution.py:251
  1178.8 3.8 slice.372
  1184.3 50.2 %reduce-scatter.10.cloned.1.call-done = bf16[512,256]{1,0:T(8,128)(2,1)} async-done(((bf16[512,2048]{1,0:T(8,128)(2,1)}), bf16[512,256]{1,0:T(8,128)(2,1)}) %reduce-scatter.10.cloned.1.call-update) | async-done | bytes 262160 | tf_op jit(solution)/shard_map/reduce_scatter | solution.py:427
  1242.6 112.7 %reduce-scatter.8.cloned.1.call-done = bf16[3,256,512]{2,1,0:T(8,128)(2,1)} async-done(((bf16[3,2048,512]{2,1,0:T(8,128)(2,1)}), bf16[3,256,512]{2,1,0:T(8,128)(2,1)}) %reduce-scatter.8.cloned.1.call-update) | async-done | bytes 786448 | tf_op jit(solution)/shard_map/reduce_scatter | solution.py:424
  1355.3 5.6 multiply_subtract_fusion.2
  1360.9 146.2 %reduce-scatter.12.cloned.1.call-done = bf16[256,2048]{1,0:T(8,128)(2,1)} async-done(((bf16[2048,2048]{1,0:T(8,128)(2,1)}), bf16[256,2048]{1,0:T(8,128)(2,1)}) %reduce-scatter.12.cloned.1.call-update) | async-done | bytes 1048592 | tf_op jit(solution)/shard_map/reduce_scatter | solution.py:430
  1507.1 7.2 multiply_subtract_fusion.1
  1514.3 145.1 %reduce-scatter.14.cloned.1.call-done = bf16[2048,256]{1,0:T(8,128)(2,1)} async-done(((bf16[2048,2048]{1,0:T(8,128)(2,1)}), bf16[2048,256]{1,0:T(8,128)(2,1)}) %reduce-scatter.14.cloned.1.call-update) | async-done | bytes 1048592 | tf_op jit(solution)/shard_map/reduce_scatter | solution.py:433
  1659.4 6.9 multiply_subtract_fusion
  (318 shorter events, 118.5 us)
Async XLA Ops:
  7.2 341.4 %copy-start = (bf16[512,2048]{1,0:T(8,128)(2,1)S(1)}, bf16[512,2048]{1,0:T(8,128)(2,1)}, u32[]{:S(2)}) copy-start(bf16[512,2048]{1,0:T(8,128)(2,1)} %param.64) | copy-start | bytes 6291460
  7.2 65.0 %copy-start.75 = (s32[8]{0:T(128)S(1)}, s32[8]{0:T(128)}, u32[]{:S(2)}) copy-start(s32[8]{0:T(128)} %param.41) | copy-start | bytes 100
  7.2 282.3 %all-gather.11.cloned.1.call-start = ((), (), s32[]{:S(2)}) async-start(), calls=%async_computation.11 | async-start | bytes 7077888 | tf_op jit(solution)/shard_map/all_gather | solution.py:317
  8.0 347.3 %all-gather.15.cloned.1.call-start = ((), (), s32[]{:S(2)}) async-start(), calls=%async_computation.13 | async-start | bytes 9437184 | tf_op jit(solution)/shard_map/all_gather | solution.py:319
  8.7 433.0 %all-gather.17.cloned.1.call-start = ((), (), s32[]{:S(2)}) async-start(), calls=%async_computation.14 | async-start | bytes 9437184 | tf_op jit(solution)/shard_map/all_gather | solution.py:320
  11.7 55.5 %all-to-all-start = ((bf16[8,32,2048]{2,1,0:T(8,128)(2,1)}), bf16[8,32,2048]{2,1,0:T(8,128)(2,1)S(1)}, u32[]{:S(2)}, u32[]{:S(2)}) async-start(bf16[8,32,2048]{2,1,0:T(8,128)(2,1)} %bitcast.197), calls=%async_computation | async-start | bytes 2097152 | tf_op jit(solution)/shard_map/all_to_all | solution.py:231
  67.3 58.3 %all-to-all-start.2 = ((bf16[8,32,2048]{2,1,0:T(8,128)(2,1)}), bf16[8,32,2048]{2,1,0:T(8,128)(2,1)}, u32[]{:S(2)}, u32[]{:S(2)}) async-start(bf16[8,32,2048]{2,1,0:T(8,128)(2,1)} %bitcast.196), calls=%async_computation.2 | async-start | bytes 2097152 | tf_op jit(solution)/shard_map/all_to_all | solution.py:234
  131.2 60.8 %all-to-all-start.1 = ((bf16[8,32,2048]{2,1,0:T(8,128)(2,1)}), bf16[8,32,2048]{2,1,0:T(8,128)(2,1)S(1)}, u32[]{:S(2)}, u32[]{:S(2)}) async-start(bf16[8,32,2048]{2,1,0:T(8,128)(2,1)} %get-tuple-element.162), calls=%async_computation.1 | async-start | bytes 2097152 | tf_op jit(solution)/shard_map/all_to_all | solution.py:239
  135.6 357.2 %all-gather.13.cloned.1.call-start = ((), (), s32[]{:S(2)}) async-start(), calls=%async_computation.12 | async-start | bytes 2359296 | tf_op jit(solution)/shard_map/all_gather | solution.py:318
  141.9 7.8 copy-start.71
  141.9 55.0 %copy-start.63 = (f32[4,2048]{1,0:T(4,128)S(1)}, f32[4,2048]{1,0:T(4,128)}, u32[]{:S(2)}) copy-start(f32[4,2048]{1,0:T(4,128)} %param.62) | copy-start | bytes 98308
  190.3 130.3 %copy-start.38 = (f32[768,16]{0,1:T(8,128)}, f32[768,16]{0,1:T(8,128)S(1)}, u32[]{:S(2)}) copy-start(f32[768,16]{0,1:T(8,128)S(1)} %get-tuple-element.153) | copy-start | bytes 147460
  190.3 130.3 %copy-start.40 = (f32[768,16]{0,1:T(8,128)}, f32[768,16]{0,1:T(8,128)S(1)}, u32[]{:S(2)}) copy-start(f32[768,16]{0,1:T(8,128)S(1)} %get-tuple-element.154) | copy-start | bytes 147460
  191.9 433.6 %copy-start.7 = (bf16[8,32,2048]{2,1,0:T(8,128)(2,1)}, bf16[8,32,2048]{2,1,0:T(8,128)(2,1)S(1)}, u32[]{:S(2)}) copy-start(bf16[8,32,2048]{2,1,0:T(8,128)(2,1)S(1)} %all-to-all-done.1) | copy-start | bytes 3145732
  191.9 46.8 %all-to-all-start.3 = ((bf16[8,32,2048]{2,1,0:T(8,128)(2,1)}), bf16[8,32,2048]{2,1,0:T(8,128)(2,1)}, u32[]{:S(2)}, u32[]{:S(2)}) async-start(bf16[8,32,2048]{2,1,0:T(8,128)(2,1)} %get-tuple-element.161), calls=%async_computation.3 | async-start | bytes 2097152 | tf_op jit(solution)/shard_map/all_to_all | solution.py:242
  196.2 421.8 %all-reduce.12.cloned.1.call-start = ((), (), s32[]{:S(2)}) async-start(), calls=%async_computation.22 | async-start | bytes 12582912 | tf_op jit(solution)/shard_map/psum | solution.py:344
  196.9 56.8 %copy-start.50 = (f32[1,2048]{1,0:T(1,128)}, f32[1,2048]{1,0:T(1,128)S(1)}, u32[]{:S(2)}) copy-start(f32[1,2048]{1,0:T(1,128)S(1)} %get-tuple-element.147) | copy-start | bytes 24580
  196.9 51.3 %copy-start.66 = (f32[1,2048]{1,0:T(1,128)}, f32[1,2048]{1,0:T(1,128)S(1)}, u32[]{:S(2)}) copy-start(f32[1,2048]{1,0:T(1,128)S(1)} %get-tuple-element.143) | copy-start | bytes 24580
  196.9 51.3 %copy-start.67 = (f32[1,2048]{1,0:T(1,128)}, f32[1,2048]{1,0:T(1,128)S(1)}, u32[]{:S(2)}) copy-start(f32[1,2048]{1,0:T(1,128)S(1)} %get-tuple-element.144) | copy-start | bytes 24580
  199.0 156.2 %copy-start.52 = (f32[768]{0:T(1024)}, f32[768]{0:T(1024)S(1)}, u32[]{:S(2)}) copy-start(f32[768]{0:T(1024)S(1)} %broadcast_multiply_fusion.3) | copy-start | bytes 9220
  201.6 153.6 %copy-start.57 = (f32[768]{0:T(1024)}, f32[768]{0:T(1024)S(1)}, u32[]{:S(2)}) copy-start(f32[768]{0:T(1024)S(1)} %add_rsqrt_fusion.1) | copy-start | bytes 9220
  316.1 7.1 copy-start.26
  316.1 7.1 copy-start.27
  316.1 7.1 copy-start.37
  348.6 6.6 copy-start.55
  348.6 6.6 copy-start.64
  441.7 51.2 %copy-start.78 = (bf16[4,128,768]{2,1,0:T(8,128)(2,1)S(1)}, bf16[4,128,768]{2,1,0:T(8,128)(2,1)}, u32[]{:S(2)}) copy-start(bf16[4,128,768]{2,1,0:T(8,128)(2,1)} %fusion.138) | copy-start | bytes 2359300
  499.8 8.5 copy-start.12
  499.8 374.0 %all-reduce.8.cloned.1.call-start = ((), (), s32[]{:S(2)}) async-start(), calls=%async_computation.15 | async-start | bytes 4194304 | tf_op jit(solution)/shard_map/psum | solution.py:389
  618.0 7.5 copy-start.5
  618.0 7.5 copy-start.25
  786.3 38.0 %copy-start.60 = (f32[4,768]{1,0:T(4,128)S(1)}, f32[4,768]{1,0:T(4,128)}, u32[]{:S(2)}) copy-start(f32[4,768]{1,0:T(4,128)} %copy-done.59) | copy-start | bytes 36868
  786.4 38.0 %copy-start.62 = (f32[4,768]{1,0:T(4,128)S(1)}, f32[4,768]{1,0:T(4,128)}, u32[]{:S(2)}) copy-start(f32[4,768]{1,0:T(4,128)} %copy-done.61) | copy-start | bytes 36868
  824.3 246.9 %all-reduce.10.cloned.1.call-start = ((), (), s32[]{:S(2)}) async-start(), calls=%async_computation.21 | async-start | bytes 12582912 | tf_op jit(solution)/shard_map/psum | solution.py:404
  878.4 6.8 slice-start.1
  887.3 58.4 %copy-start.18 = (bf16[4,128,768]{2,1,0:T(8,128)(2,1)}, bf16[4,128,768]{2,1,0:T(8,128)(2,1)S(1)}, u32[]{:S(2)}) copy-start(bf16[4,128,768]{2,1,0:T(8,128)(2,1)S(1)} %fusion.140) | copy-start | bytes 2359300
  891.9 10.3 copy-start.47
  891.9 10.3 copy-start.49
  891.9 14.7 copy-start.43
  891.9 14.7 copy-start.45
  902.3 6.5 copy-start.39
  902.3 6.8 slice-start.3
  909.0 9.2 copy-start.19
  909.1 9.1 copy-start.21
  918.2 27.5 %slice-start.5 = ((s8[6291456]{0:T(1024)(128)(4,1)}), s8[2097152]{0:T(1024)(128)(4,1)S(1)}, s32[]{:S(2)}) async-start(s8[6291456]{0:T(1024)(128)(4,1)} %bitcast.194), calls=%async_computation.28 | async-start | bytes 4194304
  933.7 12.1 slice-start.6
  933.7 12.1 copy-start.13
  951.1 120.1 %copy-start.6 = (bf16[512,2048]{1,0:T(8,128)(2,1)S(1)}, bf16[512,2048]{1,0:T(8,128)(2,1)}, u32[]{:S(2)}) copy-start(bf16[512,2048]{1,0:T(8,128)(2,1)} %param.36) | copy-start | bytes 6291460
  951.1 120.1 %copy-start.8 = (bf16[8,32,2048]{2,1,0:T(8,128)(2,1)S(1)}, bf16[8,32,2048]{2,1,0:T(8,128)(2,1)}, u32[]{:S(2)}) copy-start(bf16[8,32,2048]{2,1,0:T(8,128)(2,1)} %copy-done.7) | copy-start | bytes 3145732
  951.1 120.1 %copy-start.51 = (f32[1,2048]{1,0:T(1,128)S(1)}, f32[1,2048]{1,0:T(1,128)}, u32[]{:S(2)}) copy-start(f32[1,2048]{1,0:T(1,128)} %copy-done.50) | copy-start | bytes 24580
  951.1 120.1 %copy-start.53 = (f32[768]{0:T(1024)S(1)}, f32[768]{0:T(1024)}, u32[]{:S(2)}) copy-start(f32[768]{0:T(1024)} %copy-done.52) | copy-start | bytes 9220
  951.1 120.1 %copy-start.56 = (f32[1,2048]{1,0:T(1,128)S(1)}, f32[1,2048]{1,0:T(1,128)}, u32[]{:S(2)}) copy-start(f32[1,2048]{1,0:T(1,128)} %get-tuple-element.149) | copy-start | bytes 24580
  951.1 120.1 %copy-start.58 = (f32[768]{0:T(1024)S(1)}, f32[768]{0:T(1024)}, u32[]{:S(2)}) copy-start(f32[768]{0:T(1024)} %copy-done.57) | copy-start | bytes 9220
  951.2 231.5 %reduce-scatter.16.cloned.1.call-start = ((), (), s32[]{:S(2)}) async-start(), calls=%async_computation.20 | async-start | bytes 589824
  1084.8 149.6 %reduce-scatter.10.cloned.1.call-start = ((), (), s32[]{:S(2)}) async-start(), calls=%async_computation.17 | async-start | bytes 2359296 | tf_op jit(solution)/shard_map/reduce_scatter | solution.py:427
  1090.4 264.8 %reduce-scatter.8.cloned.1.call-start = ((), (), s32[]{:S(2)}) async-start(), calls=%async_computation.16 | async-start | bytes 7077888 | tf_op jit(solution)/shard_map/reduce_scatter | solution.py:424
  1101.7 405.4 %reduce-scatter.12.cloned.1.call-start = ((), (), s32[]{:S(2)}) async-start(), calls=%async_computation.18 | async-start | bytes 9437184 | tf_op jit(solution)/shard_map/reduce_scatter | solution.py:430
  1113.9 545.5 %reduce-scatter.14.cloned.1.call-start = ((), (), s32[]{:S(2)}) async-start(), calls=%async_computation.19 | async-start | bytes 9437184 | tf_op jit(solution)/shard_map/reduce_scatter | solution.py:433
  1135.6 48.0 %copy-start.68 = (f32[4,256]{1,0:T(4,128)S(1)}, f32[4,256]{1,0:T(4,128)}, u32[]{:S(2)}) copy-start(f32[4,256]{1,0:T(4,128)} %param.47) | copy-start | bytes 12292
  1135.6 48.0 %copy-start.69 = (f32[4,256]{1,0:T(4,128)S(1)}, f32[4,256]{1,0:T(4,128)}, u32[]{:S(2)}) copy-start(f32[4,256]{1,0:T(4,128)} %param.52) | copy-start | bytes 12292
  1135.6 48.1 %copy-start.70 = (f32[4,256]{1,0:T(4,128)S(1)}, f32[4,256]{1,0:T(4,128)}, u32[]{:S(2)}) copy-start(f32[4,256]{1,0:T(4,128)} %param.57) | copy-start | bytes 12292
  1135.6 37.6 %all-to-all-start.4 = ((bf16[8,32,2048]{2,1,0:T(8,128)(2,1)}), bf16[8,32,2048]{2,1,0:T(8,128)(2,1)S(1)}, u32[]{:S(2)}, u32[]{:S(2)}) async-start(bf16[8,32,2048]{2,1,0:T(8,128)(2,1)} %bitcast.67), calls=%async_computation.4 | async-start | bytes 2097152 | tf_op jit(solution)/shard_map/all_to_all | solution.py:251
  1175.1 62.2 %all-to-all-start.5 = ((bf16[8,32,2048]{2,1,0:T(8,128)(2,1)}), bf16[8,32,2048]{2,1,0:T(8,128)(2,1)S(1)}, u32[]{:S(2)}, u32[]{:S(2)}) async-start(bf16[8,32,2048]{2,1,0:T(8,128)(2,1)} %select_convert_fusion), calls=%async_computation.5 | async-start | bytes 2097152 | tf_op jit(solution)/shard_map/all_to_all | solution.py:258
  1507.1 159.3 %copy-start.1 = (bf16[512,2048]{1,0:T(8,128)(2,1)S(1)}, bf16[512,2048]{1,0:T(8,128)(2,1)}, u32[]{:S(2)}) copy-start(bf16[512,2048]{1,0:T(8,128)(2,1)} %param.64) | copy-start | bytes 6291460
  (40 other events, 141.7 us)
Sparse Core Ops, SparseCore 0:
  10.2 157.6 all-gather.10
  170.1 145.9 all-gather.14
  318.1 123.5 all-gather.16
  443.6 49.2 all-gather.12
  499.9 117.9 all-reduce.11
  824.4 49.3 all-reduce.7
  951.3 119.8 all-reduce.9
  1085.0 62.2 reduce-scatter.15
  1151.4 83.0 reduce-scatter.9
  1237.9 117.3 reduce-scatter.7
  1358.9 148.1 reduce-scatter.11
  1511.0 148.3 reduce-scatter.13
where the time goes:
time: 1680 us; the launch traced here: 1670 us
  waiting for transfers between devices  995 us (59%)
  matrix products  330 us (20%)
  other arithmetic  129 us (8%)
  blocking collectives  96.6 us (6%)
  local copies, waits for them, and re-layouts  67.9 us (4%)
  starting transfers between devices  30.8 us (2%)
  between operations  23.9 us (1%)
    reduce_scatter x1, waiting for transfers between devices, per_device(): lax.psum_scatter(grad_expand.astype(jnp.bfloat16), 'dp', scatter_dimensio...  146 us
    reduce_scatter x1, waiting for transfers between devices, per_device(): lax.psum_scatter(grad_contract.astype(jnp.bfloat16), 'dp', scatter_dimens...  145 us
    psum x1, waiting for transfers between devices, per_device(): lax.psum(back_second.astype(jnp.bfloat16), 'tensor').astype(jnp.float32)  120 us
    reduce_scatter x1, waiting for transfers between devices, per_device(): lax.psum_scatter(grad_attend_in.astype(jnp.bfloat16), 'dp', scatter_dimen...  113 us
    psum x1, waiting for transfers between devices, per_device(): lax.psum(policy_part.astype(jnp.bfloat16), 'tensor').astype(jnp.float32)  105 us
    dot_general x2, matrix products, head_part(): logits = jnp.dot(unit_low, table, preferred_element_type=jnp.float32)  73.3 us
    all_gather x1, waiting for transfers between devices, per_device(): lax.all_gather(contract_copy, 'dp', axis=1, tiled=True)  59.3 us
    all_to_all x1, waiting for transfers between devices, bring_pairs(): lax.all_to_all(frozen_tail.reshape(groups, -1, width), 'dp', split_axis=0...  50.9 us
  transfers between devices with their start and end apart: 18, of which 13 were waited for; matrix products, arithmetic and copies ran while one was open for 16% of the time, Pallas kernels for 0%

commit v1 on v0

v1 whole, which is shorter than its diff:
```python
import jax
import jax.numpy as jnp
from jax import lax
from jax.experimental import pallas as pl
from jax.experimental.pallas import tpu as pltpu
from jax.sharding import PartitionSpec as P

D = 2048
HD = 128
ROT = 32
HALF = 256
STEP = 10


NORM_EPSILON = 1e-05
KTO_BETA = 2.0
ADAM_ONE = 0.9
ADAM_TWO = 0.95
ADAM_EPSILON = 1e-08
DECAY_RATE = 0.1
NORM_RATE = 0.3
ROPE_BASE = 10000.0
MASKED = -1e30

BF = jnp.bfloat16
F32 = jnp.float32


def dot(a, b, dims):
    return lax.dot_general(a, b, (dims, ((), ())), preferred_element_type=F32)


NN = ((1,), (0,))
NT = ((1,), (1,))
TN = ((0,), (0,))


def dp_shape():
    groups = lax.axis_size("dp")
    pair = 2 if groups % 2 == 0 else 1
    return groups, pair, groups // pair


def pair_swap(value):
    groups, _, _ = dp_shape()
    return lax.ppermute(value, "dp", [(i, i ^ 1) for i in range(groups)])


def dp_place():
    _, pair, _ = dp_shape()
    own = lax.axis_index("dp")
    return own // pair, own % pair


def tensor_swap(value, bit):
    return lax.ppermute(value, "tensor", [(i, i ^ bit) for i in range(lax.axis_size("tensor"))])


def ring_groups():
    _, pair, ring = dp_shape()
    return [[r * pair + p for r in range(ring)] for p in range(pair)]


def gather_ring(piece):
    return lax.all_gather(piece, "dp", axis_index_groups=ring_groups())


def scatter_ring(blocks):
    return lax.psum_scatter(blocks, "dp", axis_index_groups=ring_groups())


def by_side(mine, other, axis):
    _, low = dp_place()
    first, second = jnp.stack([mine, other], axis), jnp.stack([other, mine], axis)
    return jnp.where(low == 0, first, second)


def rows_of(mine, other):
    if other is None:
        return mine
    both = by_side(mine, other, 1)
    return both.reshape((-1,) + both.shape[2:])


def to_ring(kept, came):
    if came is not None:
        kept = (kept.astype(F32) + came.astype(F32)).astype(BF)
    return kept[:, 0]


def columns_of(mine, other):
    both = mine[:, None] if other is None else by_side(mine, other, 1)
    ring, pair, rows, slab = both.shape
    return jnp.moveaxis(both, 2, 0).reshape(rows, ring * pair * slab)


def gather_step(held, bit):
    groups = lax.axis_size("dp")
    came = lax.ppermute(held, "dp", [(i, i ^ bit) for i in range(groups)])
    return jnp.where(
        lax.axis_index("dp") & bit == 0,
        jnp.concatenate([held, came]),
        jnp.concatenate([came, held]),
    )


def gather_small(value):
    groups = lax.axis_size("dp")
    if groups & (groups - 1):
        return lax.all_gather(value, "dp")
    held = value[None]
    bit = 1
    while bit < groups:
        held = gather_step(held, bit)
        bit *= 2
    return held


def sum_small(value, axes):
    for axis in axes:
        size = lax.axis_size(axis)
        if size & (size - 1):
            value = lax.psum(value, axis)
            continue
        bit = 1
        while bit < size:
            value = value + lax.ppermute(value, axis, [(i, i ^ bit) for i in range(size)])
            bit *= 2
    return value


def tensor_near(part):
    low = lax.axis_index("tensor") % 2
    half = part.shape[0] // 2
    kept = lax.dynamic_slice_in_dim(part, low * half, half, 0)
    sent = lax.dynamic_slice_in_dim(part, (1 - low) * half, half, 0)
    return (kept.astype(F32) + tensor_swap(sent, 1).astype(F32)).astype(BF)


def tensor_far(kept):
    return (kept.astype(F32) + tensor_swap(kept, 2).astype(F32)).astype(BF)


def tensor_halves(part):
    part = part.astype(BF)
    if lax.axis_size("tensor") != 4:
        whole = lax.psum(part, "tensor")
        half = part.shape[0] // 2
        return whole[:half], whole[half:], jnp.zeros((1,), jnp.int32)
    kept = tensor_far(tensor_near(part))
    return kept, tensor_swap(kept, 1), (lax.axis_index("tensor") % 2).reshape(1)


def whole_rows(mine, other, low):
    return jnp.where(
        low[0] == 0, jnp.concatenate([mine, other], axis=0), jnp.concatenate([other, mine], axis=0)
    )


def tensor_sum(part):
    return whole_rows(*tensor_halves(part))


def back_columns(pull_logits, table, gaps):
    slices = 4
    step = table.shape[0] // slices
    groups = lax.axis_size("dp")
    product = lambda i: dot(pull_logits, table[i * step : (i + 1) * step], NT).astype(BF)
    if lax.axis_size("tensor") != 4 or groups & (groups - 1):
        return gather_small(gaps), [tensor_halves(product(i)) for i in range(slices)]
    steps = groups.bit_length() - 1
    held, hops = gaps[None], 0
    near, far, parts = [], [], []
    for i in range(slices):
        if i:
            share = -(-steps // (slices - 1))
            for _ in range(min(share, steps - hops)):
                held = gather_step(held, 1 << hops)
                hops += 1
        waits = [pull_logits, held]
        if i >= 2:
            near.append(tensor_near(parts[i - 2]))
            waits.append(near[-1])
        if i >= 3:
            far.append(tensor_far(near[i - 3]))
            waits.append(far[-1])
        waits = lax.optimization_barrier(tuple(waits))
        pull_logits, held = waits[:2]
        if i >= 2:
            near[-1] = waits[2]
        if i >= 3:
            far[-1] = waits[3]
        parts.append(product(i))
    near += [tensor_near(parts[i]) for i in range(slices - 2, slices)]
    far += [tensor_far(near[i]) for i in range(slices - 3, slices)]
    low = (lax.axis_index("tensor") % 2).reshape(1)
    return held, [(kept, tensor_swap(kept, 1), low) for kept in far]


def tensor_join(part):
    if lax.axis_size("tensor") != 4:
        return lax.all_gather(part, "tensor")
    me = lax.axis_index("tensor")
    far = tensor_swap(part, 2)
    two = jnp.where(me // 2 == 0, jnp.stack([part, far]), jnp.stack([far, part]))
    near = tensor_swap(two, 1)
    four = jnp.where(me % 2 == 0, jnp.stack([two, near], 1), jnp.stack([near, two], 1))
    return four.reshape((4,) + part.shape)


def normalize(values):
    centre = jnp.mean(values, axis=-1, keepdims=True)
    centred = values - centre
    inverse_scale = lax.rsqrt(jnp.mean(centred * centred, axis=-1, keepdims=True) + NORM_EPSILON)
    return (centred * inverse_scale, inverse_scale)


def normalize_back(upstream, unit, inverse_scale):
    return inverse_scale * (
        upstream
        - jnp.mean(upstream, axis=-1, keepdims=True)
        - unit * jnp.mean(upstream * unit, axis=-1, keepdims=True)
    )


def after(value, *others):
    return lax.optimization_barrier((value,) + others)[0]


def turn_tables(half):
    place = jnp.arange(3 * half, dtype=jnp.int32)
    place = jnp.where(place < 2 * half, place, place - half)
    freqs = ROPE_BASE ** (-jnp.arange(ROT // 2, dtype=F32) * 2.0 / ROT)
    angles = place.astype(F32)[:, None] * freqs[None, :]
    cosines, sines = jnp.cos(angles), jnp.sin(angles)
    rest = jnp.zeros((3 * half, HD - ROT), F32)
    none = jnp.zeros_like(sines)
    return jnp.stack(
        [
            jnp.concatenate([cosines, cosines, rest + 1.0], axis=1),
            jnp.concatenate([-sines, none, rest], axis=1),
            jnp.concatenate([none, sines, rest], axis=1),
        ]
    )


def turned(x, table, way):
    step = ROT // 2
    moved = pltpu.roll(x, HD - step, 1) * table[1] + pltpu.roll(x, step, 1) * table[2]
    return x * table[0] + moved * way


def seen_scores(query, near, far, half):
    scale = HD ** (-0.5)
    rows = lax.broadcasted_iota(jnp.int32, (half, half), 0)
    cols = lax.broadcasted_iota(jnp.int32, (half, half), 1)
    own = jnp.where(cols <= rows, dot(query, near, NT) * scale, MASKED)
    peak = jnp.max(own, axis=1, keepdims=True)
    if far is None:
        own = jnp.exp(own - peak)
        return own / jnp.sum(own, axis=1, keepdims=True), None
    before = dot(query, far, NT) * scale
    peak = jnp.maximum(peak, jnp.max(before, axis=1, keepdims=True))
    own, before = jnp.exp(own - peak), jnp.exp(before - peak)
    total = jnp.sum(own, axis=1, keepdims=True) + jnp.sum(before, axis=1, keepdims=True)
    return own / total, before / total


def attend_body(half, skip, x_ref, w_ref, t_ref, out_ref, q_ref, k_ref, v_ref):
    x = x_ref[...]
    raw = [dot(x[skip:], w_ref[0], NN), dot(x, w_ref[1], NN), dot(x, w_ref[2], NN)]
    for h in range(w_ref.shape[2] // HD):
        at = slice(h * HD, (h + 1) * HD)
        query = turned(raw[0][:, at], t_ref[:, skip:], 1.0).astype(BF)
        keys = turned(raw[1][:, at], t_ref[...], 1.0).astype(BF)
        values = raw[2][:, at].astype(BF)
        q_ref[:, at], k_ref[:, at], v_ref[:, at] = query, keys, values
        part = lambda x, g, gone=0: x[g * half - gone : (g + 1) * half - gone]
        for g in range(skip // half, 3):
            own, before = seen_scores(
                part(query, g, skip), part(keys, g), part(keys, 0) if g else None, half
            )
            seen = dot(own.astype(BF), part(values, g), NN)
            if g:
                seen = seen + dot(before.astype(BF), part(values, 0), NN)
            out_ref[g * half - skip : (g + 1) * half - skip, at] = seen.astype(BF)


def head_pairs(inner):
    return 2 * HD if inner % (2 * HD) == 0 else HD


def attention(first_in, weights, tables, half, skip):
    count, width = first_in.shape
    inner = weights.shape[2]
    block = head_pairs(inner)
    columns = lambda rows: pl.BlockSpec((rows, block), lambda h: (0, h))
    shape = lambda rows: jax.ShapeDtypeStruct((rows, inner), BF)
    return pl.pallas_call(
        lambda *refs: attend_body(half, skip, *refs),
        grid=(inner // block,),
        in_specs=[
            pl.BlockSpec((count, width), lambda h: (0, 0)),
            pl.BlockSpec((3, width, block), lambda h: (0, 0, h)),
            pl.BlockSpec(tables.shape, lambda h: (0, 0, 0)),
        ],
        out_specs=[columns(count - skip), columns(count - skip), columns(count), columns(count)],
        out_shape=[shape(count - skip), shape(count - skip), shape(count), shape(count)],
        compiler_params=pltpu.CompilerParams(vmem_limit_bytes=48 * 2**20),
        cost_estimate=pl.CostEstimate(
            flops=2 * count * width * inner * 3, bytes_accessed=20 * 2**20, transcendentals=0
        ),
        name="attend",
    )(first_in, weights, tables)


def attend_back_body(half, d_ref, q_ref, k_ref, v_ref, t_ref, out_ref):
    scale = HD ** (-0.5)
    for h in range(d_ref.shape[1] // HD):
        at = slice(h * HD, (h + 1) * HD)
        part = lambda ref, g: ref[g * half : (g + 1) * half, at]
        back_keys = back_values = None
        for g in (1, 2):
            query, far, near = part(q_ref, g), part(k_ref, 0), part(k_ref, g)
            upstream = part(d_ref, g - 1)
            own, before = seen_scores(query, near, far, half)
            own_pull = dot(upstream, part(v_ref, g), NT)
            far_pull = dot(upstream, part(v_ref, 0), NT)
            mean = jnp.sum(own * own_pull, axis=1, keepdims=True) + jnp.sum(
                before * far_pull, axis=1, keepdims=True
            )
            own_back = (own * (own_pull - mean)).astype(BF)
            far_back = (before * (far_pull - mean)).astype(BF)
            back_query = (dot(own_back, near, NN) + dot(far_back, far, NN)) * scale
            rows = slice(g * half, (g + 1) * half)
            out_ref[0, rows, at] = turned(
                back_query, t_ref[:, rows], -1.0
            ).astype(BF)
            out_ref[1, rows, at] = turned(
                dot(own_back, query, TN) * scale, t_ref[:, rows], -1.0
            ).astype(BF)
            out_ref[2, rows, at] = dot(own.astype(BF), upstream, TN).astype(BF)
            more_keys, more_values = dot(far_back, query, TN), dot(before.astype(BF), upstream, TN)
            back_keys = more_keys if back_keys is None else back_keys + more_keys
            back_values = more_values if back_values is None else back_values + more_values
        out_ref[0, :half, at] = jnp.zeros((half, HD), BF)
        out_ref[1, :half, at] = turned(back_keys * scale, t_ref[:, :half], -1.0).astype(BF)
        out_ref[2, :half, at] = back_values.astype(BF)


def attention_back(back_attended, query, keys, values, tables, half):
    count, inner = keys.shape
    block = head_pairs(inner)
    columns = lambda rows: pl.BlockSpec((rows, block), lambda h: (0, h))
    return pl.pallas_call(
        lambda *refs: attend_back_body(half, *refs),
        grid=(inner // block,),
        in_specs=[
            columns(count - half),
            columns(count),
            columns(count),
            columns(count),
            pl.BlockSpec(tables.shape, lambda h: (0, 0, 0)),
        ],
        out_specs=pl.BlockSpec((3, count, block), lambda h: (0, 0, h)),
        out_shape=jax.ShapeDtypeStruct((3, count, inner), BF),
        compiler_params=pltpu.CompilerParams(vmem_limit_bytes=48 * 2**20),
        cost_estimate=pl.CostEstimate(
            flops=2**31, bytes_accessed=8 * 2**20, transcendentals=2**20
        ),
        name="attend_back",
    )(back_attended, query, keys, values, tables)


def hidden_body(skip, x_ref, w_ref, out_ref, *slope_ref):
    before = dot(x_ref[...], w_ref[...], NN)
    share = 0.5 + 0.5 * lax.erf(before * 0.5**0.5)
    out_ref[...] = (before * share).astype(BF)
    if slope_ref:
        kept = before[skip:]
        bell = jnp.exp(-0.5 * kept * kept) * (2.0 * jnp.pi) ** (-0.5)
        slope_ref[0][...] = share[skip:] + kept * bell


def hidden_units(second_in, expand, skip=None):
    count, width = second_in.shape
    units = expand.shape[1]
    block = 256
    column = lambda rows: pl.BlockSpec((rows, block), lambda i: (0, i))
    out_specs, out_shape = [column(count)], [jax.ShapeDtypeStruct((count, units), BF)]
    if skip is not None:
        out_specs.append(column(count - skip))
        out_shape.append(jax.ShapeDtypeStruct((count - skip, units), F32))
    return pl.pallas_call(
        lambda *refs: hidden_body(skip, *refs),
        grid=(units // block,),
        in_specs=[pl.BlockSpec((count, width), lambda i: (0, 0)), column(width)],
        out_specs=out_specs,
        out_shape=out_shape,
        compiler_params=pltpu.CompilerParams(vmem_limit_bytes=48 * 2**20),
        cost_estimate=pl.CostEstimate(
            flops=2 * count * width * units,
            bytes_accessed=2 * width * units + 8 * count * units,
            transcendentals=count * units,
        ),
        name="hidden",
    )(second_in, expand)


def shard_of(r, side, low, pair):
    return r * pair + (low[0] + side) % pair


def grad_body(x_ref, y_ref, out_ref):
    x = x_ref[...]
    for i in range(y_ref.shape[0]):
        out_ref[0, 0, i] = dot(x, y_ref[i], TN).astype(BF)


def grad_blocks(left, right, sides):
    groups, pair, ring = dp_shape()
    low = dp_place()[1].reshape(1)
    rows = left.shape[0]
    slab = left.shape[1] // groups
    parts, _, width = right.shape
    if slab % 128:
        shards = left.reshape(rows, ring, pair, slab)
        shards = jnp.stack([shards[:, :, (low[0] + s) % pair] for s in sides], axis=2)
        out = jnp.einsum("nrsc,pnw->rspcw", shards, right, preferred_element_type=F32)
        return out.astype(BF)
    first = sides[0]
    return pl.pallas_call(
        lambda low_ref, *refs: grad_body(*refs),
        grid_spec=pltpu.PrefetchScalarGridSpec(
            num_scalar_prefetch=1,
            grid=(ring, len(sides)),
            in_specs=[
                pl.BlockSpec((rows, slab), lambda r, s, l: (0, shard_of(r, s + first, l, pair))),
                pl.BlockSpec(right.shape, lambda r, s, l: (0, 0, 0)),
            ],
            out_specs=pl.BlockSpec(
                (1, 1, parts, slab, width), lambda r, s, l: (r, s, 0, 0, 0)
            ),
        ),
        out_shape=jax.ShapeDtypeStruct((ring, len(sides), parts, slab, width), BF),
        compiler_params=pltpu.CompilerParams(vmem_limit_bytes=48 * 2**20),
        cost_estimate=pl.CostEstimate(
            flops=2 * rows * slab * ring * len(sides) * parts * width,
            bytes_accessed=2 * slab * ring * len(sides) * parts * width,
            transcendentals=0,
        ),
        name="grad_blocks",
    )(low, left, right)


def branch_body(pair, x_ref, y_ref, *refs):
    hidden_refs, attend_refs, out_ref = refs[:pair], refs[pair : 2 * pair], refs[-1]

    def write(side):
        out_ref[...] = (
            dot(x_ref[...], hidden_refs[side][0], NN) + dot(y_ref[...], attend_refs[side][0], NN)
        ).astype(BF)

    for side in range(pair):
        pl.when(pl.program_id(1) == side)(lambda: write(side))


def branch_terms(hidden, attended, contract, attend_out, start, count):
    groups, pair, ring = dp_shape()
    low = dp_place()[1].reshape(1)
    slab = contract[0].shape[2]
    if slab % 128:
        rows = slice(start, start + count)
        out = 0.0
        for x, sides in ((hidden[rows], contract), (attended[rows], attend_out)):
            if pair == 2:
                sides = [by_side(sides[0], sides[1], 1)]
            weight = sides[0].reshape(groups, x.shape[1], slab)
            out = out + jnp.einsum("nf,sfc->nsc", x, weight, preferred_element_type=F32)
        return out.reshape(count, groups * slab).astype(BF)
    weights = [*contract[:pair], *attend_out[:pair]]
    units, inner = hidden.shape[1], attended.shape[1]
    return pl.pallas_call(
        lambda low_ref, *refs: branch_body(pair, *refs),
        grid_spec=pltpu.PrefetchScalarGridSpec(
            num_scalar_prefetch=1,
            grid=(ring, pair),
            in_specs=[
                pl.BlockSpec((count, units), lambda r, s, l: (start // count, 0)),
                pl.BlockSpec((count, inner), lambda r, s, l: (start // count, 0)),
                *(pl.BlockSpec((1,) + x.shape[1:], lambda r, s, l: (r, 0, 0)) for x in weights),
            ],
            out_specs=pl.BlockSpec(
                (count, slab), lambda r, s, l: (0, shard_of(r, s, l, pair))
            ),
        ),
        out_shape=jax.ShapeDtypeStruct((count, groups * slab), BF),
        compiler_params=pltpu.CompilerParams(vmem_limit_bytes=48 * 2**20),
        cost_estimate=pl.CostEstimate(
            flops=2 * count * (units + inner) * groups * slab,
            bytes_accessed=2 * (units + inner) * groups * slab,
            transcendentals=0,
        ),
        name="branch",
    )(low, hidden, attended, *weights)


def out_body(x_ref, mine_ref, other_ref, low_ref, unit_ref, low_unit_ref, scale_ref, out_ref):
    mine = pl.program_id(0) == low_ref[0]
    branch = jnp.where(mine, mine_ref[...].astype(F32), other_ref[...].astype(F32))
    out = x_ref[...].astype(F32) + branch
    unit, scale = normalize(out)
    unit_ref[...] = unit
    low_unit_ref[...] = unit.astype(BF)
    scale_ref[...] = scale
    out_ref[...] = out.astype(BF)


def out_rows(x, halves):
    mine, other, low = halves
    rows, width = x.shape
    block = 128
    steps = rows // 2 // block
    whole = pl.BlockSpec((block, width), lambda h, i: (h * steps + i, 0))
    part = pl.BlockSpec((block, width), lambda h, i: (i, 0))
    return pl.pallas_call(
        out_body,
        grid=(2, steps),
        in_specs=[whole, part, part, pl.BlockSpec(memory_space=pltpu.SMEM)],
        out_specs=[whole, whole, pl.BlockSpec((block, 1), lambda h, i: (h * steps + i, 0)), whole],
        out_shape=[
            jax.ShapeDtypeStruct((rows, width), F32),
            jax.ShapeDtypeStruct((rows, width), BF),
            jax.ShapeDtypeStruct((rows, 1), F32),
            jax.ShapeDtypeStruct((rows, width), BF),
        ],
        compiler_params=pltpu.CompilerParams(vmem_limit_bytes=48 * 2**20),
        name="out_rows",
    )(x, mine, other, low)


def borrow_rows(tail, order, *first):
    groups = lax.axis_size("dp")
    parts = lax.axis_size("tensor")
    count, rows, width = tail.shape
    share = rows // parts
    mine = lax.dynamic_slice_in_dim(tail, lax.axis_index("tensor") * share, share, 1)
    mine = mine.reshape(count, groups, share // groups, width).swapaxes(0, 1)
    spread = after(lax.all_to_all(mine, "dp", split_axis=0, concat_axis=0, tiled=True), *first)
    landed = lax.all_to_all(
        jnp.take(spread, order, axis=0), "dp", split_axis=0, concat_axis=0, tiled=True
    )
    landed = landed.swapaxes(0, 1).reshape(count, share, width)
    return tensor_join(landed).swapaxes(0, 1).reshape(count, rows, width)


def head_stats(unit_low, table, local_targets):
    logits = dot(unit_low, table, NN)
    peak = jnp.max(logits, axis=-1)
    total = jnp.sum(jnp.exp(logits - peak[:, None]), axis=-1)
    target_hit = jnp.arange(table.shape[1], dtype=jnp.int32)[None, :] == local_targets[:, None]
    picked = jnp.sum(jnp.where(target_hit, logits, 0.0), axis=-1)
    return jnp.stack([peak, total, picked]), logits, target_hit


def join_stats(stats):
    every = lax.all_gather(stats, "tensor")
    peak = jnp.max(every[:, 0], axis=0)
    total = jnp.sum(every[:, 1] * jnp.exp(every[:, 0] - peak[None]), axis=0)
    return peak, total, jnp.sum(every[:, 2], axis=0)


def adamw_step(master, first, second, gradient, rate, decay):
    new_first = ADAM_ONE * first + (1.0 - ADAM_ONE) * gradient
    new_second = ADAM_TWO * second + (1.0 - ADAM_TWO) * gradient * gradient
    ratio = (
        new_first
        / (1.0 - ADAM_ONE**STEP)
        / (jnp.sqrt(new_second / (1.0 - ADAM_TWO**STEP)) + ADAM_EPSILON)
    )
    return (master - rate * (ratio + decay * master), new_first, new_second)


def per_device(
    policy_rows,
    frozen_rows,
    next_tokens,
    desirable,
    answer_len,
    partner,
    norms_copy,
    attend_in_copy,
    attend_out_copy,
    expand_copy,
    contract_copy,
    norms_master,
    attend_in_master,
    attend_out_master,
    expand_master,
    contract_master,
    norms_first,
    attend_in_first,
    attend_out_first,
    expand_first,
    contract_first,
    norms_second,
    attend_in_second,
    attend_out_second,
    expand_second,
    contract_second,
    frozen_norms,
    frozen_in,
    frozen_out,
    frozen_expand,
    frozen_contract,
    vocab_table,
):
    groups = lax.axis_size("dp")
    own_index = lax.axis_index("dp")
    half = policy_rows.shape[0] // 2
    inner = attend_in_copy.shape[2]
    slab = attend_in_copy.shape[1]
    width = policy_rows.shape[1]
    inverse = jnp.zeros_like(partner).at[partner].set(jnp.arange(groups, dtype=jnp.int32))
    other_index = partner[own_index]

    norms_full = gather_small(norms_copy).swapaxes(0, 1).reshape(4, width).astype(F32)
    units = expand_copy.shape[1]
    _, pair, ring = dp_shape()
    _, low = dp_place()
    swap = pair_swap if pair == 2 else (lambda value: None)
    cut = (units + inner) // 2
    out_came = swap(attend_out_copy)
    attend_mine = gather_ring(attend_in_copy)
    expand_mine = gather_ring(expand_copy)
    contract_mine = gather_ring(contract_copy)
    out_mine = gather_ring(attend_out_copy)
    out_other = None if out_came is None else gather_ring(out_came)

    other = borrow_rows(jnp.stack([frozen_rows[half:], policy_rows[half:]]), partner)
    tables = turn_tables(half)

    frozen_work = jnp.concatenate([frozen_rows, other[0]], axis=0).astype(F32)
    frozen_unit, _ = normalize(frozen_work)
    frozen_first_in = (frozen_unit * frozen_norms[0] + frozen_norms[1]).astype(BF)
    frozen_second_in = (frozen_unit[half:] * frozen_norms[2] + frozen_norms[3]).astype(BF)
    frozen_first_in, frozen_second_in, attend_mine = lax.optimization_barrier(
        (frozen_first_in, frozen_second_in, attend_mine)
    )
    attend_other = swap(attend_mine)
    frozen_attended = attention(frozen_first_in, frozen_in, tables, half, half)[0]
    (frozen_hidden,) = hidden_units(frozen_second_in, frozen_expand)
    frozen_part = dot(frozen_attended, frozen_out, NN) + dot(frozen_hidden, frozen_contract, NN)
    frozen_part, attend_other, expand_mine = lax.optimization_barrier(
        (frozen_part.astype(BF), attend_other, expand_mine)
    )
    expand_other = swap(expand_mine)
    frozen_low = out_rows(
        jnp.concatenate([frozen_rows[half:], other[0]], axis=0), tensor_halves(frozen_part)
    )[1]
    vocab_local = vocab_table.shape[1]
    targets = (
        jnp.concatenate([next_tokens[own_index], next_tokens[other_index]])
        - lax.axis_index("tensor") * vocab_local
    )
    work = jnp.concatenate([policy_rows, other[1]], axis=0).astype(F32)
    unit, inverse_scale = normalize(work)
    first_in = (unit * norms_full[0] + norms_full[1]).astype(BF)
    second_in = (unit * norms_full[2] + norms_full[3]).astype(BF)
    attend_in = rows_of(attend_mine, attend_other)
    attend_in = attend_in.swapaxes(0, 1).reshape(3, width, inner)
    attended, query, keys, values = attention(first_in, attend_in, tables, half, 0)
    second_in, contract_mine, attended, expand_other = lax.optimization_barrier(
        (second_in, contract_mine, attended, expand_other)
    )
    contract_other = swap(contract_mine)
    expand = rows_of(expand_mine, expand_other).reshape(width, units)
    hidden, slope_units = hidden_units(second_in, expand, half)
    frozen_low, hidden = lax.optimization_barrier((frozen_low, hidden))
    frozen_stats, _, _ = head_stats(frozen_low, vocab_table, targets)
    frozen_peak, frozen_total, frozen_picked = join_stats(frozen_stats)
    hidden, frozen_peak = lax.optimization_barrier((hidden, frozen_peak))

    contract, attend_out = (contract_mine, contract_other), (out_mine, out_other)
    scored_halves = tensor_halves(
        jnp.concatenate(
            [
                branch_terms(hidden, attended, contract, attend_out, g * half, half)
                for g in (1, 2)
            ],
            axis=0,
        )
    )
    unit_out, unit_low, inverse_out, out_low = out_rows(
        jnp.concatenate([policy_rows[half:], other[1]], axis=0), scored_halves
    )
    stats, logits, target_hit = head_stats(unit_low, vocab_table, targets)
    peak, total, picked = join_stats(stats)
    softmax_part = jnp.exp(logits - peak[:, None]) * (1.0 / total)[:, None]
    pull_logits = (target_hit.astype(F32) - softmax_part).astype(BF)

    log_chance = jnp.stack(
        [picked - peak - jnp.log(total), frozen_picked - frozen_peak - jnp.log(frozen_total)]
    )
    steps = jnp.arange(half, dtype=jnp.int32)
    own_count = answer_len[own_index]
    other_count = answer_len[other_index]
    own_live = (steps < own_count).astype(F32)
    other_live = (steps < other_count).astype(F32)
    own_total = own_count.astype(F32)
    other_total = other_count.astype(F32)
    own_mean = jnp.sum(log_chance[:, :half] * own_live, axis=1) / own_total
    other_mean = jnp.sum(log_chance[:, half:] * other_live, axis=1) / other_total
    gaps = jnp.stack([own_mean[0] - own_mean[1], other_mean[0] - other_mean[1]])
    every, back_parts = back_columns(pull_logits, vocab_table, gaps)
    back_parts = [whole_rows(*part) for part in back_parts]
    drift = jnp.sum(every[:, 1]) / groups
    sign = (2 * desirable - 1).astype(F32)
    settled = jax.nn.sigmoid(KTO_BETA * sign * (every[:, 0] - jax.nn.softplus(drift)))
    slope = KTO_BETA * sign * settled * (1.0 - settled)
    loss_total = jnp.sum(1.0 - settled)
    pull = jnp.sum(slope) * jax.nn.sigmoid(drift) / groups
    row_weight = jnp.concatenate(
        [-slope[own_index] * own_live / own_total, pull * other_live / other_total]
    )

    back_unit = row_weight[:, None] * jnp.concatenate(back_parts, axis=1).astype(F32)
    back_out = normalize_back(back_unit, unit_out, inverse_out)
    branch_low = back_out.astype(BF)

    features_scored = jnp.concatenate([hidden[half:], attended[half:]], axis=1)
    near_features, far_features = features_scored[:, :cut][None], features_scored[:, cut:][None]
    near_sent = grad_blocks(branch_low, near_features, (1,))
    near_came = swap(near_sent)
    far_blocks = grad_blocks(branch_low, far_features, range(pair))
    far_back = scatter_ring(far_blocks)

    contract_full = columns_of(*contract)
    back_expand = (dot(branch_low, contract_full, NT) * slope_units).astype(BF)
    expand_sent = grad_blocks(second_in[half:], back_expand[None], (1,))
    expand_came = swap(expand_sent)
    back_attended = dot(branch_low, columns_of(*attend_out), NT).astype(BF)
    back_three = attention_back(back_attended, query, keys, values, tables, half)
    attend_sent = grad_blocks(first_in, back_three, (1,))
    attend_came = swap(attend_sent)

    kept_left = after(branch_low, far_blocks, expand_sent, attend_sent)
    near_ring = to_ring(grad_blocks(kept_left, near_features, (0,)), near_came)
    grad_near = scatter_ring(near_ring)[0].astype(F32)
    second_scored, near_ring, far_back = lax.optimization_barrier(
        (second_in[half:], near_ring, far_back)
    )
    expand_kept = grad_blocks(second_scored, back_expand[None], (0,))
    expand_ring = to_ring(expand_kept, expand_came)
    grad_expand = scatter_ring(expand_ring)[0].astype(F32)
    back_expand, back_three, expand_ring = lax.optimization_barrier(
        (back_expand, back_three, expand_ring)
    )
    back_second = dot(back_expand, expand, NT)
    back_first = sum(dot(back_three[i], attend_in[i], NT) for i in range(3))

    unit_scored = unit[half:]
    grad_norms = sum_small(
        jnp.stack(
            [
                jnp.sum(back_first * unit, axis=0),
                jnp.sum(back_first, axis=0),
                jnp.sum(back_second * unit_scored, axis=0),
                jnp.sum(back_second, axis=0),
            ]
        ),
        ("tensor",),
    )
    back_h = back_first * norms_full[0] + jnp.pad(
        back_second * norms_full[2], ((half, 0), (0, 0))
    )
    back_h, attend_came = lax.optimization_barrier((tensor_sum(back_h), attend_came))
    attend_kept = grad_blocks(after(first_in, back_h), back_three, (0,))
    attend_ring = to_ring(attend_kept, attend_came)
    attend_back = scatter_ring(attend_ring)
    back_work = normalize_back(
        after(back_h, attend_ring).astype(F32), unit, inverse_scale
    ) + jnp.pad(back_out, ((half, 0), (0, 0)))
    out_prompt = work[:half] + tensor_sum(
        branch_terms(hidden, attended, contract, attend_out, 0, half)
    ).astype(F32)
    mixed = jnp.concatenate([out_prompt.astype(BF), out_low[:half]], axis=0)
    grad_norms = sum_small(after(grad_norms, attend_ring), ("dp",))
    grad_norms = lax.dynamic_slice_in_dim(grad_norms, own_index * slab, slab, 1)
    returned = borrow_rows(back_work[None, 2 * half :].astype(BF), inverse, attend_ring)[0]
    grad_far = far_back[0, 0].astype(F32)
    if pair == 2:
        grad_far = grad_far + pair_swap(far_back[1, 0]).astype(F32)
    grad_join = jnp.concatenate([grad_near.T, grad_far.T], axis=0)
    grad_contract, grad_attend_out = grad_join[:units], grad_join[units:]
    input_grad = jnp.concatenate(
        [back_work[:half], back_work[half : 2 * half] + returned.astype(F32)], axis=0
    )

    matrix_rate = 0.5 * D ** (-0.5)
    out_rate = 0.5 * max(D // HALF, 1) ** (-0.5)
    masters = (norms_master, attend_in_master, attend_out_master, expand_master, contract_master)
    firsts = (norms_first, attend_in_first, attend_out_first, expand_first, contract_first)
    seconds = (norms_second, attend_in_second, attend_out_second, expand_second, contract_second)
    rates = (NORM_RATE, matrix_rate, out_rate, matrix_rate, matrix_rate)
    decays = (0.0, DECAY_RATE, DECAY_RATE, DECAY_RATE, DECAY_RATE)
    gradients = [grad_norms, None, grad_attend_out, grad_expand, grad_contract]
    updated = [None] * 5
    for i in (2, 4, 3, 0):
        updated[i] = adamw_step(
            masters[i], firsts[i], seconds[i], gradients[i], rates[i], decays[i]
        )
    attend_back, *waited = lax.optimization_barrier(
        (attend_back, *(updated[i][0] for i in (2, 4, 3, 0)))
    )
    for i, first in zip((2, 4, 3, 0), waited):
        updated[i] = (first,) + updated[i][1:]
    updated[1] = adamw_step(
        masters[1], firsts[1], seconds[1], attend_back.astype(F32), rates[1], decays[1]
    )
    return (
        mixed,
        input_grad,
        jnp.reshape(loss_total, (1,)),
        *(step[0] for step in updated),
        *(step[1] for step in updated),
        *(step[2] for step in updated),
    )


def solution(mesh):
    rows = P("dp", None)
    all_of = P()
    state = (P(None, "dp"), P(None, "dp", "tensor"), P("tensor", "dp"), P("dp", "tensor"), P("tensor", "dp"))
    frozen = (all_of, P(None, None, "tensor"), P("tensor", None), P(None, "tensor"), P("tensor", None))
    return jax.shard_map(
        per_device,
        mesh=mesh,
        in_specs=(rows, rows) + (all_of,) * 4 + state * 4 + frozen + (P(None, "tensor"),),
        out_specs=(rows, rows, all_of) + state * 3,
        check_vma=False,
    )
```

time: 1680 us -> 1080 us (0.64)
  waiting for transfers between devices: 995 us -> 344 us
  matrix products: 330 us -> 175 us
  Pallas kernels: 0 us -> 129 us
  other arithmetic: 129 us -> 199 us
  blocking collectives: 96.6 us -> 43.2 us
  local copies, waits for them, and re-layouts: 67.9 us -> 100 us
  starting transfers between devices: 30.8 us -> 55.4 us
    reduce_scatter x4, waiting for transfers between devices: 454 us -> 0.01 us  [scatter_ring(): return lax.psum_scatter(blocks, 'dp', axis_index_groups=ring_groups())]
    psum x3 -> x0, waiting for transfers between devices: 274 us -> none  [the longest x1 120 us: per_device(): lax.psum(back_second.astype(jnp.bfloat16), 'tensor').astype(jnp.float32)]
    ppermute x0 -> x47, waiting for transfers between devices: none -> 258 us  [the longest x8 167 us: pair_swap(): return lax.ppermute(value, 'dp', [(i, i ^ 1) for i in range(groups)])]
    dot_general x32 -> x14, matrix products: 321 us -> 175 us  [dot(): return lax.dot_general(a, b, (dims, ((), ())), preferred_element_type=F32)]
    pallas_call x0 -> x17, Pallas kernels: none -> 129 us  [the longest x7 29.2 us: grad_blocks(): pl.pallas_call(lambda low_ref, *refs: grad_body(*refs), grid_spec=pltpu.P...]
    all_to_all x6 -> x3, waiting for transfers between devices: 165 us -> 50.6 us  [the longest x2 38.9 us: borrow_rows(): lax.all_to_all(mine, 'dp', split_axis=0, concat_axis=0, tiled=True)]
    all_gather x4 -> x5, waiting for transfers between devices: 98.6 us -> 33.5 us  [gather_ring(): return lax.all_gather(piece, 'dp', axis_index_groups=ring_groups())]
    all_gather x4 -> x2, blocking collectives: 55.8 us -> 10.7 us  [join_stats(): every = lax.all_gather(stats, 'tensor')]
  transfers between devices with their start and end apart: 18 -> 59, of which waited for: 13 -> 21; matrix products, arithmetic and copies ran while one was open for 16% -> 34% of each run, Pallas kernels for 0% -> 9%
where the time goes in v1:
time: 1080 us; the launch traced here: 1070 us
  waiting for transfers between devices  344 us (32%)
  other arithmetic  199 us (18%)
  matrix products  175 us (16%)
  Pallas kernels  129 us (12%)
  local copies, waits for them, and re-layouts  100 us (9%)
  starting transfers between devices  55.4 us (5%)
  blocking collectives  43.2 us (4%)
  between operations  23.5 us (2%)
    dot_general x14, matrix products, dot(): return lax.dot_general(a, b, (dims, ((), ())), preferred_element_type=F32)  175 us
    ppermute x8, waiting for transfers between devices, pair_swap(): return lax.ppermute(value, 'dp', [(i, i ^ 1) for i in range(groups)])  167 us
    ppermute x28, waiting for transfers between devices, tensor_swap(): lax.ppermute(value, 'tensor', [(i, i ^ bit) for i in range(lax.axis_size(...  84.6 us
    unnamed x212, local copies, waits for them, and re-layouts  47.5 us
    all_to_all x2, waiting for transfers between devices, borrow_rows(): lax.all_to_all(mine, 'dp', split_axis=0, concat_axis=0, tiled=True)  38.9 us
    all_gather x5, waiting for transfers between devices, gather_ring(): return lax.all_gather(piece, 'dp', axis_index_groups=ring_groups())  33.5 us
    all_to_all x1, blocking collectives, borrow_rows(): lax.all_to_all(jnp.take(spread, order, axis=0), 'dp', split_axis=0, conca...  32.4 us
    pallas_call x7, Pallas kernels, grad_blocks(): pl.pallas_call(lambda low_ref, *refs: grad_body(*refs), grid_spec=pltpu.P...  29.2 us
  transfers between devices with their start and end apart: 59, of which 21 were waited for; matrix products, arithmetic and copies ran while one was open for 34% of the time, Pallas kernels for 9%

profile of v1, /device:TPU:0, one launch (start us, length us, event | category | flops | bytes accessed | tf_op | source)
XLA Modules:
  0.0 1070.2 jit_solution(17288962671062750540)
XLA Ops:
  13.6 7.4 all-to-all-start
  21.6 28.3 %all-to-all-done = bf16[8,2,8,2048]{3,2,1,0:T(8,128)(2,1)S(1)} async-done(((bf16[8,2,8,2048]{3,2,1,0:T(8,128)(2,1)}), bf16[8,2,8,2048]{3,2,1,0:T(8,128)(2,1)S(1)}, u32[]{:S(2)}, u32[]{:S(2)}) %all-to-all-start) | async-done | bytes 524320 | tf_op jit(solution)/shard_map/all_to_all | solution.py:549
  50.6 32.4 %all_to_all.20 = bf16[8,2,8,2048]{3,2,1,0:T(8,128)(2,1)S(1)} all-to-all(bf16[8,2,8,2048]{3,2,1,0:T(8,128)(2,1)S(1)} %broadcast_select_fusion), channel_id=1, replica_groups=mesh['dp'=8,'tensor'=4] {'dp'}, dimensions={0} | all-to-all | bytes 1048576 | tf_op jit(solution)/shard_map/all_to_all | solution.py:550
  88.0 7.4 collective-permute-done
  126.1 8.9 hidden.2
  135.0 6.9 fusion.105
  142.0 13.2 %attend.2 = (bf16[512,512]{1,0:T(8,128)(2,1)S(1)}, bf16[512,512]{1,0:T(8,128)(2,1)}, bf16[768,512]{1,0:T(8,128)(2,1)}, bf16[768,512]{1,0:T(8,128)(2,1)}) custom-call(bf16[768,2048]{1,0:T(8,128)(2,1)} %get-tuple-element.71.refs_0_, bf16[3,2048,512]{2,1,0:T(8,128)(2,1)} %refs_1_.2, f32[3,768,128]{2,1,0:T(8,128)S(1)} %pad_maximum_fusion.9.refs_2_.refs_4_), custom_call_target="tpu_custom_call" | custom-call | flops 4831838208 | bytes 20971520 | tf_op jit(solution)/shard_map/attend/pallas_call | solution.py:299
  157.8 21.4 %all-gather.17.cloned.1.call-done = bf16[1024,2048]{1,0:T(8,128)(2,1)} async-done(((bf16[256,2048]{1,0:T(8,128)(2,1)}), bf16[1024,2048]{1,0:T(8,128)(2,1)}) %all-gather.17.cloned.1.call-update) | async-done | bytes 4194320 | tf_op jit(solution)/shard_map/all_gather | solution.py:65
  194.8 7.3 subtract_multiply_fusion
  202.2 14.8 %collective-permute-done.4 = bf16[256,2048]{1,0:T(8,128)(2,1)S(1)} collective-permute-done((bf16[256,2048]{1,0:T(8,128)(2,1)S(1)}, bf16[256,2048]{1,0:T(8,128)(2,1)S(1)}, u32[]{:S(2)}, u32[]{:S(2)}) %collective-permute-start.4) | collective-permute-done | bytes 1048608 | tf_op jit(solution)/shard_map/ppermute | solution.py:56
  224.5 14.8 %attend.3 = (bf16[768,512]{1,0:T(8,128)(2,1)S(1)}, bf16[768,512]{1,0:T(8,128)(2,1)S(1)}, bf16[768,512]{1,0:T(8,128)(2,1)S(1)}, bf16[768,512]{1,0:T(8,128)(2,1)S(1)}) custom-call(bf16[768,2048]{1,0:T(8,128)(2,1)} %get-tuple-element.113.refs_0_, bf16[3,2048,512]{2,1,0:T(8,128)(2,1)} %bitcast.247, f32[3,768,128]{2,1,0:T(8,128)S(1)} %pad_maximum_fusion.9.refs_2_.refs_4_), custom_call_target="tpu_custom_call" | custom-call | flops 4831838208 | bytes 20971520 | tf_op jit(solution)/shard_map/attend/pallas_call | solution.py:299
  242.1 5.8 out_rows.2
  247.9 12.1 %all-gather.19.cloned.1.call-done = bf16[8192,256]{1,0:T(8,128)(2,1)} async-done(((bf16[2048,256]{1,0:T(8,128)(2,1)}), bf16[8192,256]{1,0:T(8,128)(2,1)}) %all-gather.19.cloned.1.call-update) | async-done | bytes 4194320 | tf_op jit(solution)/shard_map/all_gather | solution.py:65
  260.0 17.5 %collective-permute-done.9 = bf16[4,256,2048]{2,1,0:T(8,128)(2,1)} collective-permute-done((bf16[4,256,2048]{2,1,0:T(8,128)(2,1)}, bf16[4,256,2048]{2,1,0:T(8,128)(2,1)}, u32[]{:S(2)}, u32[]{:S(2)}) %collective-permute-start.9) | collective-permute-done | bytes 4194336 | tf_op jit(solution)/shard_map/ppermute | solution.py:46
  277.5 10.3 maximum_select_fusion
  287.8 13.6 %hidden.3 = (bf16[768,2048]{1,0:T(8,128)(2,1)S(1)}, f32[512,2048]{1,0:T(8,128)}) custom-call(bf16[768,2048]{1,0:T(8,128)(2,1)} %get-tuple-element.80.refs_0_, bf16[2048,2048]{1,0:T(8,128)(2,1)} %bitcast.253), custom_call_target="tpu_custom_call" | custom-call | flops 6442450944 | bytes 20971520 | tf_op jit(solution)/shard_map/hidden/pallas_call | solution.py:394
  304.5 34.7 %fusion.103 = (f32[512]{0:T(512)S(1)}, f32[512,12576]{0,1:T(8,128)}) fusion(bf16[512,2048]{1,0:T(8,128)(2,1)S(1)} %get-tuple-element.84, bf16[2048,12576]{0,1:T(8,128)(2,1)} %param.63), kind=kOutput, calls=%fused_computation.274 | convolution fusion | flops 26380222464 | bytes 79366144 | tf_op jit(solution)/shard_map/dot_general | solution.py:30
  339.2 11.8 %exponential_reduce_fusion.1 = (f32[512]{0:T(512)S(1)}, f32[512]{0:T(512)S(1)}) fusion(f32[512,12576]{0,1:T(8,128)} %get-tuple-element.319, f32[512]{0:T(512)S(1)} %get-tuple-element.318, s32[512]{0:T(512)S(1)} %add_subtract_fusion), kind=kLoop, calls=%fused_computation.8 | loop fusion | flops 32193536 | bytes 25763840 | tf_op jit(solution)/shard_map/reduce_sum | solution.py:560
  351.0 5.2 all-gather.7
  356.3 39.2 %collective-permute-done.10.refs_3_ = bf16[4,2048,256]{2,1,0:T(8,128)(2,1)} collective-permute-done((bf16[4,2048,256]{2,1,0:T(8,128)(2,1)}, bf16[4,2048,256]{2,1,0:T(8,128)(2,1)}, u32[]{:S(2)}, u32[]{:S(2)}) %collective-permute-start.10) | collective-permute-done | bytes 4194336 | tf_op jit(solution)/shard_map/ppermute | solution.py:46
  397.9 9.5 branch.5
  407.5 9.4 branch.4
  423.1 23.7 %collective-permute-done.16 = bf16[256,2048]{1,0:T(8,128)(2,1)S(1)} collective-permute-done((bf16[256,2048]{1,0:T(8,128)(2,1)S(1)}, bf16[256,2048]{1,0:T(8,128)(2,1)S(1)}, u32[]{:S(2)}, u32[]{:S(2)}) %collective-permute-start.16) | collective-permute-done | bytes 1048608 | tf_op jit(solution)/shard_map/ppermute | solution.py:56
  456.9 6.1 out_rows.3
  463.0 34.7 %fusion.104 = (f32[512]{0:T(512)S(1)}, f32[512,12576]{0,1:T(8,128)}) fusion(bf16[512,2048]{1,0:T(8,128)(2,1)S(1)} %get-tuple-element.90, bf16[2048,12576]{0,1:T(8,128)(2,1)} %param.63), kind=kOutput, calls=%fused_computation.275 | convolution fusion | flops 26380222464 | bytes 79366144 | tf_op jit(solution)/shard_map/dot_general | solution.py:30
  497.7 12.3 %exponential_reduce_fusion = (f32[512]{0:T(512)S(1)}, f32[512]{0:T(512)S(1)}) fusion(f32[512,12576]{0,1:T(8,128)} %get-tuple-element.321, f32[512]{0:T(512)S(1)} %get-tuple-element.320, s32[512]{0:T(512)S(1)} %add_subtract_fusion), kind=kLoop, calls=%fused_computation.5 | loop fusion | flops 32193536 | bytes 25763840 | tf_op jit(solution)/shard_map/reduce_sum | solution.py:560
  510.0 5.5 all-gather.8
  517.0 9.1 subtract_convert_fusion
  528.7 13.8 %fusion.32 = bf16[512,512]{1,0:T(8,128)(2,1)S(1)} fusion(bf16[512,12576]{0,1:T(8,128)(2,1)} %subtract_convert_fusion, bf16[2048,12576]{0,1:T(8,128)(2,1)} %param.63), kind=kOutput, calls=%fused_computation.110 | convolution fusion | flops 6593708032 | bytes 26279936 | tf_op jit(solution)/shard_map/dot_general | solution.py:30
  548.5 13.8 %fusion.35 = bf16[512,512]{1,0:T(8,128)(2,1)S(1)} fusion(bf16[512,12576]{0,1:T(8,128)(2,1)} %subtract_convert_fusion, bf16[2048,12576]{0,1:T(8,128)(2,1)} %param.63), kind=kOutput, calls=%fused_computation.111 | convolution fusion | flops 6593708032 | bytes 26279936 | tf_op jit(solution)/shard_map/dot_general | solution.py:30
  569.3 14.2 %fusion.38 = bf16[512,512]{1,0:T(8,128)(2,1)S(1)} fusion(bf16[512,12576]{0,1:T(8,128)(2,1)} %subtract_convert_fusion, bf16[2048,12576]{0,1:T(8,128)(2,1)} %param.63), kind=kOutput, calls=%fused_computation.112 | convolution fusion | flops 6593708032 | bytes 26279936 | tf_op jit(solution)/shard_map/dot_general | solution.py:30
  593.0 13.8 %fusion.41 = bf16[512,512]{1,0:T(8,128)(2,1)S(1)} fusion(bf16[512,12576]{0,1:T(8,128)(2,1)} %subtract_convert_fusion, bf16[2048,12576]{0,1:T(8,128)(2,1)} %param.63), kind=kOutput, calls=%fused_computation.113 | convolution fusion | flops 6593708032 | bytes 26279936 | tf_op jit(solution)/shard_map/dot_general | solution.py:30
  617.8 5.0 collective-permute-done.31
  628.9 6.4 grad_blocks.7
  639.3 4.4 copy.204
  648.1 10.5 fusion.8
  658.6 11.6 %copy.203 = bf16[2048,4,2,256]{0,3,2,1:T(8,128)(2,1)} copy(bf16[2048,4,2,256]{3,0,1,2:T(8,128)(2,1)} %fusion.8) | data formatting | bytes 16777216 | tf_op jit(solution)/shard_map/transpose | solution.py:94
  674.4 8.9 multiply_convert_fusion
  683.3 4.4 grad_blocks.8
  690.3 9.4 attend_back.1.refs_1_
  701.4 4.5 grad_blocks.9
  710.0 22.5 %collective-permute-done.33 = bf16[4,1,1,256,1280]{4,3,2,1,0:T(8,128)(2,1)S(1)} collective-permute-done((bf16[4,1,1,256,1280]{4,3,2,1,0:T(8,128)(2,1)S(1)}, bf16[4,1,1,256,1280]{4,3,2,1,0:T(8,128)(2,1)S(1)}, u32[]{:S(2)}, u32[]{:S(2)}) %collective-permute-start.33) | collective-permute-done | bytes 2621472 | tf_op jit(solution)/shard_map/ppermute | solution.py:46
  734.7 5.8 fusion.94
  742.2 4.6 grad_blocks.12
  746.8 75.5 %collective-permute-done.34 = bf16[4,1,1,256,2048]{4,3,2,1,0:T(8,128)(2,1)} collective-permute-done((bf16[4,1,1,256,2048]{4,3,2,1,0:T(8,128)(2,1)}, bf16[4,1,1,256,2048]{4,3,2,1,0:T(8,128)(2,1)}, u32[]{:S(2)}, u32[]{:S(2)}) %collective-permute-start.34) | collective-permute-done | bytes 4194336 | tf_op jit(solution)/shard_map/ppermute | solution.py:46
  822.2 7.7 fusion.16
  829.9 6.3 fusion.47
  836.2 4.4 fusion.49
  842.2 11.8 %fusion.17 = (f32[2048]{0:T(1024)S(1)}, f32[2048]{0:T(1024)S(1)}, f32[512,2048]{1,0:T(8,128)}) fusion(f32[768,2048]{1,0:T(8,128)} %get-tuple-element.277, f32[2048]{0:T(1024)S(1)} %bitcast.288, bf16[512,2048]{1,0:T(8,128)(2,1)S(1)} %copy-done.18, bf16[2048,2048]{1,0:T(8,128)(2,1)} %bitcast.254), kind=kOutput, calls=%fused_computation.47 | convolution fusion | flops 4299157504 | bytes 18898944 | tf_op jit(solution)/shard_map/dot_general | solution.py:30
  854.0 7.9 add_convert_fusion.2
  865.4 9.5 branch.3
  897.7 30.9 %collective-permute-done.13 = bf16[128,2048]{1,0:T(8,128)(2,1)} collective-permute-done((bf16[128,2048]{1,0:T(8,128)(2,1)}, bf16[128,2048]{1,0:T(8,128)(2,1)}, u32[]{:S(2)}, u32[]{:S(2)}) %collective-permute-start.13) | collective-permute-done | bytes 524320 | tf_op jit(solution)/shard_map/ppermute | solution.py:56
  940.5 5.0 maximum_select_fusion.3
  945.4 9.8 collective-permute-done.38
  955.3 4.5 grad_blocks.13
  959.8 4.5 fusion.21
  964.3 6.3 multiply_reduce_fusion
  970.8 4.7 fusion.14
  989.2 10.7 all-to-all-done.2
  1002.2 4.2 all-to-all-start.3
  1009.9 11.6 %all-to-all-done.3 = bf16[8,1,8,2048]{3,2,1,0:T(8,128)(2,1)} async-done(((bf16[8,1,8,2048]{3,2,1,0:T(8,128)(2,1)}), bf16[8,1,8,2048]{3,2,1,0:T(8,128)(2,1)}, u32[]{:S(2)}, u32[]{:S(2)}) %all-to-all-start.3) | async-done | bytes 262176 | tf_op jit(solution)/shard_map/all_to_all | solution.py:550
  1022.4 6.5 multiply_subtract_fusion.1
  1048.1 7.2 multiply_subtract_fusion
  1058.1 5.4 multiply_subtract_fusion.2
  (471 shorter events, 235.6 us)
Async XLA Ops:
  7.2 148.0 %copy-start = (bf16[512,2048]{1,0:T(8,128)(2,1)S(1)}, bf16[512,2048]{1,0:T(8,128)(2,1)}, u32[]{:S(2)}) copy-start(bf16[512,2048]{1,0:T(8,128)(2,1)} %param.60) | copy-start | bytes 6291460
  7.2 103.8 %all-gather.15.cloned.1.call-start = ((), (), s32[]{:S(2)}) async-start(), calls=%async_computation.12 | async-start | bytes 3932160 | tf_op jit(solution)/shard_map/all_gather | solution.py:65
  7.9 171.2 %all-gather.17.cloned.1.call-start = ((), (), s32[]{:S(2)}) async-start(), calls=%async_computation.13 | async-start | bytes 5242880 | tf_op jit(solution)/shard_map/all_gather | solution.py:65
  8.7 251.3 %all-gather.19.cloned.1.call-start = ((), (), s32[]{:S(2)}) async-start(), calls=%async_computation.14 | async-start | bytes 5242880 | tf_op jit(solution)/shard_map/all_gather | solution.py:65
  13.6 72.1 %copy-start.90 = (bf16[4,256]{1,0:T(4,128)(2,1)S(1)}, bf16[4,256]{1,0:T(4,128)(2,1)}, u32[]{:S(2)}) copy-start(bf16[4,256]{1,0:T(4,128)(2,1)} %param.38) | copy-start | bytes 6148
  13.6 36.3 %all-to-all-start = ((bf16[8,2,8,2048]{3,2,1,0:T(8,128)(2,1)}), bf16[8,2,8,2048]{3,2,1,0:T(8,128)(2,1)S(1)}, u32[]{:S(2)}, u32[]{:S(2)}) async-start(bf16[8,2,8,2048]{3,2,1,0:T(8,128)(2,1)} %copy_bitcast_fusion.1), calls=%async_computation | async-start | bytes 1048576 | tf_op jit(solution)/shard_map/all_to_all | solution.py:549
  21.0 335.2 %all-gather.21.cloned.1.call-start = ((), (), s32[]{:S(2)}) async-start(), calls=%async_computation.15 | async-start | bytes 1310720 | tf_op jit(solution)/shard_map/all_gather | solution.py:65
  84.2 11.2 %collective-permute-start = (bf16[2,64,2048]{2,1,0:T(8,128)(2,1)}, bf16[2,64,2048]{2,1,0:T(8,128)(2,1)S(1)}, u32[]{:S(2)}, u32[]{:S(2)}) collective-permute-start(bf16[2,64,2048]{2,1,0:T(8,128)(2,1)} %get-tuple-element.289), channel_id=1, source_target_pairs={{0,2},{1,3},{2,0},{3,1},{4,6},{5,7},{6,4},{7,5},{8,10},{9,11},{10,... | collective-permute-start | bytes 1572872 | tf_op jit(solution)/shard_map/ppermute | solution.py:56
  85.7 32.9 %collective-permute-start.6 = (bf16[1,4,256]{2,1,0:T(4,128)(2,1)S(1)}, bf16[1,4,256]{2,1,0:T(4,128)(2,1)S(1)}, u32[]{:S(2)}, u32[]{:S(2)}) collective-permute-start(bf16[1,4,256]{2,1,0:T(4,128)(2,1)S(1)} %bitcast.305), channel_id=1, source_target_pairs={{0,4},{4,0},{8,12},{12,8},{16,20},{20,16},{24,28},{28,24},{1,5},{5... | collective-permute-start | bytes 6152 | tf_op jit(solution)/shard_map/ppermute | solution.py:99
  87.1 98.7 %collective-permute-start.11 = (bf16[512,256]{1,0:T(8,128)(2,1)}, bf16[512,256]{1,0:T(8,128)(2,1)}, u32[]{:S(2)}, u32[]{:S(2)}) collective-permute-start(bf16[512,256]{1,0:T(8,128)(2,1)} %param.40), channel_id=1, source_target_pairs={{0,4},{4,0},{8,12},{12,8},{16,20},{20,16},{24,28},{28,24},{1,5},{5... | collective-permute-start | bytes 786440 | tf_op jit(solution)/shard_map/ppermute | solution.py:46
  87.8 268.5 %all-gather.23.cloned.1.call-start = ((), (), s32[]{:S(2)}) async-start(), calls=%async_computation.16 | async-start | bytes 1310720 | tf_op jit(solution)/shard_map/all_gather | solution.py:65
  96.7 3.7 collective-permute-start.1
  111.0 70.8 %collective-permute-start.2 = (bf16[4,3,256,512]{3,2,1,0:T(8,128)(2,1)}, bf16[4,3,256,512]{3,2,1,0:T(8,128)(2,1)}, u32[]{:S(2)}, u32[]{:S(2)}) collective-permute-start(bf16[4,3,256,512]{3,2,1,0:T(8,128)(2,1)} %bitcast.262), channel_id=1, source_target_pairs={{0,4},{4,0},{8,12},{12,8},{16,20},{20,16},{24,28},{28,24},{1,5},{5... | collective-permute-start | bytes 9437192 | tf_op jit(solution)/shard_map/ppermute | solution.py:46
  117.8 106.7 %copy-start.26 = (f32[3,768,128]{2,1,0:T(8,128)}, f32[3,768,128]{2,1,0:T(8,128)S(1)}, u32[]{:S(2)}) copy-start(f32[3,768,128]{2,1,0:T(8,128)S(1)} %pad_maximum_fusion.9.refs_2_.refs_4_) | copy-start | bytes 3538948
  118.6 3.8 collective-permute-start.7
  122.5 61.6 %collective-permute-start.8 = (bf16[4,4,256]{2,1,0:T(4,128)(2,1)S(1)}, bf16[4,4,256]{2,1,0:T(4,128)(2,1)S(1)}, u32[]{:S(2)}, u32[]{:S(2)}) collective-permute-start(bf16[4,4,256]{2,1,0:T(4,128)(2,1)S(1)} %maximum_select_fusion.16), channel_id=1, source_target_pairs={{0,16},{4,20},{8,24},{12,28},{16,0},{20,4},{24,8},{28,12},{1,17},{... | collective-permute-start | bytes 24584 | tf_op jit(solution)/shard_map/ppermute | solution.py:99
  184.1 5.9 collective-permute-start.3
  184.1 93.4 %collective-permute-start.9 = (bf16[4,256,2048]{2,1,0:T(8,128)(2,1)}, bf16[4,256,2048]{2,1,0:T(8,128)(2,1)}, u32[]{:S(2)}, u32[]{:S(2)}) collective-permute-start(bf16[4,256,2048]{2,1,0:T(8,128)(2,1)} %bitcast.260), channel_id=1, source_target_pairs={{0,4},{4,0},{8,12},{12,8},{16,20},{20,16},{24,28},{28,24},{1,5},{5... | collective-permute-start | bytes 12582920 | tf_op jit(solution)/shard_map/ppermute | solution.py:46
  185.8 554.8 %reduce-scatter.5.cloned.1.call-start = ((), (), s32[]{:S(2)}) async-start(), calls=%async_computation.8 | async-start | bytes 6553600 | tf_op jit(solution)/shard_map/reduce_scatter | solution.py:69
  191.7 25.4 %collective-permute-start.4 = (bf16[256,2048]{1,0:T(8,128)(2,1)S(1)}, bf16[256,2048]{1,0:T(8,128)(2,1)S(1)}, u32[]{:S(2)}, u32[]{:S(2)}) collective-permute-start(bf16[256,2048]{1,0:T(8,128)(2,1)S(1)} %add_convert_fusion.13), channel_id=1, source_target_pairs={{0,2},{1,3},{2,0},{3,1},{4,6},{5,7},{6,4},{7,5},{8,10},{9,11},{10,... | collective-permute-start | bytes 3145736 | tf_op jit(solution)/shard_map/ppermute | solution.py:56
  217.4 24.7 %collective-permute-start.5 = (bf16[256,2048]{1,0:T(8,128)(2,1)S(1)}, bf16[256,2048]{1,0:T(8,128)(2,1)S(1)}, u32[]{:S(2)}, u32[]{:S(2)}) collective-permute-start(bf16[256,2048]{1,0:T(8,128)(2,1)S(1)} %add_convert_fusion.12.mine_ref), channel_id=1, source_target_pairs={{0,1},{1,0},{2,3},{3,2},{4,5},{5,4},{6,7},{7,6},{8,9},{9,8},{10,11... | collective-permute-start | bytes 3145736 | tf_op jit(solution)/shard_map/ppermute | solution.py:56
  242.1 165.3 %copy-start.13 = (bf16[768,512]{1,0:T(8,128)(2,1)}, bf16[768,512]{1,0:T(8,128)(2,1)S(1)}, u32[]{:S(2)}) copy-start(bf16[768,512]{1,0:T(8,128)(2,1)S(1)} %get-tuple-element.86.refs_1_) | copy-start | bytes 2359300
  303.0 92.5 %collective-permute-start.10 = (bf16[4,2048,256]{2,1,0:T(8,128)(2,1)}, bf16[4,2048,256]{2,1,0:T(8,128)(2,1)}, u32[]{:S(2)}, u32[]{:S(2)}) collective-permute-start(bf16[4,2048,256]{2,1,0:T(8,128)(2,1)} %bitcast.30.refs_2_), channel_id=1, source_target_pairs={{0,4},{4,0},{8,12},{12,8},{16,20},{20,16},{24,28},{28,24},{1,5},{5... | collective-permute-start | bytes 12582920 | tf_op jit(solution)/shard_map/ppermute | solution.py:46
  417.8 2.7 collective-permute-start.15
  421.5 25.3 %collective-permute-start.16 = (bf16[256,2048]{1,0:T(8,128)(2,1)S(1)}, bf16[256,2048]{1,0:T(8,128)(2,1)S(1)}, u32[]{:S(2)}, u32[]{:S(2)}) collective-permute-start(bf16[256,2048]{1,0:T(8,128)(2,1)S(1)} %add_convert_fusion.11), channel_id=1, source_target_pairs={{0,2},{1,3},{2,0},{3,1},{4,6},{5,7},{6,4},{7,5},{8,10},{9,11},{10,... | collective-permute-start | bytes 3145736 | tf_op jit(solution)/shard_map/ppermute | solution.py:56
  448.2 8.7 collective-permute-start.17
  544.0 19.2 %collective-permute-start.20 = (bf16[256,512]{1,0:T(8,128)(2,1)}, bf16[256,512]{1,0:T(8,128)(2,1)}, u32[]{:S(2)}, u32[]{:S(2)}) collective-permute-start(bf16[256,512]{1,0:T(8,128)(2,1)} %constant_dynamic-slice_fusion.5), channel_id=1, source_target_pairs={{0,1},{1,0},{2,3},{3,2},{4,5},{5,4},{6,7},{7,6},{8,9},{9,8},{10,11... | collective-permute-start | bytes 786440 | tf_op jit(solution)/shard_map/ppermute | solution.py:56
  544.3 3.5 collective-permute-start.18
  547.9 15.3 %collective-permute-start.19 = (f32[2,2]{1,0:T(2,128)S(1)}, f32[2,2]{1,0:T(2,128)S(1)}, u32[]{:S(2)}, u32[]{:S(2)}) collective-permute-start(f32[2,2]{1,0:T(2,128)S(1)} %maximum_select_fusion.19), channel_id=1, source_target_pairs={{0,8},{4,12},{8,0},{12,4},{16,24},{20,28},{24,16},{28,20},{1,9},{5... | collective-permute-start | bytes 56 | tf_op jit(solution)/shard_map/ppermute | solution.py:99
  563.1 21.2 %collective-permute-start.22 = (bf16[256,512]{1,0:T(8,128)(2,1)}, bf16[256,512]{1,0:T(8,128)(2,1)}, u32[]{:S(2)}, u32[]{:S(2)}) collective-permute-start(bf16[256,512]{1,0:T(8,128)(2,1)} %constant_dynamic-slice_fusion.4), channel_id=1, source_target_pairs={{0,1},{1,0},{2,3},{3,2},{4,5},{5,4},{6,7},{7,6},{8,9},{9,8},{10,11... | collective-permute-start | bytes 786440 | tf_op jit(solution)/shard_map/ppermute | solution.py:56
  564.2 21.9 %collective-permute-start.21 = (f32[4,2]{1,0:T(4,128)S(1)}, f32[4,2]{1,0:T(4,128)S(1)}, u32[]{:S(2)}, u32[]{:S(2)}) collective-permute-start(f32[4,2]{1,0:T(4,128)S(1)} %maximum_select_fusion.18), channel_id=1, source_target_pairs={{0,16},{4,20},{8,24},{12,28},{16,0},{20,4},{24,8},{28,12},{1,17},{... | collective-permute-start | bytes 104 | tf_op jit(solution)/shard_map/ppermute | solution.py:99
  567.8 18.5 %collective-permute-start.23 = (bf16[256,512]{1,0:T(8,128)(2,1)S(1)}, bf16[256,512]{1,0:T(8,128)(2,1)}, u32[]{:S(2)}, u32[]{:S(2)}) collective-permute-start(bf16[256,512]{1,0:T(8,128)(2,1)S(1)} %add_convert_fusion.23), channel_id=1, source_target_pairs={{0,2},{1,3},{2,0},{3,1},{4,6},{5,7},{6,4},{7,5},{8,10},{9,11},{10,... | collective-permute-start | bytes 786440 | tf_op jit(solution)/shard_map/ppermute | solution.py:56
  584.3 5.4 collective-permute-start.27
  588.6 34.4 %collective-permute-start.24 = (bf16[256,512]{1,0:T(8,128)(2,1)S(1)}, bf16[256,512]{1,0:T(8,128)(2,1)}, u32[]{:S(2)}, u32[]{:S(2)}) collective-permute-start(bf16[256,512]{1,0:T(8,128)(2,1)S(1)} %add_convert_fusion.21), channel_id=1, source_target_pairs={{0,1},{1,0},{2,3},{3,2},{4,5},{5,4},{6,7},{7,6},{8,9},{9,8},{10,11... | collective-permute-start | bytes 786440 | tf_op jit(solution)/shard_map/ppermute | solution.py:56
  589.2 25.5 %collective-permute-start.25 = (bf16[256,512]{1,0:T(8,128)(2,1)}, bf16[256,512]{1,0:T(8,128)(2,1)}, u32[]{:S(2)}, u32[]{:S(2)}) collective-permute-start(bf16[256,512]{1,0:T(8,128)(2,1)} %add_convert_fusion.22), channel_id=1, source_target_pairs={{0,2},{1,3},{2,0},{3,1},{4,6},{5,7},{6,4},{7,5},{8,10},{9,11},{10,... | collective-permute-start | bytes 786440 | tf_op jit(solution)/shard_map/ppermute | solution.py:56
  591.5 24.7 %collective-permute-start.28 = (bf16[256,512]{1,0:T(8,128)(2,1)}, bf16[256,512]{1,0:T(8,128)(2,1)}, u32[]{:S(2)}, u32[]{:S(2)}) collective-permute-start(bf16[256,512]{1,0:T(8,128)(2,1)} %add_convert_fusion.19), channel_id=1, source_target_pairs={{0,2},{1,3},{2,0},{3,1},{4,6},{5,7},{6,4},{7,5},{8,10},{9,11},{10,... | collective-permute-start | bytes 786440 | tf_op jit(solution)/shard_map/ppermute | solution.py:56
  608.3 4.6 collective-permute-start.30
  614.1 8.8 collective-permute-start.31
  616.1 8.1 collective-permute-start.26
  617.3 7.1 collective-permute-start.29
  622.9 1.7 collective-permute-start.32
  635.3 302.9 %reduce-scatter.9.cloned.1.call-start = ((), (), s32[]{:S(2)}) async-start(), calls=%async_computation.10 | async-start | bytes 3276800 | tf_op jit(solution)/shard_map/reduce_scatter | solution.py:69
  672.7 59.8 %collective-permute-start.33 = (bf16[4,1,1,256,1280]{4,3,2,1,0:T(8,128)(2,1)S(1)}, bf16[4,1,1,256,1280]{4,3,2,1,0:T(8,128)(2,1)S(1)}, u32[]{:S(2)}, u32[]{:S(2)}) collective-permute-start(bf16[4,1,1,256,1280]{4,3,2,1,0:T(8,128)(2,1)S(1)} %grad_blocks.11), channel_id=1, source_target_pairs={{0,4},{4,0},{8,12},{12,8},{16,20},{20,16},{24,28},{28,24},{1,5},{5... | collective-permute-start | bytes 7864328 | tf_op jit(solution)/shard_map/ppermute | solution.py:46
  687.7 134.5 %collective-permute-start.34 = (bf16[4,1,1,256,2048]{4,3,2,1,0:T(8,128)(2,1)}, bf16[4,1,1,256,2048]{4,3,2,1,0:T(8,128)(2,1)}, u32[]{:S(2)}, u32[]{:S(2)}) collective-permute-start(bf16[4,1,1,256,2048]{4,3,2,1,0:T(8,128)(2,1)} %grad_blocks.8), channel_id=1, source_target_pairs={{0,4},{4,0},{8,12},{12,8},{16,20},{20,16},{24,28},{28,24},{1,5},{5... | collective-permute-start | bytes 12582920 | tf_op jit(solution)/shard_map/ppermute | solution.py:46
  734.7 313.4 %reduce-scatter.11.cloned.1.call-start = ((), (), s32[]{:S(2)}) async-start(), calls=%async_computation.11 | async-start | bytes 5242880 | tf_op jit(solution)/shard_map/reduce_scatter | solution.py:69
  746.8 83.1 %copy-start.22 = (bf16[3,768,512]{2,1,0:T(8,128)(2,1)S(1)}, bf16[3,768,512]{2,1,0:T(8,128)(2,1)}, u32[]{:S(2)}) copy-start(bf16[3,768,512]{2,1,0:T(8,128)(2,1)} %attend_back.1.refs_1_) | copy-start | bytes 7077892
  840.6 214.6 %reduce-scatter.7.cloned.1.call-start = ((), (), s32[]{:S(2)}) async-start(), calls=%async_computation.9 | async-start | bytes 3932160 | tf_op jit(solution)/shard_map/reduce_scatter | solution.py:69
  864.9 11.9 %collective-permute-start.35 = (bf16[384,2048]{1,0:T(8,128)(2,1)}, bf16[384,2048]{1,0:T(8,128)(2,1)}, u32[]{:S(2)}, u32[]{:S(2)}) collective-permute-start(bf16[384,2048]{1,0:T(8,128)(2,1)} %constant_dynamic-slice_fusion.1), channel_id=1, source_target_pairs={{0,1},{1,0},{2,3},{3,2},{4,5},{5,4},{6,7},{7,6},{8,9},{9,8},{10,11... | collective-permute-start | bytes 4718600 | tf_op jit(solution)/shard_map/ppermute | solution.py:56
  876.7 4.4 collective-permute-start.12
  880.1 49.9 %collective-permute-start.36 = (bf16[384,2048]{1,0:T(8,128)(2,1)}, bf16[384,2048]{1,0:T(8,128)(2,1)}, u32[]{:S(2)}, u32[]{:S(2)}) collective-permute-start(bf16[384,2048]{1,0:T(8,128)(2,1)} %add_convert_fusion.9), channel_id=1, source_target_pairs={{0,2},{1,3},{2,0},{3,1},{4,6},{5,7},{6,4},{7,5},{8,10},{9,11},{10,... | collective-permute-start | bytes 4718600 | tf_op jit(solution)/shard_map/ppermute | solution.py:56
  883.1 45.4 %collective-permute-start.13 = (bf16[128,2048]{1,0:T(8,128)(2,1)}, bf16[128,2048]{1,0:T(8,128)(2,1)}, u32[]{:S(2)}, u32[]{:S(2)}) collective-permute-start(bf16[128,2048]{1,0:T(8,128)(2,1)} %add_convert_fusion.15), channel_id=1, source_target_pairs={{0,2},{1,3},{2,0},{3,1},{4,6},{5,7},{6,4},{7,5},{8,10},{9,11},{10,... | collective-permute-start | bytes 1572872 | tf_op jit(solution)/shard_map/ppermute | solution.py:56
  884.8 70.4 %collective-permute-start.38 = (bf16[4,1,3,256,512]{4,3,2,1,0:T(8,128)(2,1)}, bf16[4,1,3,256,512]{4,3,2,1,0:T(8,128)(2,1)}, u32[]{:S(2)}, u32[]{:S(2)}) collective-permute-start(bf16[4,1,3,256,512]{4,3,2,1,0:T(8,128)(2,1)} %copy-done.28), channel_id=1, source_target_pairs={{0,4},{4,0},{8,12},{12,8},{16,20},{20,16},{24,28},{28,24},{1,5},{5... | collective-permute-start | bytes 9437192 | tf_op jit(solution)/shard_map/ppermute | solution.py:46
  929.8 5.1 collective-permute-start.14
  933.6 6.8 collective-permute-start.37
  970.6 12.5 %collective-permute-start.42 = (f32[4,2048]{1,0:T(4,128)S(1)}, f32[4,2048]{1,0:T(4,128)S(1)}, u32[]{:S(2)}, u32[]{:S(2)}) collective-permute-start(f32[4,2048]{1,0:T(4,128)S(1)} %pad_maximum_fusion.10), channel_id=1, source_target_pairs={{0,1},{1,0},{2,3},{3,2},{4,5},{5,4},{6,7},{7,6},{8,9},{9,8},{10,11... | collective-permute-start | bytes 98312 | tf_op jit(solution)/shard_map/ppermute | solution.py:127
  979.0 20.9 %all-to-all-start.2 = ((bf16[8,1,8,2048]{3,2,1,0:T(8,128)(2,1)}), bf16[8,1,8,2048]{3,2,1,0:T(8,128)(2,1)}, u32[]{:S(2)}, u32[]{:S(2)}) async-start(bf16[8,1,8,2048]{3,2,1,0:T(8,128)(2,1)} %fusion.58), calls=%async_computation.3 | async-start | bytes 524288 | tf_op jit(solution)/shard_map/all_to_all | solution.py:549
  983.2 4.0 collective-permute-start.43
  984.5 21.9 %collective-permute-start.41 = (bf16[256,1280]{1,0:T(8,128)(2,1)}, bf16[256,1280]{1,0:T(8,128)(2,1)}, u32[]{:S(2)}, u32[]{:S(2)}) collective-permute-start(bf16[256,1280]{1,0:T(8,128)(2,1)} %slice_bitcast_fusion.1), channel_id=1, source_target_pairs={{0,4},{4,0},{8,12},{12,8},{16,20},{20,16},{24,28},{28,24},{1,5},{5... | collective-permute-start | bytes 1966088 | tf_op jit(solution)/shard_map/ppermute | solution.py:46
  987.2 20.6 %collective-permute-start.44 = (f32[4,2048]{1,0:T(4,128)S(1)}, f32[4,2048]{1,0:T(4,128)S(1)}, u32[]{:S(2)}, u32[]{:S(2)}) collective-permute-start(f32[4,2048]{1,0:T(4,128)S(1)} %fusion.127), channel_id=1, source_target_pairs={{0,4},{4,0},{8,12},{12,8},{16,20},{20,16},{24,28},{28,24},{1,5},{5... | collective-permute-start | bytes 98312 | tf_op jit(solution)/shard_map/ppermute | solution.py:127
  1002.2 19.3 %all-to-all-start.3 = ((bf16[8,1,8,2048]{3,2,1,0:T(8,128)(2,1)}), bf16[8,1,8,2048]{3,2,1,0:T(8,128)(2,1)}, u32[]{:S(2)}, u32[]{:S(2)}) async-start(bf16[8,1,8,2048]{3,2,1,0:T(8,128)(2,1)} %fusion.59), calls=%async_computation.4 | async-start | bytes 524288 | tf_op jit(solution)/shard_map/all_to_all | solution.py:550
  1007.8 21.1 %collective-permute-start.45 = (f32[4,2048]{1,0:T(4,128)S(1)}, f32[4,2048]{1,0:T(4,128)S(1)}, u32[]{:S(2)}, u32[]{:S(2)}) collective-permute-start(f32[4,2048]{1,0:T(4,128)S(1)} %add.422), channel_id=1, source_target_pairs={{0,8},{4,12},{8,0},{12,4},{16,24},{20,28},{24,16},{28,20},{1,9},{5... | collective-permute-start | bytes 98312 | tf_op jit(solution)/shard_map/ppermute | solution.py:127
  1021.5 7.9 collective-permute-start.39
  1028.9 10.7 collective-permute-start.46
  1031.4 10.0 collective-permute-start.40
  (95 other events, 705.1 us)
Sparse Core Ops, SparseCore 0:
  9.6 88.1 all-gather.14
  99.3 79.7 all-gather.16
  180.7 79.2 all-gather.18
  261.4 26.4 all-gather.20
  289.4 27.4 all-gather.22
  635.4 91.2 reduce-scatter.4
  734.8 49.4 reduce-scatter.8
  840.8 74.1 reduce-scatter.10
  970.9 67.5 reduce-scatter.6

commit v2 on v1

--- a/solution.py
+++ b/solution.py
@@ -22,6 +22,7 @@
 ROPE_BASE = 10000.0
 MASKED = -1e30
 
+LIGHT = pl.CostEstimate(flops=1, bytes_accessed=1, transcendentals=0)
 BF = jnp.bfloat16
 F32 = jnp.float32
 
@@ -130,6 +131,7 @@
 
 
 def tensor_near(part):
+    part = part.astype(BF)
     low = lax.axis_index("tensor") % 2
     half = part.shape[0] // 2
     kept = lax.dynamic_slice_in_dim(part, low * half, half, 0)
@@ -159,42 +161,6 @@
 
 def tensor_sum(part):
     return whole_rows(*tensor_halves(part))
-
-
-def back_columns(pull_logits, table, gaps):
-    slices = 4
-    step = table.shape[0] // slices
-    groups = lax.axis_size("dp")
-    product = lambda i: dot(pull_logits, table[i * step : (i + 1) * step], NT).astype(BF)
-    if lax.axis_size("tensor") != 4 or groups & (groups - 1):
-        return gather_small(gaps), [tensor_halves(product(i)) for i in range(slices)]
-    steps = groups.bit_length() - 1
-    held, hops = gaps[None], 0
-    near, far, parts = [], [], []
-    for i in range(slices):
-        if i:
-            share = -(-steps // (slices - 1))
-            for _ in range(min(share, steps - hops)):
-                held = gather_step(held, 1 << hops)
-                hops += 1
-        waits = [pull_logits, held]
-        if i >= 2:
-            near.append(tensor_near(parts[i - 2]))
-            waits.append(near[-1])
-        if i >= 3:
-            far.append(tensor_far(near[i - 3]))
-            waits.append(far[-1])
-        waits = lax.optimization_barrier(tuple(waits))
-        pull_logits, held = waits[:2]
-        if i >= 2:
-            near[-1] = waits[2]
-        if i >= 3:
-            far[-1] = waits[3]
-        parts.append(product(i))
-    near += [tensor_near(parts[i]) for i in range(slices - 2, slices)]
-    far += [tensor_far(near[i]) for i in range(slices - 3, slices)]
-    low = (lax.axis_index("tensor") % 2).reshape(1)
-    return held, [(kept, tensor_swap(kept, 1), low) for kept in far]
 
 
 def tensor_join(part):
@@ -307,9 +273,7 @@
         out_specs=[columns(count - skip), columns(count - skip), columns(count), columns(count)],
         out_shape=[shape(count - skip), shape(count - skip), shape(count), shape(count)],
         compiler_params=pltpu.CompilerParams(vmem_limit_bytes=48 * 2**20),
-        cost_estimate=pl.CostEstimate(
-            flops=2 * count * width * inner * 3, bytes_accessed=20 * 2**20, transcendentals=0
-        ),
+        cost_estimate=LIGHT,
         name="attend",
     )(first_in, weights, tables)
 
@@ -365,15 +329,12 @@
         out_specs=pl.BlockSpec((3, count, block), lambda h: (0, 0, h)),
         out_shape=jax.ShapeDtypeStruct((3, count, inner), BF),
         compiler_params=pltpu.CompilerParams(vmem_limit_bytes=48 * 2**20),
-        cost_estimate=pl.CostEstimate(
-            flops=2**31, bytes_accessed=8 * 2**20, transcendentals=2**20
-        ),
+        cost_estimate=LIGHT,
         name="attend_back",
     )(back_attended, query, keys, values, tables)
 
 
-def hidden_body(skip, x_ref, w_ref, out_ref, *slope_ref):
-    before = dot(x_ref[...], w_ref[...], NN)
+def hidden_body(skip, before, out_ref, *slope_ref):
     share = 0.5 + 0.5 * lax.erf(before * 0.5**0.5)
     out_ref[...] = (before * share).astype(BF)
     if slope_ref:
@@ -382,29 +343,97 @@
         slope_ref[0][...] = share[skip:] + kept * bell
 
 
+def over_shards(pair, low_ref, x_ref, w_refs, rows_first):
+    total = None
+    ring = w_refs[0].shape[0]
+    slab = w_refs[0].shape[1 if rows_first else 2]
+    for side in range(pair):
+        for r in range(ring):
+            at = pl.multiple_of(shard_of(r, side, low_ref, pair) * slab, slab)
+            term = dot(x_ref[:, pl.ds(at, slab)], w_refs[side][r], NN if rows_first else NT)
+            total = term if total is None else total + term
+    return total
+
+
 def hidden_units(second_in, expand, skip=None):
     count, width = second_in.shape
-    units = expand.shape[1]
+    pair = dp_shape()[1]
+    if isinstance(expand, tuple) and expand[0].shape[1] % 128:
+        expand = rows_of(*expand).reshape(width, -1)
+    sides = isinstance(expand, tuple)
+    units = expand[0].shape[2] if sides else expand.shape[1]
     block = 256
-    column = lambda rows: pl.BlockSpec((rows, block), lambda i: (0, i))
+    column = lambda rows: pl.BlockSpec((rows, block), lambda i, l: (0, i))
+    weights = list(expand[:pair]) if sides else [expand]
+    weight_specs = [
+        pl.BlockSpec(x.shape[:2] + (block,), lambda i, l: (0, 0, i)) if sides else column(width)
+        for x in weights
+    ]
     out_specs, out_shape = [column(count)], [jax.ShapeDtypeStruct((count, units), BF)]
     if skip is not None:
         out_specs.append(column(count - skip))
         out_shape.append(jax.ShapeDtypeStruct((count - skip, units), F32))
+
+    def body(low_ref, x_ref, *refs):
+        w_refs, out_refs = refs[: len(weights)], refs[len(weights) :]
+        if sides:
+            before = over_shards(pair, low_ref, x_ref, w_refs, True)
+        else:
+            before = dot(x_ref[...], w_refs[0][...], NN)
+        hidden_body(skip, before, *out_refs)
+
     return pl.pallas_call(
-        lambda *refs: hidden_body(skip, *refs),
-        grid=(units // block,),
-        in_specs=[pl.BlockSpec((count, width), lambda i: (0, 0)), column(width)],
-        out_specs=out_specs,
+        body,
+        grid_spec=pltpu.PrefetchScalarGridSpec(
+            num_scalar_prefetch=1,
+            grid=(units // block,),
+            in_specs=[pl.BlockSpec((count, width), lambda i, l: (0, 0)), *weight_specs],
+            out_specs=out_specs,
+        ),
         out_shape=out_shape,
         compiler_params=pltpu.CompilerParams(vmem_limit_bytes=48 * 2**20),
-        cost_estimate=pl.CostEstimate(
-            flops=2 * count * width * units,
-            bytes_accessed=2 * width * units + 8 * count * units,
-            transcendentals=count * units,
+        cost_estimate=LIGHT,
+        name="hidden",
+    )(dp_place()[1].reshape(1), second_in, *weights)
+
+
+def pull_units(branch_low, weights, slope=None):
+    rows, width = branch_low.shape
+    pair = dp_shape()[1]
+    units, slab = weights[0].shape[1:]
+    if slab % 128:
+        out = dot(branch_low, columns_of(*weights), NT)
+        return (out if slope is None else out * slope).astype(BF)
+    block = 256
+    weights = list(weights[:pair])
+    column = pl.BlockSpec((rows, block), lambda i, l: (0, i))
+
+    def body(low_ref, x_ref, *refs):
+        out = over_shards(pair, low_ref, x_ref, refs[:pair], False)
+        if slope is not None:
+            out = out * refs[pair][...]
+        refs[-1][...] = out.astype(BF)
+
+    return pl.pallas_call(
+        body,
+        grid_spec=pltpu.PrefetchScalarGridSpec(
+            num_scalar_prefetch=1,
+            grid=(units // block,),
+            in_specs=[
+                pl.BlockSpec((rows, width), lambda i, l: (0, 0)),
+                *(
+                    pl.BlockSpec((x.shape[0], block, slab), lambda i, l: (0, i, 0))
+                    for x in weights
+                ),
+                *([] if slope is None else [column]),
+            ],
+            out_specs=column,
         ),
-        name="hidden",
-    )(second_in, expand)
+        out_shape=jax.ShapeDtypeStruct((rows, units), BF),
+        compiler_params=pltpu.CompilerParams(vmem_limit_bytes=48 * 2**20),
+        cost_estimate=LIGHT,
+        name="pull_units",
+    )(dp_place()[1].reshape(1), branch_low, *weights, *([] if slope is None else [slope]))
 
 
 def shard_of(r, side, low, pair):
@@ -444,33 +473,18 @@
         ),
         out_shape=jax.ShapeDtypeStruct((ring, len(sides), parts, slab, width), BF),
         compiler_params=pltpu.CompilerParams(vmem_limit_bytes=48 * 2**20),
-        cost_estimate=pl.CostEstimate(
-            flops=2 * rows * slab * ring * len(sides) * parts * width,
-            bytes_accessed=2 * slab * ring * len(sides) * parts * width,
-            transcendentals=0,
-        ),
+        cost_estimate=LIGHT,
         name="grad_blocks",
     )(low, left, right)
 
 
-def branch_body(pair, x_ref, y_ref, *refs):
-    hidden_refs, attend_refs, out_ref = refs[:pair], refs[pair : 2 * pair], refs[-1]
-
-    def write(side):
-        out_ref[...] = (
-            dot(x_ref[...], hidden_refs[side][0], NN) + dot(y_ref[...], attend_refs[side][0], NN)
-        ).astype(BF)
-
-    for side in range(pair):
-        pl.when(pl.program_id(1) == side)(lambda: write(side))
-
-
-def branch_terms(hidden, attended, contract, attend_out, start, count):
+def branch_terms(hidden, attended, contract, attend_out, blocks, half):
     groups, pair, ring = dp_shape()
     low = dp_place()[1].reshape(1)
     slab = contract[0].shape[2]
+    count = half * len(blocks)
     if slab % 128:
-        rows = slice(start, start + count)
+        rows = slice(blocks[0] * half, blocks[0] * half + count)
         out = 0.0
         for x, sides in ((hidden[rows], contract), (attended[rows], attend_out)):
             if pair == 2:
@@ -479,15 +493,28 @@
             out = out + jnp.einsum("nf,sfc->nsc", x, weight, preferred_element_type=F32)
         return out.reshape(count, groups * slab).astype(BF)
     weights = [*contract[:pair], *attend_out[:pair]]
-    units, inner = hidden.shape[1], attended.shape[1]
+    row_block = lambda x, b: pl.BlockSpec((half, x.shape[1]), lambda r, s, l: (b, 0))
+
+    def body(low_ref, *refs):
+        x_refs, refs = refs[: 2 * len(blocks)], refs[2 * len(blocks) :]
+
+        def write(side):
+            for i in range(len(blocks)):
+                refs[-1][i * half : (i + 1) * half] = (
+                    dot(x_refs[2 * i][...], refs[side][0], NN)
+                    + dot(x_refs[2 * i + 1][...], refs[pair + side][0], NN)
+                ).astype(BF)
+
+        for side in range(pair):
+            pl.when(pl.program_id(1) == side)(lambda: write(side))
+
     return pl.pallas_call(
-        lambda low_ref, *refs: branch_body(pair, *refs),
+        body,
         grid_spec=pltpu.PrefetchScalarGridSpec(
             num_scalar_prefetch=1,
             grid=(ring, pair),
             in_specs=[
-                pl.BlockSpec((count, units), lambda r, s, l: (start // count, 0)),
-                pl.BlockSpec((count, inner), lambda r, s, l: (start // count, 0)),
+                *(row_block(x, b) for b in blocks for x in (hidden, attended)),
                 *(pl.BlockSpec((1,) + x.shape[1:], lambda r, s, l: (r, 0, 0)) for x in weights),
             ],
             out_specs=pl.BlockSpec(
@@ -496,13 +523,51 @@
         ),
         out_shape=jax.ShapeDtypeStruct((count, groups * slab), BF),
         compiler_params=pltpu.CompilerParams(vmem_limit_bytes=48 * 2**20),
-        cost_estimate=pl.CostEstimate(
-            flops=2 * count * (units + inner) * groups * slab,
-            bytes_accessed=2 * (units + inner) * groups * slab,
-            transcendentals=0,
+        cost_estimate=LIGHT,
+        name="branch",
+    )(low, *[hidden, attended] * len(blocks), *weights)
+
+
+def shard_terms(lefts, weights):
+    groups, pair, ring = dp_shape()
+    low = dp_place()[1].reshape(1)
+    weights = list(weights[:pair])
+    count = lefts.shape[1]
+    parts, slab, depth = weights[0].shape[1:]
+    if slab % 128:
+        whole = by_side(weights[0], weights[1], 1) if pair == 2 else weights[0]
+        whole = whole.reshape(groups, parts, slab, depth)
+        out = jnp.einsum("pnk,gpsk->ngs", lefts, whole, preferred_element_type=F32)
+        return out.reshape(count, groups * slab)
+
+    def body(low_ref, x_ref, *refs):
+        def write(side):
+            total = dot(x_ref[0], refs[side][0, 0], NT)
+            for i in range(1, parts):
+                total = total + dot(x_ref[i], refs[side][0, i], NT)
+            refs[-1][...] = total
+
+        for side in range(pair):
+            pl.when(pl.program_id(1) == side)(lambda: write(side))
+
+    return pl.pallas_call(
+        body,
+        grid_spec=pltpu.PrefetchScalarGridSpec(
+            num_scalar_prefetch=1,
+            grid=(ring, pair),
+            in_specs=[
+                pl.BlockSpec(lefts.shape, lambda r, s, l: (0, 0, 0)),
+                *(pl.BlockSpec((1,) + x.shape[1:], lambda r, s, l: (r, 0, 0, 0)) for x in weights),
+            ],
+            out_specs=pl.BlockSpec(
+                (count, slab), lambda r, s, l: (0, shard_of(r, s, l, pair))
+            ),
         ),
-        name="branch",
-    )(low, hidden, attended, *weights)
+        out_shape=jax.ShapeDtypeStruct((count, groups * slab), F32),
+        compiler_params=pltpu.CompilerParams(vmem_limit_bytes=48 * 2**20),
+        cost_estimate=LIGHT,
+        name="shard_terms",
+    )(low, lefts, *weights)
 
 
 def out_body(x_ref, mine_ref, other_ref, low_ref, unit_ref, low_unit_ref, scale_ref, out_ref):
@@ -535,11 +600,12 @@
             jax.ShapeDtypeStruct((rows, width), BF),
         ],
         compiler_params=pltpu.CompilerParams(vmem_limit_bytes=48 * 2**20),
+        cost_estimate=LIGHT,
         name="out_rows",
     )(x, mine, other, low)
 
 
-def borrow_rows(tail, order, *first):
+def borrow_rows(tail, order, first=(), last=()):
     groups = lax.axis_size("dp")
     parts = lax.axis_size("tensor")
     count, rows, width = tail.shape
@@ -551,16 +617,140 @@
         jnp.take(spread, order, axis=0), "dp", split_axis=0, concat_axis=0, tiled=True
     )
     landed = landed.swapaxes(0, 1).reshape(count, share, width)
-    return tensor_join(landed).swapaxes(0, 1).reshape(count, rows, width)
-
-
-def head_stats(unit_low, table, local_targets):
-    logits = dot(unit_low, table, NN)
-    peak = jnp.max(logits, axis=-1)
-    total = jnp.sum(jnp.exp(logits - peak[:, None]), axis=-1)
-    target_hit = jnp.arange(table.shape[1], dtype=jnp.int32)[None, :] == local_targets[:, None]
-    picked = jnp.sum(jnp.where(target_hit, logits, 0.0), axis=-1)
-    return jnp.stack([peak, total, picked]), logits, target_hit
+    return tensor_join(after(landed, *last)).swapaxes(0, 1).reshape(count, rows, width)
+
+
+TILE = 1280
+CHUNK = 256
+
+
+def head_body(vocab, x_ref, w_ref, t_ref, *refs):
+    logits_ref, stats_ref, peak_ref, total_ref, picked_ref = refs if len(refs) == 5 else (None, *refs)
+    step = pl.program_id(0)
+
+    @pl.when(step == 0)
+    def _():
+        peak_ref[...] = jnp.full(peak_ref.shape, MASKED, F32)
+        total_ref[...] = jnp.zeros(total_ref.shape, F32)
+        picked_ref[...] = jnp.zeros(picked_ref.shape, F32)
+
+    x, target = x_ref[...], t_ref[...]
+    lanes = lax.broadcasted_iota(jnp.int32, (x.shape[0], 128), 1)
+    for c in range(0, TILE, CHUNK):
+        logits = dot(x, w_ref[c : c + CHUNK], NT)
+        if logits_ref is not None:
+            logits_ref[:, c : c + CHUNK] = logits
+        parts = []
+        picked = picked_ref[...]
+        for d in range(0, CHUNK, 128):
+            column = lanes + (step * TILE + c + d)
+            part = jnp.where(column < vocab, logits[:, d : d + 128], MASKED)
+            picked = picked + jnp.where(column == target, part, 0.0)
+            parts.append(part)
+        picked_ref[...] = picked
+        old = peak_ref[...]
+        peak = old
+        for part in parts:
+            peak = jnp.maximum(peak, part)
+        total = total_ref[...] * jnp.exp(old - peak)
+        for part in parts:
+            total = total + jnp.exp(part - peak)
+        peak_ref[...] = peak
+        total_ref[...] = total
+
+    @pl.when(step == pl.num_programs(0) - 1)
+    def _():
+        peak = jnp.max(peak_ref[...], axis=1, keepdims=True)
+        total = jnp.sum(total_ref[...] * jnp.exp(peak_ref[...] - peak), axis=1, keepdims=True)
+        picked = jnp.sum(picked_ref[...], axis=1, keepdims=True)
+        rows = jnp.where(lanes == 0, peak, jnp.where(lanes == 1, total, picked))
+        stats_ref[...] = rows.T[:8]
+
+
+def head_stats(unit_low, table, local_targets, keep):
+    rows, width = unit_low.shape
+    vocab = table.shape[0]
+    tiles = pl.cdiv(vocab, TILE)
+    out_specs = [pl.BlockSpec((8, rows), lambda i: (0, 0))]
+    out_shape = [jax.ShapeDtypeStruct((8, rows), F32)]
+    if keep:
+        out_specs.insert(0, pl.BlockSpec((rows, TILE), lambda i: (0, i)))
+        out_shape.insert(0, jax.ShapeDtypeStruct((rows, vocab), F32))
+    out = pl.pallas_call(
+        lambda *refs: head_body(vocab, *refs),
+        grid=(tiles,),
+        in_specs=[
+            pl.BlockSpec((rows, width), lambda i: (0, 0)),
+            pl.BlockSpec((TILE, width), lambda i: (i, 0)),
+            pl.BlockSpec((rows, 1), lambda i: (0, 0)),
+        ],
+        out_specs=out_specs,
+        out_shape=out_shape,
+        scratch_shapes=[pltpu.VMEM((rows, 128), F32)] * 3,
+        compiler_params=pltpu.CompilerParams(vmem_limit_bytes=48 * 2**20),
+        cost_estimate=LIGHT,
+        name="head",
+    )(unit_low, table, local_targets[:, None])
+    return out[-1][:3], out[0] if keep else None
+
+
+def head_pull_body(vocab, tiles, x_ref, w_ref, row_ref, t_ref, out_ref, pull_ref, total_ref):
+    step = pl.program_id(0)
+
+    @pl.when(step == 0)
+    def _():
+        total_ref[...] = jnp.zeros(total_ref.shape, F32)
+
+    def add(masked):
+        for c in range(0, TILE, CHUNK):
+            at = slice(c, c + CHUNK)
+            column = lax.broadcasted_iota(jnp.int32, (x_ref.shape[0], CHUNK), 1)
+            column = column + (step * TILE + c)
+            pull = jnp.where(column == t_ref[...], 1.0, 0.0) - jnp.exp(
+                x_ref[:, at] - row_ref[:, 0:1]
+            ) * row_ref[:, 1:2]
+            if masked:
+                pull = jnp.where(column < vocab, pull, 0.0)
+            pull_ref[:, at] = pull.astype(BF)
+        width = w_ref.shape[1]
+        for c in range(0, width, width // 4):
+            at = slice(c, c + width // 4)
+            weight = w_ref[:, at]
+            if masked:
+                seen = lax.broadcasted_iota(jnp.int32, weight.shape, 0)
+                seen = seen < vocab - (tiles - 1) * TILE
+                weight = jnp.where(seen, weight.astype(F32), 0.0).astype(BF)
+            total_ref[:, at] += dot(pull_ref[...], weight, NN)
+
+    pl.when(step < tiles - 1)(lambda: add(False))
+    pl.when(step == tiles - 1)(lambda: add(True))
+
+    @pl.when(step == tiles - 1)
+    def _():
+        out_ref[...] = total_ref[...].astype(BF)
+
+
+def head_pull(logits, table, row, targets):
+    rows, vocab = logits.shape
+    width = table.shape[1]
+    tiles = pl.cdiv(vocab, TILE)
+    whole = lambda x: pl.BlockSpec(x, lambda i: (0, 0))
+    return pl.pallas_call(
+        lambda *refs: head_pull_body(vocab, tiles, *refs),
+        grid=(tiles,),
+        in_specs=[
+            pl.BlockSpec((rows, TILE), lambda i: (0, i)),
+            pl.BlockSpec((TILE, width), lambda i: (i, 0)),
+            whole((rows, 2)),
+            whole((rows, 1)),
+        ],
+        out_specs=whole((rows, width)),
+        out_shape=jax.ShapeDtypeStruct((rows, width), BF),
+        scratch_shapes=[pltpu.VMEM((rows, TILE), BF), pltpu.VMEM((rows, width), F32)],
+        compiler_params=pltpu.CompilerParams(vmem_limit_bytes=48 * 2**20),
+        cost_estimate=LIGHT,
+        name="head_pull",
+    )(logits, table, row, targets[:, None])
 
 
 def join_stats(stats):
@@ -636,16 +826,18 @@
     contract_mine = gather_ring(contract_copy)
     out_mine = gather_ring(attend_out_copy)
     out_other = None if out_came is None else gather_ring(out_came)
+    norms_full = norms_full if out_came is None else after(norms_full, out_came)
 
     other = borrow_rows(jnp.stack([frozen_rows[half:], policy_rows[half:]]), partner)
+    other, attend_mine = lax.optimization_barrier((other, attend_mine))
     tables = turn_tables(half)
 
     frozen_work = jnp.concatenate([frozen_rows, other[0]], axis=0).astype(F32)
     frozen_unit, _ = normalize(frozen_work)
     frozen_first_in = (frozen_unit * frozen_norms[0] + frozen_norms[1]).astype(BF)
     frozen_second_in = (frozen_unit[half:] * frozen_norms[2] + frozen_norms[3]).astype(BF)
-    frozen_first_in, frozen_second_in, attend_mine = lax.optimization_barrier(
-        (frozen_first_in, frozen_second_in, attend_mine)
+    frozen_first_in, frozen_second_in, norms_full = lax.optimization_barrier(
+        (frozen_first_in, frozen_second_in, norms_full)
     )
     attend_other = swap(attend_mine)
     frozen_attended = attention(frozen_first_in, frozen_in, tables, half, half)[0]
@@ -659,10 +851,12 @@
         jnp.concatenate([frozen_rows[half:], other[0]], axis=0), tensor_halves(frozen_part)
     )[1]
     vocab_local = vocab_table.shape[1]
+    table = vocab_table.T
     targets = (
         jnp.concatenate([next_tokens[own_index], next_tokens[other_index]])
         - lax.axis_index("tensor") * vocab_local
     )
+    targets = jnp.where((targets >= 0) & (targets < vocab_local), targets, -1)
     work = jnp.concatenate([policy_rows, other[1]], axis=0).astype(F32)
     unit, inverse_scale = normalize(work)
     first_in = (unit * norms_full[0] + norms_full[1]).astype(BF)
@@ -674,31 +868,21 @@
         (second_in, contract_mine, attended, expand_other)
     )
     contract_other = swap(contract_mine)
-    expand = rows_of(expand_mine, expand_other).reshape(width, units)
-    hidden, slope_units = hidden_units(second_in, expand, half)
-    frozen_low, hidden = lax.optimization_barrier((frozen_low, hidden))
-    frozen_stats, _, _ = head_stats(frozen_low, vocab_table, targets)
+    frozen_low, second_in = lax.optimization_barrier((frozen_low, second_in))
+    frozen_stats, _ = head_stats(frozen_low, table, targets, False)
     frozen_peak, frozen_total, frozen_picked = join_stats(frozen_stats)
-    hidden, frozen_peak = lax.optimization_barrier((hidden, frozen_peak))
+    second_in, frozen_peak = lax.optimization_barrier((second_in, frozen_peak))
+    hidden, slope_units = hidden_units(second_in, (expand_mine, expand_other), half)
 
     contract, attend_out = (contract_mine, contract_other), (out_mine, out_other)
     scored_halves = tensor_halves(
-        jnp.concatenate(
-            [
-                branch_terms(hidden, attended, contract, attend_out, g * half, half)
-                for g in (1, 2)
-            ],
-            axis=0,
-        )
+        branch_terms(hidden, attended, contract, attend_out, (1, 2), half)
     )
     unit_out, unit_low, inverse_out, out_low = out_rows(
         jnp.concatenate([policy_rows[half:], other[1]], axis=0), scored_halves
     )
-    stats, logits, target_hit = head_stats(unit_low, vocab_table, targets)
+    stats, logits = head_stats(unit_low, table, targets, True)
     peak, total, picked = join_stats(stats)
-    softmax_part = jnp.exp(logits - peak[:, None]) * (1.0 / total)[:, None]
-    pull_logits = (target_hit.astype(F32) - softmax_part).astype(BF)
-
     log_chance = jnp.stack(
         [picked - peak - jnp.log(total), frozen_picked - frozen_peak - jnp.log(frozen_total)]
     )
@@ -712,8 +896,10 @@
     own_mean = jnp.sum(log_chance[:, :half] * own_live, axis=1) / own_total
     other_mean = jnp.sum(log_chance[:, half:] * other_live, axis=1) / other_total
     gaps = jnp.stack([own_mean[0] - own_mean[1], other_mean[0] - other_mean[1]])
-    every, back_parts = back_columns(pull_logits, vocab_table, gaps)
-    back_parts = [whole_rows(*part) for part in back_parts]
+    row = jnp.stack([peak, 1.0 / total], axis=1)
+    every = gather_small(gaps)
+    back_part = head_pull(logits, table, row, targets)
+    back_sum = tensor_sum(back_part)
     drift = jnp.sum(every[:, 1]) / groups
     sign = (2 * desirable - 1).astype(F32)
     settled = jax.nn.sigmoid(KTO_BETA * sign * (every[:, 0] - jax.nn.softplus(drift)))
@@ -724,7 +910,7 @@
         [-slope[own_index] * own_live / own_total, pull * other_live / other_total]
     )
 
-    back_unit = row_weight[:, None] * jnp.concatenate(back_parts, axis=1).astype(F32)
+    back_unit = row_weight[:, None] * back_sum.astype(F32)
     back_out = normalize_back(back_unit, unit_out, inverse_out)
     branch_low = back_out.astype(BF)
 
@@ -732,32 +918,36 @@
     near_features, far_features = features_scored[:, :cut][None], features_scored[:, cut:][None]
     near_sent = grad_blocks(branch_low, near_features, (1,))
     near_came = swap(near_sent)
+    branch_low = after(branch_low, near_sent)
     far_blocks = grad_blocks(branch_low, far_features, range(pair))
     far_back = scatter_ring(far_blocks)
 
-    contract_full = columns_of(*contract)
-    back_expand = (dot(branch_low, contract_full, NT) * slope_units).astype(BF)
+    branch_low = after(branch_low, far_blocks)
+    back_expand = pull_units(branch_low, contract, slope_units)
     expand_sent = grad_blocks(second_in[half:], back_expand[None], (1,))
+    near_kept = grad_blocks(after(branch_low, expand_sent), near_features, (0,))
+    near_ring = to_ring(near_kept, near_came)
+    grad_near = scatter_ring(near_ring)[0].astype(F32)
+
+    expand_sent, branch_low, back_expand, near_ring = lax.optimization_barrier(
+        (expand_sent, branch_low, back_expand, near_ring)
+    )
     expand_came = swap(expand_sent)
-    back_attended = dot(branch_low, columns_of(*attend_out), NT).astype(BF)
+    back_attended = pull_units(branch_low, attend_out)
     back_three = attention_back(back_attended, query, keys, values, tables, half)
     attend_sent = grad_blocks(first_in, back_three, (1,))
-    attend_came = swap(attend_sent)
-
-    kept_left = after(branch_low, far_blocks, expand_sent, attend_sent)
-    near_ring = to_ring(grad_blocks(kept_left, near_features, (0,)), near_came)
-    grad_near = scatter_ring(near_ring)[0].astype(F32)
-    second_scored, near_ring, far_back = lax.optimization_barrier(
-        (second_in[half:], near_ring, far_back)
-    )
+    second_scored, far_back = lax.optimization_barrier((second_in[half:], far_back, attend_sent))[:2]
     expand_kept = grad_blocks(second_scored, back_expand[None], (0,))
     expand_ring = to_ring(expand_kept, expand_came)
-    grad_expand = scatter_ring(expand_ring)[0].astype(F32)
-    back_expand, back_three, expand_ring = lax.optimization_barrier(
-        (back_expand, back_three, expand_ring)
-    )
-    back_second = dot(back_expand, expand, NT)
-    back_first = sum(dot(back_three[i], attend_in[i], NT) for i in range(3))
+    expand_back = scatter_ring(expand_ring)
+
+    attend_sent, back_expand, back_three, expand_ring = lax.optimization_barrier(
+        (attend_sent, back_expand, back_three, expand_ring)
+    )
+    attend_came = swap(attend_sent)
+    sided = lambda sides: [x if x is None else x[:, None] for x in sides]
+    back_second = shard_terms(back_expand[None], sided((expand_mine, expand_other)))
+    back_first = shard_terms(back_three, (attend_mine, attend_other))
 
     unit_scored = unit[half:]
     grad_norms = sum_small(
@@ -774,23 +964,32 @@
     back_h = back_first * norms_full[0] + jnp.pad(
         back_second * norms_full[2], ((half, 0), (0, 0))
     )
-    back_h, attend_came = lax.optimization_barrier((tensor_sum(back_h), attend_came))
+    four = lax.axis_size("tensor") == 4
+    back_h = tensor_near(back_h) if four else lax.psum(back_h.astype(BF), "tensor")
     attend_kept = grad_blocks(after(first_in, back_h), back_three, (0,))
     attend_ring = to_ring(attend_kept, attend_came)
+    across = tensor_swap(back_h, 2) if four else back_h
+    attend_ring, expand_back, across = lax.optimization_barrier((attend_ring, expand_back, across))
+    if four:
+        back_h = (back_h.astype(F32) + across.astype(F32)).astype(BF)
+        low_row = (lax.axis_index("tensor") % 2).reshape(1)
+        back_h = whole_rows(back_h, tensor_swap(back_h, 1), low_row)
+    grad_expand = expand_back[0].astype(F32)
     attend_back = scatter_ring(attend_ring)
+    hidden = after(hidden, attend_ring)
     back_work = normalize_back(
-        after(back_h, attend_ring).astype(F32), unit, inverse_scale
+        back_h.astype(F32), unit, inverse_scale
     ) + jnp.pad(back_out, ((half, 0), (0, 0)))
     out_prompt = work[:half] + tensor_sum(
-        branch_terms(hidden, attended, contract, attend_out, 0, half)
+        branch_terms(hidden, attended, contract, attend_out, (0,), half)
     ).astype(F32)
     mixed = jnp.concatenate([out_prompt.astype(BF), out_low[:half]], axis=0)
     grad_norms = sum_small(after(grad_norms, attend_ring), ("dp",))
     grad_norms = lax.dynamic_slice_in_dim(grad_norms, own_index * slab, slab, 1)
-    returned = borrow_rows(back_work[None, 2 * half :].astype(BF), inverse, attend_ring)[0]
+    returned = borrow_rows(back_work[None, 2 * half :].astype(BF), inverse, (attend_ring,), (attend_back,))[0]
     grad_far = far_back[0, 0].astype(F32)
     if pair == 2:
-        grad_far = grad_far + pair_swap(far_back[1, 0]).astype(F32)
+        grad_far = grad_far + pair_swap(after(far_back[1, 0], attend_ring)).astype(F32)
     grad_join = jnp.concatenate([grad_near.T, grad_far.T], axis=0)
     grad_contract, grad_attend_out = grad_join[:units], grad_join[units:]
     input_grad = jnp.concatenate(

time: 1080 us -> 974 us (0.902)
  matrix products: 175 us -> 9.84 us
  Pallas kernels: 129 us -> 279 us
  other arithmetic: 199 us -> 153 us
  blocking collectives: 43.2 us -> 10.4 us
  local copies, waits for them, and re-layouts: 100 us -> 72.7 us
  waiting for transfers between devices: 344 us -> 363 us
    dot_general x14 -> x2, matrix products: 175 us -> 9.84 us  [dot(): return lax.dot_general(a, b, (dims, ((), ())), preferred_element_type=F32)]
    pallas_call x5 -> x11, Pallas kernels: 50.8 us -> 199 us  [the longest x2 76.7 us: head_stats(): pl.pallas_call(lambda *refs: head_body(vocab, *refs), grid=(tiles,), in_s...]
    all_to_all x1 -> x0, blocking collectives: 32.4 us -> none  [borrow_rows(): lax.all_to_all(jnp.take(spread, order, axis=0), 'dp', split_axis=0, conca...]
    all_gather x5, waiting for transfers between devices: 33.5 us -> 55.3 us  [gather_ring(): return lax.all_gather(piece, 'dp', axis_index_groups=ring_groups())]
    reduce_sum x2 -> x1, other arithmetic: 24 us -> 4.69 us  [per_device(): jnp.sum(back_second * unit_scored, axis=0)]
    all_to_all x1 -> x2, waiting for transfers between devices: 11.6 us -> 29.9 us  [borrow_rows(): lax.all_to_all(jnp.take(spread, order, axis=0), 'dp', split_axis=0, conca...]
    transpose x2 -> x0, other arithmetic: 14.5 us -> none  [columns_of(): return jnp.moveaxis(both, 2, 0).reshape(rows, ring * pair * slab)]
    ppermute x8, waiting for transfers between devices: 167 us -> 155 us  [pair_swap(): return lax.ppermute(value, 'dp', [(i, i ^ 1) for i in range(groups)])]
  transfers between devices with their start and end apart: 59 -> 51, of which waited for: 21 -> 22; matrix products, arithmetic and copies ran while one was open for 34% -> 21% of each run, Pallas kernels for 9% -> 18%
where the time goes in v2:
time: 974 us; the launch traced here: 963 us
  waiting for transfers between devices  363 us (37%)
  Pallas kernels  279 us (29%)
  other arithmetic  153 us (16%)
  local copies, waits for them, and re-layouts  72.7 us (7%)
  starting transfers between devices  50.8 us (5%)
  between operations  23.6 us (2%)
  blocking collectives  10.4 us (1%)
  matrix products  9.84 us (1%)
    ppermute x8, waiting for transfers between devices, pair_swap(): return lax.ppermute(value, 'dp', [(i, i ^ 1) for i in range(groups)])  155 us
    pallas_call x2, Pallas kernels, head_stats(): pl.pallas_call(lambda *refs: head_body(vocab, *refs), grid=(tiles,), in_s...  76.7 us
    ppermute x19, waiting for transfers between devices, tensor_swap(): lax.ppermute(value, 'tensor', [(i, i ^ bit) for i in range(lax.axis_size(...  72.6 us
    all_gather x5, waiting for transfers between devices, gather_ring(): return lax.all_gather(piece, 'dp', axis_index_groups=ring_groups())  55.3 us
    unnamed x192, local copies, waits for them, and re-layouts  43.3 us
    pallas_call x1, Pallas kernels, head_pull(): pl.pallas_call(lambda *refs: head_pull_body(vocab, tiles, *refs), grid=(t...  41.9 us
    pallas_call x7, Pallas kernels, grad_blocks(): pl.pallas_call(lambda low_ref, *refs: grad_body(*refs), grid_spec=pltpu.P...  30.7 us
    all_to_all x2, waiting for transfers between devices, borrow_rows(): lax.all_to_all(jnp.take(spread, order, axis=0), 'dp', split_axis=0, conca...  29.9 us
  transfers between devices with their start and end apart: 51, of which 22 were waited for; matrix products, arithmetic and copies ran while one was open for 21% of the time, Pallas kernels for 18%

profile of v2, /device:TPU:0, one launch (start us, length us, event | category | flops | bytes accessed | tf_op | source)
XLA Modules:
  0.0 962.5 jit_solution(5284761811708282849)
XLA Ops:
  8.7 3.3 fusion.64
  12.9 7.3 all-to-all-start
  20.7 28.1 %all-to-all-done = bf16[8,2,8,2048]{3,2,1,0:T(8,128)(2,1)S(1)} async-done(((bf16[8,2,8,2048]{3,2,1,0:T(8,128)(2,1)}), bf16[8,2,8,2048]{3,2,1,0:T(8,128)(2,1)S(1)}, u32[]{:S(2)}, u32[]{:S(2)}) %all-to-all-start) | async-done | bytes 524320 | tf_op jit(solution)/shard_map/all_to_all | solution.py:615
  50.3 3.6 all-to-all-start.1
  56.1 27.0 %all-to-all-done.1 = bf16[8,2,8,2048]{3,2,1,0:T(8,128)(2,1)S(1)} async-done(((bf16[8,2,8,2048]{3,2,1,0:T(8,128)(2,1)}), bf16[8,2,8,2048]{3,2,1,0:T(8,128)(2,1)S(1)}, u32[]{:S(2)}, u32[]{:S(2)}) %all-to-all-start.1) | async-done | bytes 524320 | tf_op jit(solution)/shard_map/all_to_all | solution.py:616
  88.9 7.3 collective-permute-done
  120.2 3.4 fusion
  124.2 13.0 %attend.2 = (bf16[512,512]{1,0:T(8,128)(2,1)S(1)}, bf16[512,512]{1,0:T(8,128)(2,1)}, bf16[768,512]{1,0:T(8,128)(2,1)}, bf16[768,512]{1,0:T(8,128)(2,1)}) custom-call(bf16[768,2048]{1,0:T(8,128)(2,1)} %get-tuple-element.76.refs_0_, bf16[3,2048,512]{2,1,0:T(8,128)(2,1)} %refs_1_.1, f32[3,768,128]{2,1,0:T(8,128)S(1)} %pad_maximum_fusion.8.refs_2_.refs_4_), custom_call_target="tpu_custom_call" | custom-call | flops 1 | bytes 1 | tf_op jit(solution)/shard_map/attend/pallas_call | solution.py:265
  137.2 8.9 hidden.2
  146.1 7.2 fusion.71
  156.0 22.4 %all-gather.17.cloned.1.call-done = bf16[1024,2048]{1,0:T(8,128)(2,1)} async-done(((bf16[256,2048]{1,0:T(8,128)(2,1)}), bf16[1024,2048]{1,0:T(8,128)(2,1)}) %all-gather.17.cloned.1.call-update) | async-done | bytes 4194320 | tf_op jit(solution)/shard_map/all_gather | solution.py:66
  178.3 6.8 collective-permute-done.6.refs_1_
  191.6 7.4 subtract_multiply_fusion
  200.0 5.6 maximum_select_fusion
  206.3 3.2 copy.229
  209.5 15.1 %attend.3 = (bf16[768,512]{1,0:T(8,128)(2,1)S(1)}, bf16[768,512]{1,0:T(8,128)(2,1)S(1)}, bf16[768,512]{1,0:T(8,128)(2,1)S(1)}, bf16[768,512]{1,0:T(8,128)(2,1)S(1)}) custom-call(bf16[768,2048]{1,0:T(8,128)(2,1)} %get-tuple-element.113.refs_0_, bf16[3,2048,512]{2,1,0:T(8,128)(2,1)} %bitcast.203, f32[3,768,128]{2,1,0:T(8,128)S(1)} %pad_maximum_fusion.8.refs_2_.refs_4_), custom_call_target="tpu_custom_call" | custom-call | flops 1 | bytes 1 | tf_op jit(solution)/shard_map/attend/pallas_call | solution.py:265
  226.3 32.9 %all-gather.19.cloned.1.call-done = bf16[8192,256]{1,0:T(8,128)(2,1)} async-done(((bf16[2048,256]{1,0:T(8,128)(2,1)}), bf16[8192,256]{1,0:T(8,128)(2,1)}) %all-gather.19.cloned.1.call-update) | async-done | bytes 4194320 | tf_op jit(solution)/shard_map/all_gather | solution.py:66
  259.3 16.6 %collective-permute-done.10.refs_1_ = bf16[4,256,2048]{2,1,0:T(8,128)(2,1)} collective-permute-done((bf16[4,256,2048]{2,1,0:T(8,128)(2,1)}, bf16[4,256,2048]{2,1,0:T(8,128)(2,1)}, u32[]{:S(2)}, u32[]{:S(2)}) %collective-permute-start.10) | collective-permute-done | bytes 4194336 | tf_op jit(solution)/shard_map/ppermute | solution.py:47
  282.0 19.5 %collective-permute-done.8 = bf16[256,2048]{1,0:T(8,128)(2,1)} collective-permute-done((bf16[256,2048]{1,0:T(8,128)(2,1)}, bf16[256,2048]{1,0:T(8,128)(2,1)}, u32[]{:S(2)}, u32[]{:S(2)}) %collective-permute-start.8) | collective-permute-done | bytes 1048608 | tf_op jit(solution)/shard_map/ppermute | solution.py:57
  307.1 3.1 pad_maximum_fusion.4.x_ref
  310.2 6.1 out_rows.2
  316.3 37.6 %head.2 = f32[8,512]{1,0:T(8,128)S(1)} custom-call(bf16[512,2048]{1,0:T(8,128)(2,1)S(1)} %get-tuple-element.88.refs_0_, bf16[12576,2048]{1,0:T(8,128)(2,1)} %bitcast.193, s32[512,1]{1,0:T(8,128)S(1)} %and_select_fusion.refs_2_.refs_3_), custom_call_target="tpu_custom_call" | custom-call | flops 1 | bytes 1 | tf_op jit(solution)/shard_map/head/pallas_call | solution.py:679
  353.9 5.2 all-gather.7
  360.3 13.5 %hidden.3 = (bf16[768,2048]{1,0:T(8,128)(2,1)S(1)}, f32[512,2048]{1,0:T(8,128)}) custom-call(s32[1]{0:T(128)} %bitcast.16.low_ref, bf16[768,2048]{1,0:T(8,128)(2,1)} %get-tuple-element.89.x_ref, bf16[4,256,2048]{2,1,0:T(8,128)(2,1)} %bitcast.208, bf16[4,256,2048]{2,1,0:T(8,128)(2,1)} %collective-permute-done.10.refs_1_), custom_call_target="tpu_custom_call" | custom-call | flops 1 | bytes 1 | tf_op jit(solution)/shard_map/hidden/pallas_call | solution.py:385
  377.9 11.3 %branch.2 = bf16[512,2048]{1,0:T(8,128)(2,1)S(1)} custom-call(s32[1]{0:T(128)} %bitcast.16.low_ref, bf16[768,2048]{1,0:T(8,128)(2,1)} %copy-done.2, bf16[768,512]{1,0:T(8,128)(2,1)S(1)} %get-tuple-element.92.refs_1_.refs_3_, bf16[768,2048]{1,0:T(8,128)(2,1)} %copy-done.2, bf16[768,512]{1,0:T(8,128)(2,1)S(1)} %get-tuple-element.92.refs_1_.refs_3_, ...), custom_call_target="tpu_custom_call" | custom-call | flops 1 | bytes 1 | tf_op jit(solution)/shard_map/branch/pallas_call | solution.py:511
  394.0 23.9 %collective-permute-done.13 = bf16[256,2048]{1,0:T(8,128)(2,1)S(1)} collective-permute-done((bf16[256,2048]{1,0:T(8,128)(2,1)S(1)}, bf16[256,2048]{1,0:T(8,128)(2,1)S(1)}, u32[]{:S(2)}, u32[]{:S(2)}) %collective-permute-start.13) | collective-permute-done | bytes 1048608 | tf_op jit(solution)/shard_map/ppermute | solution.py:57
  420.3 3.1 pad_maximum_fusion.5.x_ref
  423.4 5.7 out_rows.3
  429.1 39.0 %head.3 = (f32[512,12576]{1,0:T(8,128)}, f32[8,512]{1,0:T(8,128)S(1)}) custom-call(bf16[512,2048]{1,0:T(8,128)(2,1)S(1)} %get-tuple-element.95.refs_0_, bf16[12576,2048]{1,0:T(8,128)(2,1)} %bitcast.194, s32[512,1]{1,0:T(8,128)S(1)} %and_select_fusion.refs_2_.refs_3_), custom_call_target="tpu_custom_call" | custom-call | flops 1 | bytes 1 | tf_op jit(solution)/shard_map/head/pallas_call | solution.py:679
  468.1 5.2 all-gather.8
  474.1 41.9 %head_pull.1 = bf16[512,2048]{1,0:T(8,128)(2,1)S(1)} custom-call(f32[512,12576]{1,0:T(8,128)} %get-tuple-element.98.refs_0_, bf16[12576,2048]{1,0:T(8,128)(2,1)} %bitcast.195, f32[512,2]{1,0:T(8,128)S(1)} %copy.237.refs_2_, s32[512,1]{1,0:T(8,128)S(1)} %and_select_fusion.refs_2_.refs_3_), custom_call_target="tpu_custom_call" | custom-call | flops 1 | bytes 1 | tf_op jit(solution)/shard_map/head_pull/pallas_call | solution.py:738
  531.9 14.8 %collective-permute-done.19 = bf16[256,2048]{1,0:T(8,128)(2,1)} collective-permute-done((bf16[256,2048]{1,0:T(8,128)(2,1)S(1)}, bf16[256,2048]{1,0:T(8,128)(2,1)}, u32[]{:S(2)}, u32[]{:S(2)}) %collective-permute-start.19) | collective-permute-done | bytes 1048608 | tf_op jit(solution)/shard_map/ppermute | solution.py:57
  549.7 3.3 collective-permute-done.17
  560.4 3.2 fusion.11
  564.2 4.5 fusion.61
  571.2 6.6 grad_blocks.8
  580.3 10.5 %pull_units.2 = bf16[512,2048]{1,0:T(8,128)(2,1)S(1)} custom-call(s32[1]{0:T(128)} %bitcast.16.low_ref, bf16[512,2048]{1,0:T(8,128)(2,1)S(1)} %get-tuple-element.104.refs_0_.x_ref, bf16[4,2048,256]{2,1,0:T(8,128)(2,1)} %bitcast.200, bf16[4,2048,256]{2,1,0:T(8,128)(2,1)} %collective-permute-done.11.refs_5_.refs_1_.refs_3_, f32[512,2048]{1,0:T(8,128)} %get-tuple-element.102.refs_2_), custom_call_target="tpu_custom_call" | custom-call | flops 1 | bytes 1 | tf_op jit(solution)/shard_map/pull_units/pallas_call | solution.py:417
  590.8 4.4 grad_blocks.9
  597.7 38.6 %collective-permute-done.21 = bf16[4,1,1,256,1280]{4,3,2,1,0:T(8,128)(2,1)S(1)} collective-permute-done((bf16[4,1,1,256,1280]{4,3,2,1,0:T(8,128)(2,1)}, bf16[4,1,1,256,1280]{4,3,2,1,0:T(8,128)(2,1)S(1)}, u32[]{:S(2)}, u32[]{:S(2)}) %collective-permute-start.21) | collective-permute-done | bytes 2621472 | tf_op jit(solution)/shard_map/ppermute | solution.py:47
  643.3 9.5 attend_back.1.refs_1_.x_ref
  654.4 5.8 grad_blocks.11
  660.2 10.2 %reduce-scatter.5.cloned.1.call-done = bf16[1,2,1,256,1280]{4,3,1,2,0:T(8,128)(2,1)} async-done(((bf16[4,2,1,256,1280]{4,3,1,2,0:T(8,128)(2,1)}), bf16[1,2,1,256,1280]{4,3,1,2,0:T(8,128)(2,1)}) %reduce-scatter.5.cloned.1.call-update) | async-done | bytes 1310736 | tf_op jit(solution)/shard_map/reduce_scatter | solution.py:70
  672.0 4.4 grad_blocks.12
  676.4 53.5 %collective-permute-done.22 = bf16[4,1,1,256,2048]{4,3,2,1,0:T(8,128)(2,1)} collective-permute-done((bf16[4,1,1,256,2048]{4,3,2,1,0:T(8,128)(2,1)}, bf16[4,1,1,256,2048]{4,3,2,1,0:T(8,128)(2,1)}, u32[]{:S(2)}, u32[]{:S(2)}) %collective-permute-start.22) | collective-permute-done | bytes 4194336 | tf_op jit(solution)/shard_map/ppermute | solution.py:47
  729.9 7.8 fusion.7
  739.3 12.6 %shard_terms.2 = f32[768,2048]{1,0:T(8,128)} custom-call(s32[1]{0:T(128)} %bitcast.16.low_ref, bf16[3,768,512]{2,1,0:T(8,128)(2,1)S(1)} %copy-done.5, bf16[4,3,256,512]{3,2,1,0:T(8,128)(2,1)} %bitcast.14.refs_0_, bf16[4,3,256,512]{3,2,1,0:T(8,128)(2,1)} %collective-permute-done.6.refs_1_), custom_call_target="tpu_custom_call" | custom-call | flops 1 | bytes 1 | tf_op jit(solution)/shard_map/shard_terms/pallas_call | solution.py:553
  751.9 11.8 %shard_terms.3 = f32[512,2048]{1,0:T(8,128)} custom-call(s32[1]{0:T(128)} %bitcast.16.low_ref, bf16[1,512,2048]{2,1,0:T(8,128)(2,1)S(1)} %bitcast.186, bf16[4,1,256,2048]{3,2,1,0:T(8,128)(2,1)} %bitcast.209, bf16[4,1,256,2048]{3,2,1,0:T(8,128)(2,1)} %bitcast.70.refs_1_), custom_call_target="tpu_custom_call" | custom-call | flops 1 | bytes 1 | tf_op jit(solution)/shard_map/shard_terms/pallas_call | solution.py:553
  763.7 4.7 fusion.8
  779.0 3.0 copy.250
  786.9 3.9 add_convert_fusion.9
  792.4 3.6 fusion.53
  801.1 4.6 grad_blocks.13
  805.8 38.2 %collective-permute-done.24 = bf16[4,1,3,256,512]{4,3,2,1,0:T(8,128)(2,1)} collective-permute-done((bf16[4,1,3,256,512]{4,3,2,1,0:T(8,128)(2,1)}, bf16[4,1,3,256,512]{4,3,2,1,0:T(8,128)(2,1)}, u32[]{:S(2)}, u32[]{:S(2)}) %collective-permute-start.24) | collective-permute-done | bytes 3145760 | tf_op jit(solution)/shard_map/ppermute | solution.py:47
  844.0 4.6 fusion.12
  851.8 10.2 %branch.3 = bf16[256,2048]{1,0:T(8,128)(2,1)S(1)} custom-call(s32[1]{0:T(128)} %bitcast.16.low_ref, bf16[768,2048]{1,0:T(8,128)(2,1)} %copy-done.2, bf16[768,512]{1,0:T(8,128)(2,1)S(1)} %copy-done.14, bf16[4,2048,256]{2,1,0:T(8,128)(2,1)} %bitcast.201, bf16[4,2048,256]{2,1,0:T(8,128)(2,1)} %collective-permute-done.11.refs_5_.refs_1_.refs_3_, ...), custom_call_target="tpu_custom_call" | custom-call | flops 1 | bytes 1 | tf_op jit(solution)/shard_map/branch/pallas_call | solution.py:511
  862.6 3.9 multiply_subtract_fusion
  870.4 5.4 multiply_subtract_fusion.1
  875.8 4.8 collective-permute-done.27
  881.7 7.4 multiply_reduce_fusion
  889.7 11.1 %fusion.5 = f32[768,2048]{1,0:T(8,128)S(1)} fusion(f32[512,2048]{1,0:T(8,128)S(1)} %copy-done.39, f32[768]{0:T(1024)S(1)} %broadcast_multiply_fusion.1, f32[768]{0:T(1024)S(1)} %broadcast_multiply_fusion.2, f32[768]{0:T(1024)S(1)} %copy-done.69, f32[768]{0:T(1024)S(1)} %copy-done.67, bf16[384,2048]{1,0:T(8,128)(2,1)S(1)} %add_convert_fusion.8, ...), kind=kLoop, calls=%fused_computation.14 | loop fusion | flops 33030144 | bytes 16789504 | tf_op jit(solution)/shard_map/add | solution.py:980
  905.9 4.1 all-to-all-start.2
  925.5 3.6 all-to-all-start.3
  931.8 3.0 collective-permute-start.37
  945.9 5.3 multiply_subtract_fusion.2
  (412 shorter events, 182.0 us)
Async XLA Ops:
  7.2 146.1 %copy-start = (bf16[512,2048]{1,0:T(8,128)(2,1)S(1)}, bf16[512,2048]{1,0:T(8,128)(2,1)}, u32[]{:S(2)}) copy-start(bf16[512,2048]{1,0:T(8,128)(2,1)} %param.60) | copy-start | bytes 6291460
  7.2 105.8 %all-gather.15.cloned.1.call-start = ((), (), s32[]{:S(2)}) async-start(), calls=%async_computation.12 | async-start | bytes 3932160 | tf_op jit(solution)/shard_map/all_gather | solution.py:66
  7.9 170.4 %all-gather.17.cloned.1.call-start = ((), (), s32[]{:S(2)}) async-start(), calls=%async_computation.13 | async-start | bytes 5242880 | tf_op jit(solution)/shard_map/all_gather | solution.py:66
  12.9 36.0 %all-to-all-start = ((bf16[8,2,8,2048]{3,2,1,0:T(8,128)(2,1)}), bf16[8,2,8,2048]{3,2,1,0:T(8,128)(2,1)S(1)}, u32[]{:S(2)}, u32[]{:S(2)}) async-start(bf16[8,2,8,2048]{3,2,1,0:T(8,128)(2,1)} %copy_bitcast_fusion.1), calls=%async_computation | async-start | bytes 1048576 | tf_op jit(solution)/shard_map/all_to_all | solution.py:615
  50.3 32.9 %all-to-all-start.1 = ((bf16[8,2,8,2048]{3,2,1,0:T(8,128)(2,1)}), bf16[8,2,8,2048]{3,2,1,0:T(8,128)(2,1)S(1)}, u32[]{:S(2)}, u32[]{:S(2)}) async-start(bf16[8,2,8,2048]{3,2,1,0:T(8,128)(2,1)} %broadcast_select_fusion), calls=%async_computation.1 | async-start | bytes 1048576 | tf_op jit(solution)/shard_map/all_to_all | solution.py:616
  53.9 205.4 %all-gather.19.cloned.1.call-start = ((), (), s32[]{:S(2)}) async-start(), calls=%async_computation.14 | async-start | bytes 5242880 | tf_op jit(solution)/shard_map/all_gather | solution.py:66
  53.9 44.8 %collective-permute-start.2 = (bf16[1,4,256]{2,1,0:T(4,128)(2,1)}, bf16[1,4,256]{2,1,0:T(4,128)(2,1)}, u32[]{:S(2)}, u32[]{:S(2)}) collective-permute-start(bf16[1,4,256]{2,1,0:T(4,128)(2,1)} %bitcast.22), channel_id=1, source_target_pairs={{0,4},{4,0},{8,12},{12,8},{16,20},{20,16},{24,28},{28,24},{1,5},{5... | collective-permute-start | bytes 6152 | tf_op jit(solution)/shard_map/ppermute | solution.py:100
  55.9 51.9 %collective-permute-start.5 = (bf16[512,256]{1,0:T(8,128)(2,1)}, bf16[512,256]{1,0:T(8,128)(2,1)}, u32[]{:S(2)}, u32[]{:S(2)}) collective-permute-start(bf16[512,256]{1,0:T(8,128)(2,1)} %param.40), channel_id=1, source_target_pairs={{0,4},{4,0},{8,12},{12,8},{16,20},{20,16},{24,28},{28,24},{1,5},{5... | collective-permute-start | bytes 786440 | tf_op jit(solution)/shard_map/ppermute | solution.py:47
  56.1 319.4 %all-gather.21.cloned.1.call-start = ((), (), s32[]{:S(2)}) async-start(), calls=%async_computation.15 | async-start | bytes 1310720 | tf_op jit(solution)/shard_map/all_gather | solution.py:66
  83.2 15.4 %copy-start.47 = (bf16[2,64,2048]{2,1,0:T(8,128)(2,1)}, bf16[2,64,2048]{2,1,0:T(8,128)(2,1)S(1)}, u32[]{:S(2)}) copy-start(bf16[2,64,2048]{2,1,0:T(8,128)(2,1)S(1)} %copy_bitcast_fusion) | copy-start | bytes 1572868
  83.2 13.0 %collective-permute-start = (bf16[2,64,2048]{2,1,0:T(8,128)(2,1)S(1)}, bf16[2,64,2048]{2,1,0:T(8,128)(2,1)S(1)}, u32[]{:S(2)}, u32[]{:S(2)}) collective-permute-start(bf16[2,64,2048]{2,1,0:T(8,128)(2,1)S(1)} %copy_bitcast_fusion), channel_id=1, source_target_pairs={{0,2},{1,3},{2,0},{3,1},{4,6},{5,7},{6,4},{7,5},{8,10},{9,11},{10,... | collective-permute-start | bytes 1572872 | tf_op jit(solution)/shard_map/ppermute | solution.py:57
  97.4 12.1 %collective-permute-start.1 = (bf16[2,2,64,2048]{3,2,1,0:T(8,128)(2,1)}, bf16[2,2,64,2048]{3,2,1,0:T(8,128)(2,1)}, u32[]{:S(2)}, u32[]{:S(2)}) collective-permute-start(bf16[2,2,64,2048]{3,2,1,0:T(8,128)(2,1)} %maximum_select_fusion.5), channel_id=1, source_target_pairs={{0,1},{1,0},{2,3},{3,2},{4,5},{5,4},{6,7},{7,6},{8,9},{9,8},{10,11... | collective-permute-start | bytes 3145736 | tf_op jit(solution)/shard_map/ppermute | solution.py:57
  99.5 3.7 collective-permute-start.3
  103.2 4.6 collective-permute-start.4
  116.4 68.7 %collective-permute-start.6 = (bf16[4,3,256,512]{3,2,1,0:T(8,128)(2,1)}, bf16[4,3,256,512]{3,2,1,0:T(8,128)(2,1)}, u32[]{:S(2)}, u32[]{:S(2)}) collective-permute-start(bf16[4,3,256,512]{3,2,1,0:T(8,128)(2,1)} %bitcast.14.refs_0_), channel_id=1, source_target_pairs={{0,4},{4,0},{8,12},{12,8},{16,20},{20,16},{24,28},{28,24},{1,5},{5... | collective-permute-start | bytes 9437192 | tf_op jit(solution)/shard_map/ppermute | solution.py:47
  156.0 33.5 %copy-start.29 = (bf16[512,2048]{1,0:T(8,128)(2,1)S(1)}, bf16[512,2048]{1,0:T(8,128)(2,1)}, u32[]{:S(2)}) copy-start(bf16[512,2048]{1,0:T(8,128)(2,1)} %param.32) | copy-start | bytes 6291460
  185.2 90.7 %collective-permute-start.10 = (bf16[4,256,2048]{2,1,0:T(8,128)(2,1)}, bf16[4,256,2048]{2,1,0:T(8,128)(2,1)}, u32[]{:S(2)}, u32[]{:S(2)}) collective-permute-start(bf16[4,256,2048]{2,1,0:T(8,128)(2,1)} %bitcast.207), channel_id=1, source_target_pairs={{0,4},{4,0},{8,12},{12,8},{16,20},{20,16},{24,28},{28,24},{1,5},{5... | collective-permute-start | bytes 12582920 | tf_op jit(solution)/shard_map/ppermute | solution.py:47
  200.0 77.5 %collective-permute-start.7 = (bf16[256,2048]{1,0:T(8,128)(2,1)}, bf16[256,2048]{1,0:T(8,128)(2,1)}, u32[]{:S(2)}, u32[]{:S(2)}) collective-permute-start(bf16[256,2048]{1,0:T(8,128)(2,1)} %constant_dynamic-slice_fusion.7), channel_id=1, source_target_pairs={{0,1},{1,0},{2,3},{3,2},{4,5},{5,4},{6,7},{7,6},{8,9},{9,8},{10,11... | collective-permute-start | bytes 3145736 | tf_op jit(solution)/shard_map/ppermute | solution.py:57
  226.3 55.7 %copy-start.23 = (bf16[768,512]{1,0:T(8,128)(2,1)}, bf16[768,512]{1,0:T(8,128)(2,1)S(1)}, u32[]{:S(2)}) copy-start(bf16[768,512]{1,0:T(8,128)(2,1)S(1)} %get-tuple-element.105.refs_1_) | copy-start | bytes 2359300
  226.3 291.7 %copy-start.13 = (bf16[768,512]{1,0:T(8,128)(2,1)}, bf16[768,512]{1,0:T(8,128)(2,1)S(1)}, u32[]{:S(2)}) copy-start(bf16[768,512]{1,0:T(8,128)(2,1)S(1)} %get-tuple-element.92.refs_1_.refs_3_) | copy-start | bytes 2359300
  275.9 99.5 %collective-permute-start.11 = (bf16[4,2048,256]{2,1,0:T(8,128)(2,1)}, bf16[4,2048,256]{2,1,0:T(8,128)(2,1)}, u32[]{:S(2)}, u32[]{:S(2)}) collective-permute-start(bf16[4,2048,256]{2,1,0:T(8,128)(2,1)} %bitcast.198), channel_id=1, source_target_pairs={{0,4},{4,0},{8,12},{12,8},{16,20},{20,16},{24,28},{28,24},{1,5},{5... | collective-permute-start | bytes 12582920 | tf_op jit(solution)/shard_map/ppermute | solution.py:47
  277.5 97.9 %all-gather.23.cloned.1.call-start = ((), (), s32[]{:S(2)}) async-start(), calls=%async_computation.16 | async-start | bytes 1310720 | tf_op jit(solution)/shard_map/all_gather | solution.py:66
  277.5 26.0 %copy-start.84 = (s32[8]{0:T(128)S(1)}, s32[8]{0:T(128)}, u32[]{:S(2)}) copy-start(s32[8]{0:T(128)} %param.37) | copy-start | bytes 100
  280.5 21.0 %collective-permute-start.8 = (bf16[256,2048]{1,0:T(8,128)(2,1)}, bf16[256,2048]{1,0:T(8,128)(2,1)}, u32[]{:S(2)}, u32[]{:S(2)}) collective-permute-start(bf16[256,2048]{1,0:T(8,128)(2,1)} %add_convert_fusion.15), channel_id=1, source_target_pairs={{0,2},{1,3},{2,0},{3,1},{4,6},{5,7},{6,4},{7,5},{8,10},{9,11},{10,... | collective-permute-start | bytes 3145736 | tf_op jit(solution)/shard_map/ppermute | solution.py:57
  282.0 388.4 %reduce-scatter.5.cloned.1.call-start = ((), (), s32[]{:S(2)}) async-start(), calls=%async_computation.8 | async-start | bytes 6553600 | tf_op jit(solution)/shard_map/reduce_scatter | solution.py:70
  303.4 6.7 collective-permute-start.9
  389.3 29.1 %copy-start.81 = (s32[8]{0:T(128)S(1)}, s32[8]{0:T(128)}, u32[]{:S(2)}) copy-start(s32[8]{0:T(128)} %param.36) | copy-start | bytes 100
  389.3 2.7 collective-permute-start.12
  392.4 25.5 %collective-permute-start.13 = (bf16[256,2048]{1,0:T(8,128)(2,1)S(1)}, bf16[256,2048]{1,0:T(8,128)(2,1)S(1)}, u32[]{:S(2)}, u32[]{:S(2)}) collective-permute-start(bf16[256,2048]{1,0:T(8,128)(2,1)S(1)} %add_convert_fusion.13), channel_id=1, source_target_pairs={{0,2},{1,3},{2,0},{3,1},{4,6},{5,7},{6,4},{7,5},{8,10},{9,11},{10,... | collective-permute-start | bytes 3145736 | tf_op jit(solution)/shard_map/ppermute | solution.py:57
  418.3 5.1 collective-permute-start.14
  474.1 43.7 %copy-start.3 = (bf16[768,2048]{1,0:T(8,128)(2,1)S(1)}, bf16[768,2048]{1,0:T(8,128)(2,1)}, u32[]{:S(2)}) copy-start(bf16[768,2048]{1,0:T(8,128)(2,1)} %copy-done.2) | copy-start | bytes 9437188
  516.1 4.8 collective-permute-start.18
  521.3 25.4 %collective-permute-start.19 = (bf16[256,2048]{1,0:T(8,128)(2,1)S(1)}, bf16[256,2048]{1,0:T(8,128)(2,1)}, u32[]{:S(2)}, u32[]{:S(2)}) collective-permute-start(bf16[256,2048]{1,0:T(8,128)(2,1)S(1)} %add_convert_fusion.11), channel_id=1, source_target_pairs={{0,2},{1,3},{2,0},{3,1},{4,6},{5,7},{6,4},{7,5},{8,10},{9,11},{10,... | collective-permute-start | bytes 3145736 | tf_op jit(solution)/shard_map/ppermute | solution.py:57
  526.9 3.5 collective-permute-start.15
  530.4 18.0 %collective-permute-start.16 = (f32[2,2]{1,0:T(2,128)S(1)}, f32[2,2]{1,0:T(2,128)S(1)}, u32[]{:S(2)}, u32[]{:S(2)}) collective-permute-start(f32[2,2]{1,0:T(2,128)S(1)} %maximum_select_fusion.13), channel_id=1, source_target_pairs={{0,8},{4,12},{8,0},{12,4},{16,24},{20,28},{24,16},{28,20},{1,9},{5... | collective-permute-start | bytes 56 | tf_op jit(solution)/shard_map/ppermute | solution.py:100
  548.3 15.3 %copy-start.42 = (bf16[256,2048]{1,0:T(8,128)(2,1)}, bf16[256,2048]{1,0:T(8,128)(2,1)S(1)}, u32[]{:S(2)}) copy-start(bf16[256,2048]{1,0:T(8,128)(2,1)S(1)} %add_convert_fusion.10) | copy-start | bytes 3145732
  548.3 12.0 %collective-permute-start.20 = (bf16[256,2048]{1,0:T(8,128)(2,1)S(1)}, bf16[256,2048]{1,0:T(8,128)(2,1)S(1)}, u32[]{:S(2)}, u32[]{:S(2)}) collective-permute-start(bf16[256,2048]{1,0:T(8,128)(2,1)S(1)} %add_convert_fusion.10), channel_id=1, source_target_pairs={{0,1},{1,0},{2,3},{3,2},{4,5},{5,4},{6,7},{7,6},{8,9},{9,8},{10,11... | collective-permute-start | bytes 3145736 | tf_op jit(solution)/shard_map/ppermute | solution.py:57
  548.4 4.5 collective-permute-start.17
  577.8 219.2 %reduce-scatter.11.cloned.1.call-start = ((), (), s32[]{:S(2)}) async-start(), calls=%async_computation.11 | async-start | bytes 3276800 | tf_op jit(solution)/shard_map/reduce_scatter | solution.py:70
  577.8 58.4 %collective-permute-start.21 = (bf16[4,1,1,256,1280]{4,3,2,1,0:T(8,128)(2,1)}, bf16[4,1,1,256,1280]{4,3,2,1,0:T(8,128)(2,1)S(1)}, u32[]{:S(2)}, u32[]{:S(2)}) collective-permute-start(bf16[4,1,1,256,1280]{4,3,2,1,0:T(8,128)(2,1)} %copy-done.22), channel_id=1, source_target_pairs={{0,4},{4,0},{8,12},{12,8},{16,20},{20,16},{24,28},{28,24},{1,5},{5... | collective-permute-start | bytes 7864328 | tf_op jit(solution)/shard_map/ppermute | solution.py:47
  638.4 210.2 %reduce-scatter.7.cloned.1.call-start = ((), (), s32[]{:S(2)}) async-start(), calls=%async_computation.9 | async-start | bytes 5242880 | tf_op jit(solution)/shard_map/reduce_scatter | solution.py:70
  638.5 91.4 %collective-permute-start.22 = (bf16[4,1,1,256,2048]{4,3,2,1,0:T(8,128)(2,1)}, bf16[4,1,1,256,2048]{4,3,2,1,0:T(8,128)(2,1)}, u32[]{:S(2)}, u32[]{:S(2)}) collective-permute-start(bf16[4,1,1,256,2048]{4,3,2,1,0:T(8,128)(2,1)} %grad_blocks.9), channel_id=1, source_target_pairs={{0,4},{4,0},{8,12},{12,8},{16,20},{20,16},{24,28},{28,24},{1,5},{5... | collective-permute-start | bytes 12582920 | tf_op jit(solution)/shard_map/ppermute | solution.py:47
  654.4 16.0 %copy-start.7 = (bf16[512,2048]{1,0:T(8,128)(2,1)S(1)}, bf16[512,2048]{1,0:T(8,128)(2,1)}, u32[]{:S(2)}) copy-start(bf16[512,2048]{1,0:T(8,128)(2,1)} %copy-done.6) | copy-start | bytes 6291460
  737.7 200.0 %reduce-scatter.9.cloned.1.call-start = ((), (), s32[]{:S(2)}) async-start(), calls=%async_computation.10 | async-start | bytes 3932160 | tf_op jit(solution)/shard_map/reduce_scatter | solution.py:70
  739.3 12.6 %copy-start.8 = (bf16[512,2048]{1,0:T(8,128)(2,1)S(1)}, bf16[512,2048]{1,0:T(8,128)(2,1)}, u32[]{:S(2)}) copy-start(bf16[512,2048]{1,0:T(8,128)(2,1)} %copy-done.6) | copy-start | bytes 6291460
  773.2 13.8 %collective-permute-start.23 = (bf16[384,2048]{1,0:T(8,128)(2,1)}, bf16[384,2048]{1,0:T(8,128)(2,1)}, u32[]{:S(2)}, u32[]{:S(2)}) collective-permute-start(bf16[384,2048]{1,0:T(8,128)(2,1)} %constant_dynamic-slice_fusion.2), channel_id=1, source_target_pairs={{0,1},{1,0},{2,3},{3,2},{4,5},{5,4},{6,7},{7,6},{8,9},{9,8},{10,11... | collective-permute-start | bytes 4718600 | tf_op jit(solution)/shard_map/ppermute | solution.py:57
  773.2 70.8 %collective-permute-start.24 = (bf16[4,1,3,256,512]{4,3,2,1,0:T(8,128)(2,1)}, bf16[4,1,3,256,512]{4,3,2,1,0:T(8,128)(2,1)}, u32[]{:S(2)}, u32[]{:S(2)}) collective-permute-start(bf16[4,1,3,256,512]{4,3,2,1,0:T(8,128)(2,1)} %grad_blocks.11), channel_id=1, source_target_pairs={{0,4},{4,0},{8,12},{12,8},{16,20},{20,16},{24,28},{28,24},{1,5},{5... | collective-permute-start | bytes 9437192 | tf_op jit(solution)/shard_map/ppermute | solution.py:47
  790.8 57.8 %collective-permute-start.25 = (bf16[384,2048]{1,0:T(8,128)(2,1)}, bf16[384,2048]{1,0:T(8,128)(2,1)}, u32[]{:S(2)}, u32[]{:S(2)}) collective-permute-start(bf16[384,2048]{1,0:T(8,128)(2,1)} %add_convert_fusion.9), channel_id=1, source_target_pairs={{0,2},{1,3},{2,0},{3,1},{4,6},{5,7},{6,4},{7,5},{8,10},{9,11},{10,... | collective-permute-start | bytes 4718600 | tf_op jit(solution)/shard_map/ppermute | solution.py:57
  851.3 11.3 %copy-start.55 = (f32[256,2048]{1,0:T(8,128)S(1)}, f32[256,2048]{1,0:T(8,128)}, u32[]{:S(2)}) copy-start(f32[256,2048]{1,0:T(8,128)} %param.46) | copy-start | bytes 6291460
  851.4 30.2 %collective-permute-start.29 = (bf16[384,2048]{1,0:T(8,128)(2,1)S(1)}, bf16[384,2048]{1,0:T(8,128)(2,1)}, u32[]{:S(2)}, u32[]{:S(2)}) collective-permute-start(bf16[384,2048]{1,0:T(8,128)(2,1)S(1)} %add_convert_fusion.8), channel_id=1, source_target_pairs={{0,1},{1,0},{2,3},{3,2},{4,5},{5,4},{6,7},{7,6},{8,9},{9,8},{10,11... | collective-permute-start | bytes 4718600 | tf_op jit(solution)/shard_map/ppermute | solution.py:57
  851.4 17.5 %collective-permute-start.32 = (bf16[256,1280]{1,0:T(8,128)(2,1)}, bf16[256,1280]{1,0:T(8,128)(2,1)}, u32[]{:S(2)}, u32[]{:S(2)}) collective-permute-start(bf16[256,1280]{1,0:T(8,128)(2,1)} %slice_bitcast_fusion.3), channel_id=1, source_target_pairs={{0,4},{4,0},{8,12},{12,8},{16,20},{20,16},{24,28},{28,24},{1,5},{5... | collective-permute-start | bytes 1966088 | tf_op jit(solution)/shard_map/ppermute | solution.py:47
  862.1 4.4 collective-permute-start.26
  866.7 14.0 %collective-permute-start.27 = (bf16[128,2048]{1,0:T(8,128)(2,1)S(1)}, bf16[128,2048]{1,0:T(8,128)(2,1)S(1)}, u32[]{:S(2)}, u32[]{:S(2)}) collective-permute-start(bf16[128,2048]{1,0:T(8,128)(2,1)S(1)} %add_convert_fusion.17), channel_id=1, source_target_pairs={{0,2},{1,3},{2,0},{3,1},{4,6},{5,7},{6,4},{7,5},{8,10},{9,11},{10,... | collective-permute-start | bytes 1572872 | tf_op jit(solution)/shard_map/ppermute | solution.py:57
  868.9 12.7 %slice-start = ((s8[6291456]{0:T(1024)(128)(4,1)}), s8[4194304]{0:T(1024)(128)(4,1)S(1)}, s32[]{:S(2)}) async-start(s8[6291456]{0:T(1024)(128)(4,1)} %bitcast.196), calls=%async_computation.17 | async-start | bytes 8388608
  881.6 47.5 %collective-permute-start.28 = (bf16[128,2048]{1,0:T(8,128)(2,1)}, bf16[128,2048]{1,0:T(8,128)(2,1)}, u32[]{:S(2)}, u32[]{:S(2)}) collective-permute-start(bf16[128,2048]{1,0:T(8,128)(2,1)} %add_convert_fusion.16), channel_id=1, source_target_pairs={{0,1},{1,0},{2,3},{3,2},{4,5},{5,4},{6,7},{7,6},{8,9},{9,8},{10,11... | collective-permute-start | bytes 1572872 | tf_op jit(solution)/shard_map/ppermute | solution.py:57
  889.1 14.4 %collective-permute-start.33 = (f32[4,2048]{1,0:T(4,128)S(1)}, f32[4,2048]{1,0:T(4,128)S(1)}, u32[]{:S(2)}, u32[]{:S(2)}) collective-permute-start(f32[4,2048]{1,0:T(4,128)S(1)} %pad_maximum_fusion.9), channel_id=1, source_target_pairs={{0,1},{1,0},{2,3},{3,2},{4,5},{5,4},{6,7},{7,6},{8,9},{9,8},{10,11... | collective-permute-start | bytes 98312 | tf_op jit(solution)/shard_map/ppermute | solution.py:128
  903.6 6.3 collective-permute-start.34
  905.9 18.2 %all-to-all-start.2 = ((bf16[8,1,8,2048]{3,2,1,0:T(8,128)(2,1)}), bf16[8,1,8,2048]{3,2,1,0:T(8,128)(2,1)S(1)}, u32[]{:S(2)}, u32[]{:S(2)}) async-start(bf16[8,1,8,2048]{3,2,1,0:T(8,128)(2,1)} %fusion.26), calls=%async_computation.4 | async-start | bytes 524288 | tf_op jit(solution)/shard_map/all_to_all | solution.py:615
  910.0 12.6 %collective-permute-start.35 = (f32[4,2048]{1,0:T(4,128)S(1)}, f32[4,2048]{1,0:T(4,128)S(1)}, u32[]{:S(2)}, u32[]{:S(2)}) collective-permute-start(f32[4,2048]{1,0:T(4,128)S(1)} %fusion.76), channel_id=1, source_target_pairs={{0,4},{4,0},{8,12},{12,8},{16,20},{20,16},{24,28},{28,24},{1,5},{5... | collective-permute-start | bytes 98312 | tf_op jit(solution)/shard_map/ppermute | solution.py:128
  922.6 9.2 collective-permute-start.36
  925.5 12.2 %all-to-all-start.3 = ((bf16[8,1,8,2048]{3,2,1,0:T(8,128)(2,1)}), bf16[8,1,8,2048]{3,2,1,0:T(8,128)(2,1)S(1)}, u32[]{:S(2)}, u32[]{:S(2)}) async-start(bf16[8,1,8,2048]{3,2,1,0:T(8,128)(2,1)} %fusion.27), calls=%async_computation.5 | async-start | bytes 524288 | tf_op jit(solution)/shard_map/all_to_all | solution.py:616
  931.8 9.3 collective-permute-start.37
  937.7 6.8 collective-permute-start.30
  945.8 6.5 collective-permute-start.31
  (76 other events, 377.7 us)
Sparse Core Ops, SparseCore 0:
  9.6 87.2 all-gather.14
  98.5 79.7 all-gather.16
  179.9 79.2 all-gather.18
  277.6 26.4 all-gather.20
  305.5 27.4 all-gather.22
  577.9 92.4 reduce-scatter.4
  672.7 52.6 reduce-scatter.10
  737.8 75.4 reduce-scatter.6
  848.7 58.8 reduce-scatter.8

commit v3 on v2

--- a/solution.py
+++ b/solution.py
@@ -143,13 +143,15 @@
     return (kept.astype(F32) + tensor_swap(kept, 2).astype(F32)).astype(BF)
 
 
-def tensor_halves(part):
+def tensor_halves(part, *beside):
     part = part.astype(BF)
     if lax.axis_size("tensor") != 4:
         whole = lax.psum(part, "tensor")
         half = part.shape[0] // 2
         return whole[:half], whole[half:], jnp.zeros((1,), jnp.int32)
     kept = tensor_far(tensor_near(part))
+    if beside:
+        kept = after(kept, *beside)
     return kept, tensor_swap(kept, 1), (lax.axis_index("tensor") % 2).reshape(1)
 
 
@@ -605,6 +607,43 @@
     )(x, mine, other, low)
 
 
+def pull_body(mine_ref, other_ref, low_ref, weight_ref, unit_ref, scale_ref, out_ref, low_out_ref):
+    mine = pl.program_id(0) == low_ref[0]
+    upstream = jnp.where(mine, mine_ref[...].astype(F32), other_ref[...].astype(F32))
+    out = normalize_back(upstream * weight_ref[...], unit_ref[...], scale_ref[...])
+    out_ref[...] = out
+    low_out_ref[...] = out.astype(BF)
+
+
+def pull_rows(halves, weight, unit, scale):
+    mine, other, low = halves
+    rows, width = unit.shape
+    block = 128
+    steps = rows // 2 // block
+    whole = lambda columns: pl.BlockSpec((block, columns), lambda h, i: (h * steps + i, 0))
+    part = pl.BlockSpec((block, width), lambda h, i: (i, 0))
+    return pl.pallas_call(
+        pull_body,
+        grid=(2, steps),
+        in_specs=[
+            part,
+            part,
+            pl.BlockSpec(memory_space=pltpu.SMEM),
+            whole(1),
+            whole(width),
+            whole(1),
+        ],
+        out_specs=[whole(width), whole(width)],
+        out_shape=[
+            jax.ShapeDtypeStruct((rows, width), F32),
+            jax.ShapeDtypeStruct((rows, width), BF),
+        ],
+        compiler_params=pltpu.CompilerParams(vmem_limit_bytes=48 * 2**20),
+        cost_estimate=LIGHT,
+        name="pull_rows",
+    )(mine, other, low, weight, unit, scale)
+
+
 def borrow_rows(tail, order, first=(), last=()):
     groups = lax.axis_size("dp")
     parts = lax.axis_size("tensor")
@@ -622,6 +661,7 @@
 
 TILE = 1280
 CHUNK = 256
+PULL_CHUNK = 640
 
 
 def head_body(vocab, x_ref, w_ref, t_ref, *refs):
@@ -702,9 +742,9 @@
         total_ref[...] = jnp.zeros(total_ref.shape, F32)
 
     def add(masked):
-        for c in range(0, TILE, CHUNK):
-            at = slice(c, c + CHUNK)
-            column = lax.broadcasted_iota(jnp.int32, (x_ref.shape[0], CHUNK), 1)
+        for c in range(0, TILE, PULL_CHUNK):
+            at = slice(c, c + PULL_CHUNK)
+            column = lax.broadcasted_iota(jnp.int32, (x_ref.shape[0], PULL_CHUNK), 1)
             column = column + (step * TILE + c)
             pull = jnp.where(column == t_ref[...], 1.0, 0.0) - jnp.exp(
                 x_ref[:, at] - row_ref[:, 0:1]
@@ -899,7 +939,6 @@
     row = jnp.stack([peak, 1.0 / total], axis=1)
     every = gather_small(gaps)
     back_part = head_pull(logits, table, row, targets)
-    back_sum = tensor_sum(back_part)
     drift = jnp.sum(every[:, 1]) / groups
     sign = (2 * desirable - 1).astype(F32)
     settled = jax.nn.sigmoid(KTO_BETA * sign * (every[:, 0] - jax.nn.softplus(drift)))
@@ -910,9 +949,8 @@
         [-slope[own_index] * own_live / own_total, pull * other_live / other_total]
     )
 
-    back_unit = row_weight[:, None] * back_sum.astype(F32)
-    back_out = normalize_back(back_unit, unit_out, inverse_out)
-    branch_low = back_out.astype(BF)
+    back_sum = tensor_halves(back_part, row_weight)
+    back_out, branch_low = pull_rows(back_sum, row_weight[:, None], unit_out, inverse_out)
 
     features_scored = jnp.concatenate([hidden[half:], attended[half:]], axis=1)
     near_features, far_features = features_scored[:, :cut][None], features_scored[:, cut:][None]
@@ -936,15 +974,6 @@
     back_attended = pull_units(branch_low, attend_out)
     back_three = attention_back(back_attended, query, keys, values, tables, half)
     attend_sent = grad_blocks(first_in, back_three, (1,))
-    second_scored, far_back = lax.optimization_barrier((second_in[half:], far_back, attend_sent))[:2]
-    expand_kept = grad_blocks(second_scored, back_expand[None], (0,))
-    expand_ring = to_ring(expand_kept, expand_came)
-    expand_back = scatter_ring(expand_ring)
-
-    attend_sent, back_expand, back_three, expand_ring = lax.optimization_barrier(
-        (attend_sent, back_expand, back_three, expand_ring)
-    )
-    attend_came = swap(attend_sent)
     sided = lambda sides: [x if x is None else x[:, None] for x in sides]
     back_second = shard_terms(back_expand[None], sided((expand_mine, expand_other)))
     back_first = shard_terms(back_three, (attend_mine, attend_other))
@@ -966,7 +995,18 @@
     )
     four = lax.axis_size("tensor") == 4
     back_h = tensor_near(back_h) if four else lax.psum(back_h.astype(BF), "tensor")
-    attend_kept = grad_blocks(after(first_in, back_h), back_three, (0,))
+    second_scored, far_back = lax.optimization_barrier(
+        (second_in[half:], far_back, attend_sent, back_h)
+    )[:2]
+    expand_kept = grad_blocks(second_scored, back_expand[None], (0,))
+    expand_ring = to_ring(expand_kept, expand_came)
+    expand_back = scatter_ring(expand_ring)
+
+    attend_sent, back_three, expand_ring = lax.optimization_barrier(
+        (attend_sent, back_three, expand_ring)
+    )
+    attend_came = swap(attend_sent)
+    attend_kept = grad_blocks(after(first_in, expand_ring), back_three, (0,))
     attend_ring = to_ring(attend_kept, attend_came)
     across = tensor_swap(back_h, 2) if four else back_h
     attend_ring, expand_back, across = lax.optimization_barrier((attend_ring, expand_back, across))

time: 974 us -> 933 us (0.958)
  waiting for transfers between devices: 363 us -> 326 us
  other arithmetic: 153 us -> 141 us
    ppermute x8, waiting for transfers between devices: 155 us -> 124 us  [pair_swap(): return lax.ppermute(value, 'dp', [(i, i ^ 1) for i in range(groups)])]
  transfers between devices with their start and end apart: 51 -> 51, of which waited for: 22 -> 21; matrix products, arithmetic and copies ran while one was open for 21% -> 21% of each run, Pallas kernels for 18% -> 18%
where the time goes in v3:
time: 933 us; the launch traced here: 921 us
  waiting for transfers between devices  326 us (35%)
  Pallas kernels  278 us (30%)
  other arithmetic  141 us (15%)
  local copies, waits for them, and re-layouts  79.3 us (8%)
  starting transfers between devices  52.3 us (6%)
  between operations  23.8 us (3%)
  blocking collectives  10.4 us (1%)
  matrix products  10.1 us (1%)
    ppermute x8, waiting for transfers between devices, pair_swap(): return lax.ppermute(value, 'dp', [(i, i ^ 1) for i in range(groups)])  124 us
    pallas_call x2, Pallas kernels, head_stats(): pl.pallas_call(lambda *refs: head_body(vocab, *refs), grid=(tiles,), in_s...  76.8 us
    ppermute x19, waiting for transfers between devices, tensor_swap(): lax.ppermute(value, 'tensor', [(i, i ^ bit) for i in range(lax.axis_size(...  72.4 us
    all_gather x5, waiting for transfers between devices, gather_ring(): return lax.all_gather(piece, 'dp', axis_index_groups=ring_groups())  55.2 us
    unnamed x192, local copies, waits for them, and re-layouts  50.4 us
    pallas_call x1, Pallas kernels, head_pull(): pl.pallas_call(lambda *refs: head_pull_body(vocab, tiles, *refs), grid=(t...  36.8 us
    all_to_all x2, waiting for transfers between devices, borrow_rows(): lax.all_to_all(jnp.take(spread, order, axis=0), 'dp', split_axis=0, conca...  29.9 us
    pallas_call x7, Pallas kernels, grad_blocks(): pl.pallas_call(lambda low_ref, *refs: grad_body(*refs), grid_spec=pltpu.P...  29.7 us
  transfers between devices with their start and end apart: 51, of which 21 were waited for; matrix products, arithmetic and copies ran while one was open for 21% of the time, Pallas kernels for 18%

profile of v3, /device:TPU:0, one launch (start us, length us, event | category | flops | bytes accessed | tf_op | source)
XLA Modules:
  0.0 920.9 jit_solution(6713044027214968995)
XLA Ops:
  8.7 3.3 fusion.63
  12.9 7.3 all-to-all-start
  20.7 28.1 %all-to-all-done = bf16[8,2,8,2048]{3,2,1,0:T(8,128)(2,1)S(1)} async-done(((bf16[8,2,8,2048]{3,2,1,0:T(8,128)(2,1)}), bf16[8,2,8,2048]{3,2,1,0:T(8,128)(2,1)S(1)}, u32[]{:S(2)}, u32[]{:S(2)}) %all-to-all-start) | async-done | bytes 524320 | tf_op jit(solution)/shard_map/all_to_all | solution.py:654
  50.3 3.6 all-to-all-start.1
  56.1 27.0 %all-to-all-done.1 = bf16[8,2,8,2048]{3,2,1,0:T(8,128)(2,1)S(1)} async-done(((bf16[8,2,8,2048]{3,2,1,0:T(8,128)(2,1)}), bf16[8,2,8,2048]{3,2,1,0:T(8,128)(2,1)S(1)}, u32[]{:S(2)}, u32[]{:S(2)}) %all-to-all-start.1) | async-done | bytes 524320 | tf_op jit(solution)/shard_map/all_to_all | solution.py:655
  88.9 7.3 collective-permute-done
  120.2 3.4 fusion
  124.2 13.0 %attend.2 = (bf16[512,512]{1,0:T(8,128)(2,1)S(1)}, bf16[512,512]{1,0:T(8,128)(2,1)}, bf16[768,512]{1,0:T(8,128)(2,1)}, bf16[768,512]{1,0:T(8,128)(2,1)}) custom-call(bf16[768,2048]{1,0:T(8,128)(2,1)} %get-tuple-element.77.refs_0_, bf16[3,2048,512]{2,1,0:T(8,128)(2,1)} %refs_1_.1, f32[3,768,128]{2,1,0:T(8,128)S(1)} %pad_maximum_fusion.8.refs_2_.refs_4_), custom_call_target="tpu_custom_call" | custom-call | flops 1 | bytes 1 | tf_op jit(solution)/shard_map/attend/pallas_call | solution.py:267
  137.2 8.9 hidden.2
  146.1 7.5 fusion.70
  156.3 22.1 %all-gather.17.cloned.1.call-done = bf16[1024,2048]{1,0:T(8,128)(2,1)} async-done(((bf16[256,2048]{1,0:T(8,128)(2,1)}), bf16[1024,2048]{1,0:T(8,128)(2,1)}) %all-gather.17.cloned.1.call-update) | async-done | bytes 4194320 | tf_op jit(solution)/shard_map/all_gather | solution.py:66
  178.3 6.8 collective-permute-done.6.refs_1_
  191.6 7.4 subtract_multiply_fusion
  200.1 5.4 maximum_select_fusion
  206.1 3.2 copy.234
  209.3 15.0 %attend.3 = (bf16[768,512]{1,0:T(8,128)(2,1)S(1)}, bf16[768,512]{1,0:T(8,128)(2,1)S(1)}, bf16[768,512]{1,0:T(8,128)(2,1)S(1)}, bf16[768,512]{1,0:T(8,128)(2,1)S(1)}) custom-call(bf16[768,2048]{1,0:T(8,128)(2,1)} %get-tuple-element.293.refs_0_, bf16[3,2048,512]{2,1,0:T(8,128)(2,1)} %bitcast.203, f32[3,768,128]{2,1,0:T(8,128)S(1)} %pad_maximum_fusion.8.refs_2_.refs_4_), custom_call_target="tpu_custom_call" | custom-call | flops 1 | bytes 1 | tf_op jit(solution)/shard_map/attend/pallas_call | solution.py:267
  226.1 33.1 %all-gather.19.cloned.1.call-done = bf16[8192,256]{1,0:T(8,128)(2,1)} async-done(((bf16[2048,256]{1,0:T(8,128)(2,1)}), bf16[8192,256]{1,0:T(8,128)(2,1)}) %all-gather.19.cloned.1.call-update) | async-done | bytes 4194320 | tf_op jit(solution)/shard_map/all_gather | solution.py:66
  259.3 16.6 %collective-permute-done.10.refs_1_ = bf16[4,256,2048]{2,1,0:T(8,128)(2,1)} collective-permute-done((bf16[4,256,2048]{2,1,0:T(8,128)(2,1)}, bf16[4,256,2048]{2,1,0:T(8,128)(2,1)}, u32[]{:S(2)}, u32[]{:S(2)}) %collective-permute-start.10) | collective-permute-done | bytes 4194336 | tf_op jit(solution)/shard_map/ppermute | solution.py:47
  281.1 19.2 %collective-permute-done.8 = bf16[256,2048]{1,0:T(8,128)(2,1)} collective-permute-done((bf16[256,2048]{1,0:T(8,128)(2,1)S(1)}, bf16[256,2048]{1,0:T(8,128)(2,1)}, u32[]{:S(2)}, u32[]{:S(2)}) %collective-permute-start.8) | collective-permute-done | bytes 1048608 | tf_op jit(solution)/shard_map/ppermute | solution.py:57
  305.6 3.1 pad_maximum_fusion.4.x_ref
  308.7 5.6 out_rows.2
  314.3 37.6 %head.2 = f32[8,512]{1,0:T(8,128)S(1)} custom-call(bf16[512,2048]{1,0:T(8,128)(2,1)S(1)} %get-tuple-element.89.refs_0_, bf16[12576,2048]{1,0:T(8,128)(2,1)} %bitcast.193, s32[512,1]{1,0:T(8,128)S(1)} %and_select_fusion.refs_2_.refs_3_), custom_call_target="tpu_custom_call" | custom-call | flops 1 | bytes 1 | tf_op jit(solution)/shard_map/head/pallas_call | solution.py:719
  351.9 5.2 all-gather.7
  357.2 13.3 %hidden.3 = (bf16[768,2048]{1,0:T(8,128)(2,1)S(1)}, f32[512,2048]{1,0:T(8,128)}) custom-call(s32[1]{0:T(128)} %bitcast.16.low_ref, bf16[768,2048]{1,0:T(8,128)(2,1)} %get-tuple-element.90.x_ref, bf16[4,256,2048]{2,1,0:T(8,128)(2,1)} %bitcast.210, bf16[4,256,2048]{2,1,0:T(8,128)(2,1)} %collective-permute-done.10.refs_1_), custom_call_target="tpu_custom_call" | custom-call | flops 1 | bytes 1 | tf_op jit(solution)/shard_map/hidden/pallas_call | solution.py:387
  374.6 11.3 %branch.2 = bf16[512,2048]{1,0:T(8,128)(2,1)S(1)} custom-call(s32[1]{0:T(128)} %bitcast.16.low_ref, bf16[768,2048]{1,0:T(8,128)(2,1)} %copy-done.2, bf16[768,512]{1,0:T(8,128)(2,1)S(1)} %get-tuple-element.93.refs_1_.refs_3_, bf16[768,2048]{1,0:T(8,128)(2,1)} %copy-done.2, bf16[768,512]{1,0:T(8,128)(2,1)S(1)} %get-tuple-element.93.refs_1_.refs_3_, ...), custom_call_target="tpu_custom_call" | custom-call | flops 1 | bytes 1 | tf_op jit(solution)/shard_map/branch/pallas_call | solution.py:513
  390.7 23.9 %collective-permute-done.13 = bf16[256,2048]{1,0:T(8,128)(2,1)S(1)} collective-permute-done((bf16[256,2048]{1,0:T(8,128)(2,1)S(1)}, bf16[256,2048]{1,0:T(8,128)(2,1)S(1)}, u32[]{:S(2)}, u32[]{:S(2)}) %collective-permute-start.13) | collective-permute-done | bytes 1048608 | tf_op jit(solution)/shard_map/ppermute | solution.py:57
  418.3 3.1 pad_maximum_fusion.5.x_ref
  421.4 5.1 out_rows.3
  426.6 39.2 %head.3 = (f32[512,12576]{1,0:T(8,128)}, f32[8,512]{1,0:T(8,128)S(1)}) custom-call(bf16[512,2048]{1,0:T(8,128)(2,1)S(1)} %get-tuple-element.95.refs_0_, bf16[12576,2048]{1,0:T(8,128)(2,1)} %bitcast.194, s32[512,1]{1,0:T(8,128)S(1)} %and_select_fusion.refs_2_.refs_3_), custom_call_target="tpu_custom_call" | custom-call | flops 1 | bytes 1 | tf_op jit(solution)/shard_map/head/pallas_call | solution.py:719
  465.7 5.2 all-gather.8
  471.2 36.8 %head_pull.1 = bf16[512,2048]{1,0:T(8,128)(2,1)S(1)} custom-call(f32[512,12576]{1,0:T(8,128)} %get-tuple-element.96.refs_0_, bf16[12576,2048]{1,0:T(8,128)(2,1)} %bitcast.195, f32[512,2]{1,0:T(8,128)S(1)} %copy.237.refs_2_, s32[512,1]{1,0:T(8,128)S(1)} %and_select_fusion.refs_2_.refs_3_), custom_call_target="tpu_custom_call" | custom-call | flops 1 | bytes 1 | tf_op jit(solution)/shard_map/head_pull/pallas_call | solution.py:778
  513.0 3.1 collective-permute-done.17
  522.2 3.3 collective-permute-done.19
  531.6 12.1 %collective-permute-done.16 = bf16[256,2048]{1,0:T(8,128)(2,1)} collective-permute-done((bf16[256,2048]{1,0:T(8,128)(2,1)}, bf16[256,2048]{1,0:T(8,128)(2,1)}, u32[]{:S(2)}, u32[]{:S(2)}) %collective-permute-start.16) | collective-permute-done | bytes 1048608 | tf_op jit(solution)/shard_map/ppermute | solution.py:57
  552.8 6.7 pull_rows.1
  562.0 6.7 grad_blocks.8
  570.9 10.5 %pull_units.2 = bf16[512,2048]{1,0:T(8,128)(2,1)S(1)} custom-call(s32[1]{0:T(128)} %bitcast.16.low_ref, bf16[512,2048]{1,0:T(8,128)(2,1)S(1)} %get-tuple-element.107.refs_0_.x_ref, bf16[4,2048,256]{2,1,0:T(8,128)(2,1)} %bitcast.200, bf16[4,2048,256]{2,1,0:T(8,128)(2,1)} %collective-permute-done.11.refs_5_.refs_1_.refs_3_, f32[512,2048]{1,0:T(8,128)} %get-tuple-element.105.refs_2_), custom_call_target="tpu_custom_call" | custom-call | flops 1 | bytes 1 | tf_op jit(solution)/shard_map/pull_units/pallas_call | solution.py:419
  581.5 4.4 grad_blocks.9
  588.4 38.9 %collective-permute-done.21 = bf16[4,1,1,256,1280]{4,3,2,1,0:T(8,128)(2,1)S(1)} collective-permute-done((bf16[4,1,1,256,1280]{4,3,2,1,0:T(8,128)(2,1)}, bf16[4,1,1,256,1280]{4,3,2,1,0:T(8,128)(2,1)S(1)}, u32[]{:S(2)}, u32[]{:S(2)}) %collective-permute-start.21) | collective-permute-done | bytes 2621472 | tf_op jit(solution)/shard_map/ppermute | solution.py:47
  634.3 9.4 %attend_back.1.refs_1_.x_ref = bf16[3,768,512]{2,1,0:T(8,128)(2,1)} custom-call(bf16[512,512]{1,0:T(8,128)(2,1)S(1)} %pull_units.3.refs_0_, bf16[768,512]{1,0:T(8,128)(2,1)S(1)} %copy-done.28, bf16[768,512]{1,0:T(8,128)(2,1)S(1)} %copy-done.30, bf16[768,512]{1,0:T(8,128)(2,1)S(1)} %copy-done.32, f32[3,768,128]{2,1,0:T(8,128)S(1)} %copy-done.10), custom_call_target="tpu_custom_call" | custom-call | flops 1 | bytes 1 | tf_op jit(solution)/shard_map/attend_back/pallas_call | solution.py:321
  645.4 11.8 %shard_terms.2 = f32[768,2048]{1,0:T(8,128)} custom-call(s32[1]{0:T(128)} %bitcast.16.low_ref, bf16[3,768,512]{2,1,0:T(8,128)(2,1)S(1)} %copy-done.4, bf16[4,3,256,512]{3,2,1,0:T(8,128)(2,1)} %bitcast.14.refs_0_, bf16[4,3,256,512]{3,2,1,0:T(8,128)(2,1)} %collective-permute-done.6.refs_1_), custom_call_target="tpu_custom_call" | custom-call | flops 1 | bytes 1 | tf_op jit(solution)/shard_map/shard_terms/pallas_call | solution.py:555
  657.2 11.8 %shard_terms.3 = f32[512,2048]{1,0:T(8,128)} custom-call(s32[1]{0:T(128)} %bitcast.16.low_ref, bf16[1,512,2048]{2,1,0:T(8,128)(2,1)S(1)} %bitcast.185, bf16[4,1,256,2048]{3,2,1,0:T(8,128)(2,1)} %bitcast.211, bf16[4,1,256,2048]{3,2,1,0:T(8,128)(2,1)} %bitcast.69.refs_1_), custom_call_target="tpu_custom_call" | custom-call | flops 1 | bytes 1 | tf_op jit(solution)/shard_map/shard_terms/pallas_call | solution.py:555
  669.0 3.8 fusion.8
  678.8 4.6 grad_blocks.11
  685.2 3.2 add_convert_fusion.9
  691.5 4.5 grad_blocks.12
  696.1 25.1 %collective-permute-done.23 = bf16[4,1,1,256,2048]{4,3,2,1,0:T(8,128)(2,1)} collective-permute-done((bf16[4,1,1,256,2048]{4,3,2,1,0:T(8,128)(2,1)}, bf16[4,1,1,256,2048]{4,3,2,1,0:T(8,128)(2,1)}, u32[]{:S(2)}, u32[]{:S(2)}) %collective-permute-start.23) | collective-permute-done | bytes 4194336 | tf_op jit(solution)/shard_map/ppermute | solution.py:47
  721.1 7.8 fusion.7
  732.2 3.1 copy.254
  746.6 5.1 fusion.53
  755.0 4.6 grad_blocks.13
  760.4 36.7 %collective-permute-done.24 = bf16[4,1,3,256,512]{4,3,2,1,0:T(8,128)(2,1)} collective-permute-done((bf16[4,1,3,256,512]{4,3,2,1,0:T(8,128)(2,1)}, bf16[4,1,3,256,512]{4,3,2,1,0:T(8,128)(2,1)}, u32[]{:S(2)}, u32[]{:S(2)}) %collective-permute-start.24) | collective-permute-done | bytes 3145760 | tf_op jit(solution)/shard_map/ppermute | solution.py:47
  797.2 4.5 fusion.11
  808.3 9.8 %branch.3 = bf16[256,2048]{1,0:T(8,128)(2,1)S(1)} custom-call(s32[1]{0:T(128)} %bitcast.16.low_ref, bf16[768,2048]{1,0:T(8,128)(2,1)} %copy-done.2, bf16[768,512]{1,0:T(8,128)(2,1)S(1)} %copy-done.16, bf16[4,2048,256]{2,1,0:T(8,128)(2,1)} %bitcast.201, bf16[4,2048,256]{2,1,0:T(8,128)(2,1)} %collective-permute-done.11.refs_5_.refs_1_.refs_3_, ...), custom_call_target="tpu_custom_call" | custom-call | flops 1 | bytes 1 | tf_op jit(solution)/shard_map/branch/pallas_call | solution.py:513
  818.4 5.3 multiply_subtract_fusion
  827.0 3.6 multiply_subtract_fusion.1
  830.6 7.5 collective-permute-done.27
  839.1 7.6 multiply_reduce_fusion
  847.3 11.1 %fusion.5 = f32[768,2048]{1,0:T(8,128)S(1)} fusion(f32[512,2048]{1,0:T(8,128)S(1)} %copy-done.53, f32[768]{0:T(1024)S(1)} %broadcast_multiply_fusion.1, f32[768]{0:T(1024)S(1)} %broadcast_multiply_fusion.2, f32[768]{0:T(1024)S(1)} %copy-done.72, f32[768]{0:T(1024)S(1)} %copy-done.70, bf16[384,2048]{1,0:T(8,128)(2,1)S(1)} %add_convert_fusion.8, ...), kind=kLoop, calls=%fused_computation.14 | loop fusion | flops 33030144 | bytes 16789504 | tf_op jit(solution)/shard_map/add | solution.py:1020
  863.7 4.5 all-to-all-start.2
  875.8 3.0 copy.262
  883.7 3.6 all-to-all-start.3
  890.0 3.0 collective-permute-start.37
  904.0 5.3 multiply_subtract_fusion.2
  (410 shorter events, 182.9 us)
Async XLA Ops:
  7.2 146.4 %copy-start = (bf16[512,2048]{1,0:T(8,128)(2,1)S(1)}, bf16[512,2048]{1,0:T(8,128)(2,1)}, u32[]{:S(2)}) copy-start(bf16[512,2048]{1,0:T(8,128)(2,1)} %param.60) | copy-start | bytes 6291460
  7.2 105.8 %all-gather.15.cloned.1.call-start = ((), (), s32[]{:S(2)}) async-start(), calls=%async_computation.12 | async-start | bytes 3932160 | tf_op jit(solution)/shard_map/all_gather | solution.py:66
  7.9 170.4 %all-gather.17.cloned.1.call-start = ((), (), s32[]{:S(2)}) async-start(), calls=%async_computation.13 | async-start | bytes 5242880 | tf_op jit(solution)/shard_map/all_gather | solution.py:66
  12.9 36.0 %all-to-all-start = ((bf16[8,2,8,2048]{3,2,1,0:T(8,128)(2,1)}), bf16[8,2,8,2048]{3,2,1,0:T(8,128)(2,1)S(1)}, u32[]{:S(2)}, u32[]{:S(2)}) async-start(bf16[8,2,8,2048]{3,2,1,0:T(8,128)(2,1)} %copy_bitcast_fusion.1), calls=%async_computation | async-start | bytes 1048576 | tf_op jit(solution)/shard_map/all_to_all | solution.py:654
  50.3 32.9 %all-to-all-start.1 = ((bf16[8,2,8,2048]{3,2,1,0:T(8,128)(2,1)}), bf16[8,2,8,2048]{3,2,1,0:T(8,128)(2,1)S(1)}, u32[]{:S(2)}, u32[]{:S(2)}) async-start(bf16[8,2,8,2048]{3,2,1,0:T(8,128)(2,1)} %broadcast_select_fusion), calls=%async_computation.1 | async-start | bytes 1048576 | tf_op jit(solution)/shard_map/all_to_all | solution.py:655
  53.9 205.4 %all-gather.19.cloned.1.call-start = ((), (), s32[]{:S(2)}) async-start(), calls=%async_computation.14 | async-start | bytes 5242880 | tf_op jit(solution)/shard_map/all_gather | solution.py:66
  53.9 44.8 %collective-permute-start.2 = (bf16[1,4,256]{2,1,0:T(4,128)(2,1)}, bf16[1,4,256]{2,1,0:T(4,128)(2,1)}, u32[]{:S(2)}, u32[]{:S(2)}) collective-permute-start(bf16[1,4,256]{2,1,0:T(4,128)(2,1)} %bitcast.22), channel_id=1, source_target_pairs={{0,4},{4,0},{8,12},{12,8},{16,20},{20,16},{24,28},{28,24},{1,5},{5... | collective-permute-start | bytes 6152 | tf_op jit(solution)/shard_map/ppermute | solution.py:100
  55.9 51.9 %collective-permute-start.5 = (bf16[512,256]{1,0:T(8,128)(2,1)}, bf16[512,256]{1,0:T(8,128)(2,1)}, u32[]{:S(2)}, u32[]{:S(2)}) collective-permute-start(bf16[512,256]{1,0:T(8,128)(2,1)} %param.40), channel_id=1, source_target_pairs={{0,4},{4,0},{8,12},{12,8},{16,20},{20,16},{24,28},{28,24},{1,5},{5... | collective-permute-start | bytes 786440 | tf_op jit(solution)/shard_map/ppermute | solution.py:47
  56.1 316.0 %all-gather.21.cloned.1.call-start = ((), (), s32[]{:S(2)}) async-start(), calls=%async_computation.15 | async-start | bytes 1310720 | tf_op jit(solution)/shard_map/all_gather | solution.py:66
  83.2 15.4 %copy-start.52 = (bf16[2,64,2048]{2,1,0:T(8,128)(2,1)}, bf16[2,64,2048]{2,1,0:T(8,128)(2,1)S(1)}, u32[]{:S(2)}) copy-start(bf16[2,64,2048]{2,1,0:T(8,128)(2,1)S(1)} %copy_bitcast_fusion) | copy-start | bytes 1572868
  83.2 13.0 %collective-permute-start = (bf16[2,64,2048]{2,1,0:T(8,128)(2,1)S(1)}, bf16[2,64,2048]{2,1,0:T(8,128)(2,1)S(1)}, u32[]{:S(2)}, u32[]{:S(2)}) collective-permute-start(bf16[2,64,2048]{2,1,0:T(8,128)(2,1)S(1)} %copy_bitcast_fusion), channel_id=1, source_target_pairs={{0,2},{1,3},{2,0},{3,1},{4,6},{5,7},{6,4},{7,5},{8,10},{9,11},{10,... | collective-permute-start | bytes 1572872 | tf_op jit(solution)/shard_map/ppermute | solution.py:57
  97.4 12.1 %collective-permute-start.1 = (bf16[2,2,64,2048]{3,2,1,0:T(8,128)(2,1)}, bf16[2,2,64,2048]{3,2,1,0:T(8,128)(2,1)}, u32[]{:S(2)}, u32[]{:S(2)}) collective-permute-start(bf16[2,2,64,2048]{3,2,1,0:T(8,128)(2,1)} %maximum_select_fusion.4), channel_id=1, source_target_pairs={{0,1},{1,0},{2,3},{3,2},{4,5},{5,4},{6,7},{7,6},{8,9},{9,8},{10,11... | collective-permute-start | bytes 3145736 | tf_op jit(solution)/shard_map/ppermute | solution.py:57
  99.5 3.7 collective-permute-start.3
  103.2 4.6 collective-permute-start.4
  104.9 104.4 %copy-start.9 = (f32[3,768,128]{2,1,0:T(8,128)}, f32[3,768,128]{2,1,0:T(8,128)S(1)}, u32[]{:S(2)}) copy-start(f32[3,768,128]{2,1,0:T(8,128)S(1)} %pad_maximum_fusion.8.refs_2_.refs_4_) | copy-start | bytes 3538948
  116.5 68.7 %collective-permute-start.6 = (bf16[4,3,256,512]{3,2,1,0:T(8,128)(2,1)}, bf16[4,3,256,512]{3,2,1,0:T(8,128)(2,1)}, u32[]{:S(2)}, u32[]{:S(2)}) collective-permute-start(bf16[4,3,256,512]{3,2,1,0:T(8,128)(2,1)} %bitcast.14.refs_0_), channel_id=1, source_target_pairs={{0,4},{4,0},{8,12},{12,8},{16,20},{20,16},{24,28},{28,24},{1,5},{5... | collective-permute-start | bytes 9437192 | tf_op jit(solution)/shard_map/ppermute | solution.py:47
  156.3 33.2 %copy-start.35 = (bf16[512,2048]{1,0:T(8,128)(2,1)S(1)}, bf16[512,2048]{1,0:T(8,128)(2,1)}, u32[]{:S(2)}) copy-start(bf16[512,2048]{1,0:T(8,128)(2,1)} %param.32) | copy-start | bytes 6291460
  185.2 90.7 %collective-permute-start.10 = (bf16[4,256,2048]{2,1,0:T(8,128)(2,1)}, bf16[4,256,2048]{2,1,0:T(8,128)(2,1)}, u32[]{:S(2)}, u32[]{:S(2)}) collective-permute-start(bf16[4,256,2048]{2,1,0:T(8,128)(2,1)} %bitcast.209), channel_id=1, source_target_pairs={{0,4},{4,0},{8,12},{12,8},{16,20},{20,16},{24,28},{28,24},{1,5},{5... | collective-permute-start | bytes 12582920 | tf_op jit(solution)/shard_map/ppermute | solution.py:47
  200.1 77.5 %collective-permute-start.7 = (bf16[256,2048]{1,0:T(8,128)(2,1)}, bf16[256,2048]{1,0:T(8,128)(2,1)}, u32[]{:S(2)}, u32[]{:S(2)}) collective-permute-start(bf16[256,2048]{1,0:T(8,128)(2,1)} %constant_dynamic-slice_fusion.7), channel_id=1, source_target_pairs={{0,1},{1,0},{2,3},{3,2},{4,5},{5,4},{6,7},{7,6},{8,9},{9,8},{10,11... | collective-permute-start | bytes 3145736 | tf_op jit(solution)/shard_map/ppermute | solution.py:57
  226.1 55.0 %copy-start.27 = (bf16[768,512]{1,0:T(8,128)(2,1)}, bf16[768,512]{1,0:T(8,128)(2,1)S(1)}, u32[]{:S(2)}) copy-start(bf16[768,512]{1,0:T(8,128)(2,1)S(1)} %get-tuple-element.108.refs_1_) | copy-start | bytes 2359300
  226.1 146.0 %copy-start.14 = (bf16[768,512]{1,0:T(8,128)(2,1)}, bf16[768,512]{1,0:T(8,128)(2,1)S(1)}, u32[]{:S(2)}) copy-start(bf16[768,512]{1,0:T(8,128)(2,1)S(1)} %get-tuple-element.93.refs_1_.refs_3_) | copy-start | bytes 2359300
  275.9 96.2 %collective-permute-start.11 = (bf16[4,2048,256]{2,1,0:T(8,128)(2,1)}, bf16[4,2048,256]{2,1,0:T(8,128)(2,1)}, u32[]{:S(2)}, u32[]{:S(2)}) collective-permute-start(bf16[4,2048,256]{2,1,0:T(8,128)(2,1)} %bitcast.198), channel_id=1, source_target_pairs={{0,4},{4,0},{8,12},{12,8},{16,20},{20,16},{24,28},{28,24},{1,5},{5... | collective-permute-start | bytes 12582920 | tf_op jit(solution)/shard_map/ppermute | solution.py:47
  277.5 94.6 %all-gather.23.cloned.1.call-start = ((), (), s32[]{:S(2)}) async-start(), calls=%async_computation.16 | async-start | bytes 1310720 | tf_op jit(solution)/shard_map/all_gather | solution.py:66
  277.5 24.5 %copy-start.82 = (s32[8]{0:T(128)S(1)}, s32[8]{0:T(128)}, u32[]{:S(2)}) copy-start(s32[8]{0:T(128)} %param.37) | copy-start | bytes 100
  279.5 20.8 %collective-permute-start.8 = (bf16[256,2048]{1,0:T(8,128)(2,1)S(1)}, bf16[256,2048]{1,0:T(8,128)(2,1)}, u32[]{:S(2)}, u32[]{:S(2)}) collective-permute-start(bf16[256,2048]{1,0:T(8,128)(2,1)S(1)} %add_convert_fusion.15), channel_id=1, source_target_pairs={{0,2},{1,3},{2,0},{3,1},{4,6},{5,7},{6,4},{7,5},{8,10},{9,11},{10,... | collective-permute-start | bytes 3145736 | tf_op jit(solution)/shard_map/ppermute | solution.py:57
  281.1 407.3 %reduce-scatter.5.cloned.1.call-start = ((), (), s32[]{:S(2)}) async-start(), calls=%async_computation.8 | async-start | bytes 6553600 | tf_op jit(solution)/shard_map/reduce_scatter | solution.py:70
  302.0 6.7 collective-permute-start.9
  386.0 29.1 %copy-start.78 = (s32[8]{0:T(128)S(1)}, s32[8]{0:T(128)}, u32[]{:S(2)}) copy-start(s32[8]{0:T(128)} %param.36) | copy-start | bytes 100
  386.0 2.7 collective-permute-start.12
  389.2 25.4 %collective-permute-start.13 = (bf16[256,2048]{1,0:T(8,128)(2,1)S(1)}, bf16[256,2048]{1,0:T(8,128)(2,1)S(1)}, u32[]{:S(2)}, u32[]{:S(2)}) collective-permute-start(bf16[256,2048]{1,0:T(8,128)(2,1)S(1)} %add_convert_fusion.13), channel_id=1, source_target_pairs={{0,2},{1,3},{2,0},{3,1},{4,6},{5,7},{6,4},{7,5},{8,10},{9,11},{10,... | collective-permute-start | bytes 3145736 | tf_op jit(solution)/shard_map/ppermute | solution.py:57
  415.0 6.4 collective-permute-start.14
  426.6 39.2 %copy-start.33 = (f32[512,1]{1,0:T(8,128)}, f32[512,1]{1,0:T(8,128)S(1)}, u32[]{:S(2)}) copy-start(f32[512,1]{1,0:T(8,128)S(1)} %get-tuple-element.101.scale_ref) | copy-start | bytes 6148
  508.0 19.0 %copy-start.79 = (s32[8]{0:T(128)S(1)}, s32[8]{0:T(128)}, u32[]{:S(2)}) copy-start(s32[8]{0:T(128)} %param.35) | copy-start | bytes 100
  508.2 10.0 %collective-permute-start.15 = (bf16[256,2048]{1,0:T(8,128)(2,1)S(1)}, bf16[256,2048]{1,0:T(8,128)(2,1)S(1)}, u32[]{:S(2)}, u32[]{:S(2)}) collective-permute-start(bf16[256,2048]{1,0:T(8,128)(2,1)S(1)} %constant_dynamic-slice_fusion.3), channel_id=1, source_target_pairs={{0,1},{1,0},{2,3},{3,2},{4,5},{5,4},{6,7},{7,6},{8,9},{9,8},{10,11... | collective-permute-start | bytes 3145736 | tf_op jit(solution)/shard_map/ppermute | solution.py:57
  512.6 3.5 collective-permute-start.17
  516.1 30.4 %copy-start.3 = (bf16[768,2048]{1,0:T(8,128)(2,1)S(1)}, bf16[768,2048]{1,0:T(8,128)(2,1)}, u32[]{:S(2)}) copy-start(bf16[768,2048]{1,0:T(8,128)(2,1)} %copy-done.2) | copy-start | bytes 9437188
  516.1 4.8 collective-permute-start.18
  519.5 24.1 %collective-permute-start.16 = (bf16[256,2048]{1,0:T(8,128)(2,1)}, bf16[256,2048]{1,0:T(8,128)(2,1)}, u32[]{:S(2)}, u32[]{:S(2)}) collective-permute-start(bf16[256,2048]{1,0:T(8,128)(2,1)} %add_convert_fusion.11), channel_id=1, source_target_pairs={{0,2},{1,3},{2,0},{3,1},{4,6},{5,7},{6,4},{7,5},{8,10},{9,11},{10,... | collective-permute-start | bytes 3145736 | tf_op jit(solution)/shard_map/ppermute | solution.py:57
  521.0 4.5 collective-permute-start.19
  546.5 4.4 collective-permute-start.20
  568.7 184.0 %reduce-scatter.11.cloned.1.call-start = ((), (), s32[]{:S(2)}) async-start(), calls=%async_computation.11 | async-start | bytes 3276800 | tf_op jit(solution)/shard_map/reduce_scatter | solution.py:70
  568.7 58.6 %collective-permute-start.21 = (bf16[4,1,1,256,1280]{4,3,2,1,0:T(8,128)(2,1)}, bf16[4,1,1,256,1280]{4,3,2,1,0:T(8,128)(2,1)S(1)}, u32[]{:S(2)}, u32[]{:S(2)}) collective-permute-start(bf16[4,1,1,256,1280]{4,3,2,1,0:T(8,128)(2,1)} %copy-done.25), channel_id=1, source_target_pairs={{0,4},{4,0},{8,12},{12,8},{16,20},{20,16},{24,28},{28,24},{1,5},{5... | collective-permute-start | bytes 7864328 | tf_op jit(solution)/shard_map/ppermute | solution.py:47
  629.5 174.9 %reduce-scatter.7.cloned.1.call-start = ((), (), s32[]{:S(2)}) async-start(), calls=%async_computation.9 | async-start | bytes 5242880 | tf_op jit(solution)/shard_map/reduce_scatter | solution.py:70
  629.6 91.6 %collective-permute-start.23 = (bf16[4,1,1,256,2048]{4,3,2,1,0:T(8,128)(2,1)}, bf16[4,1,1,256,2048]{4,3,2,1,0:T(8,128)(2,1)}, u32[]{:S(2)}, u32[]{:S(2)}) collective-permute-start(bf16[4,1,1,256,2048]{4,3,2,1,0:T(8,128)(2,1)} %grad_blocks.9), channel_id=1, source_target_pairs={{0,4},{4,0},{8,12},{12,8},{16,20},{20,16},{24,28},{28,24},{1,5},{5... | collective-permute-start | bytes 12582920 | tf_op jit(solution)/shard_map/ppermute | solution.py:47
  634.3 34.7 %slice-start.4 = ((s8[6291456]{0:T(1024)(128)(4,1)}), s8[2097152]{0:T(1024)(128)(4,1)S(1)}, s32[]{:S(2)}) async-start(s8[6291456]{0:T(1024)(128)(4,1)} %bitcast.207), calls=%async_computation.21 | async-start | bytes 4194304
  645.4 23.6 %slice-start.5 = ((s8[6291456]{0:T(1024)(128)(4,1)}), s8[4194304]{0:T(1024)(128)(4,1)S(1)}, s32[]{:S(2)}) async-start(s8[6291456]{0:T(1024)(128)(4,1)} %bitcast.207), calls=%async_computation.22 | async-start | bytes 8388608
  677.8 7.4 collective-permute-start.22
  728.9 166.9 %reduce-scatter.9.cloned.1.call-start = ((), (), s32[]{:S(2)}) async-start(), calls=%async_computation.10 | async-start | bytes 3932160 | tf_op jit(solution)/shard_map/reduce_scatter | solution.py:70
  729.0 68.2 %collective-permute-start.24 = (bf16[4,1,3,256,512]{4,3,2,1,0:T(8,128)(2,1)}, bf16[4,1,3,256,512]{4,3,2,1,0:T(8,128)(2,1)}, u32[]{:S(2)}, u32[]{:S(2)}) collective-permute-start(bf16[4,1,3,256,512]{4,3,2,1,0:T(8,128)(2,1)} %copy-done.24), channel_id=1, source_target_pairs={{0,4},{4,0},{8,12},{12,8},{16,20},{20,16},{24,28},{28,24},{1,5},{5... | collective-permute-start | bytes 9437192 | tf_op jit(solution)/shard_map/ppermute | solution.py:47
  745.2 56.5 %collective-permute-start.25 = (bf16[384,2048]{1,0:T(8,128)(2,1)}, bf16[384,2048]{1,0:T(8,128)(2,1)}, u32[]{:S(2)}, u32[]{:S(2)}) collective-permute-start(bf16[384,2048]{1,0:T(8,128)(2,1)} %add_convert_fusion.9), channel_id=1, source_target_pairs={{0,2},{1,3},{2,0},{3,1},{4,6},{5,7},{6,4},{7,5},{8,10},{9,11},{10,... | collective-permute-start | bytes 4718600 | tf_op jit(solution)/shard_map/ppermute | solution.py:57
  806.6 32.4 %collective-permute-start.29 = (bf16[384,2048]{1,0:T(8,128)(2,1)S(1)}, bf16[384,2048]{1,0:T(8,128)(2,1)}, u32[]{:S(2)}, u32[]{:S(2)}) collective-permute-start(bf16[384,2048]{1,0:T(8,128)(2,1)S(1)} %add_convert_fusion.8), channel_id=1, source_target_pairs={{0,1},{1,0},{2,3},{3,2},{4,5},{5,4},{6,7},{7,6},{8,9},{9,8},{10,11... | collective-permute-start | bytes 4718600 | tf_op jit(solution)/shard_map/ppermute | solution.py:57
  806.7 18.8 %collective-permute-start.32 = (bf16[256,1280]{1,0:T(8,128)(2,1)}, bf16[256,1280]{1,0:T(8,128)(2,1)}, u32[]{:S(2)}, u32[]{:S(2)}) collective-permute-start(bf16[256,1280]{1,0:T(8,128)(2,1)} %slice_bitcast_fusion.3), channel_id=1, source_target_pairs={{0,4},{4,0},{8,12},{12,8},{16,20},{20,16},{24,28},{28,24},{1,5},{5... | collective-permute-start | bytes 1966088 | tf_op jit(solution)/shard_map/ppermute | solution.py:47
  818.2 5.5 collective-permute-start.26
  823.8 14.3 %collective-permute-start.27 = (bf16[128,2048]{1,0:T(8,128)(2,1)S(1)}, bf16[128,2048]{1,0:T(8,128)(2,1)S(1)}, u32[]{:S(2)}, u32[]{:S(2)}) collective-permute-start(bf16[128,2048]{1,0:T(8,128)(2,1)S(1)} %add_convert_fusion.17), channel_id=1, source_target_pairs={{0,2},{1,3},{2,0},{3,1},{4,6},{5,7},{6,4},{7,5},{8,10},{9,11},{10,... | collective-permute-start | bytes 1572872 | tf_op jit(solution)/shard_map/ppermute | solution.py:57
  839.0 48.3 %collective-permute-start.28 = (bf16[128,2048]{1,0:T(8,128)(2,1)}, bf16[128,2048]{1,0:T(8,128)(2,1)}, u32[]{:S(2)}, u32[]{:S(2)}) collective-permute-start(bf16[128,2048]{1,0:T(8,128)(2,1)} %add_convert_fusion.16), channel_id=1, source_target_pairs={{0,1},{1,0},{2,3},{3,2},{4,5},{5,4},{6,7},{7,6},{8,9},{9,8},{10,11... | collective-permute-start | bytes 1572872 | tf_op jit(solution)/shard_map/ppermute | solution.py:57
  846.8 14.4 %collective-permute-start.33 = (f32[4,2048]{1,0:T(4,128)S(1)}, f32[4,2048]{1,0:T(4,128)S(1)}, u32[]{:S(2)}, u32[]{:S(2)}) collective-permute-start(f32[4,2048]{1,0:T(4,128)S(1)} %pad_maximum_fusion.9), channel_id=1, source_target_pairs={{0,1},{1,0},{2,3},{3,2},{4,5},{5,4},{6,7},{7,6},{8,9},{9,8},{10,11... | collective-permute-start | bytes 98312 | tf_op jit(solution)/shard_map/ppermute | solution.py:128
  861.2 6.9 collective-permute-start.34
  863.7 18.6 %all-to-all-start.2 = ((bf16[8,1,8,2048]{3,2,1,0:T(8,128)(2,1)}), bf16[8,1,8,2048]{3,2,1,0:T(8,128)(2,1)S(1)}, u32[]{:S(2)}, u32[]{:S(2)}) async-start(bf16[8,1,8,2048]{3,2,1,0:T(8,128)(2,1)} %fusion.25), calls=%async_computation.4 | async-start | bytes 524288 | tf_op jit(solution)/shard_map/all_to_all | solution.py:654
  868.2 12.6 %collective-permute-start.35 = (f32[4,2048]{1,0:T(4,128)S(1)}, f32[4,2048]{1,0:T(4,128)S(1)}, u32[]{:S(2)}, u32[]{:S(2)}) collective-permute-start(f32[4,2048]{1,0:T(4,128)S(1)} %fusion.75), channel_id=1, source_target_pairs={{0,4},{4,0},{8,12},{12,8},{16,20},{20,16},{24,28},{28,24},{1,5},{5... | collective-permute-start | bytes 98312 | tf_op jit(solution)/shard_map/ppermute | solution.py:128
  880.8 9.2 %collective-permute-start.36 = (f32[4,2048]{1,0:T(4,128)S(1)}, f32[4,2048]{1,0:T(4,128)S(1)}, u32[]{:S(2)}, u32[]{:S(2)}) collective-permute-start(f32[4,2048]{1,0:T(4,128)S(1)} %add.383), channel_id=1, source_target_pairs={{0,8},{4,12},{8,0},{12,4},{16,24},{20,28},{24,16},{28,20},{1,9},{5... | collective-permute-start | bytes 98312 | tf_op jit(solution)/shard_map/ppermute | solution.py:128
  883.7 12.2 %all-to-all-start.3 = ((bf16[8,1,8,2048]{3,2,1,0:T(8,128)(2,1)}), bf16[8,1,8,2048]{3,2,1,0:T(8,128)(2,1)S(1)}, u32[]{:S(2)}, u32[]{:S(2)}) async-start(bf16[8,1,8,2048]{3,2,1,0:T(8,128)(2,1)} %fusion.26), calls=%async_computation.5 | async-start | bytes 524288 | tf_op jit(solution)/shard_map/all_to_all | solution.py:655
  890.0 9.1 collective-permute-start.37
  895.9 6.8 collective-permute-start.30
  903.9 6.5 collective-permute-start.31
  (76 other events, 413.0 us)
Sparse Core Ops, SparseCore 0:
  9.6 87.2 all-gather.14
  98.5 79.7 all-gather.16
  179.9 79.2 all-gather.18
  277.6 26.4 all-gather.20
  305.5 27.4 all-gather.22
  568.8 92.2 reduce-scatter.4
  663.4 52.6 reduce-scatter.10
  729.1 75.2 reduce-scatter.6
  806.8 60.7 reduce-scatter.8

commit v4 on v3

--- a/solution.py
+++ b/solution.py
@@ -937,8 +937,10 @@
     other_mean = jnp.sum(log_chance[:, half:] * other_live, axis=1) / other_total
     gaps = jnp.stack([own_mean[0] - own_mean[1], other_mean[0] - other_mean[1]])
     row = jnp.stack([peak, 1.0 / total], axis=1)
-    every = gather_small(gaps)
     back_part = head_pull(logits, table, row, targets)
+    if lax.axis_size("tensor") == 4:
+        back_part = tensor_near(back_part)
+    every = gather_small(after(gaps, back_part))
     drift = jnp.sum(every[:, 1]) / groups
     sign = (2 * desirable - 1).astype(F32)
     settled = jax.nn.sigmoid(KTO_BETA * sign * (every[:, 0] - jax.nn.softplus(drift)))
@@ -949,7 +951,12 @@
         [-slope[own_index] * own_live / own_total, pull * other_live / other_total]
     )
 
-    back_sum = tensor_halves(back_part, row_weight)
+    if lax.axis_size("tensor") == 4:
+        back_part = after(tensor_far(back_part), row_weight)
+        side_row = (lax.axis_index("tensor") % 2).reshape(1)
+        back_sum = (back_part, tensor_swap(back_part, 1), side_row)
+    else:
+        back_sum = tensor_halves(back_part)
     back_out, branch_low = pull_rows(back_sum, row_weight[:, None], unit_out, inverse_out)
 
     features_scored = jnp.concatenate([hidden[half:], attended[half:]], axis=1)

time: 933 us -> 929 us (level)
  transfers between devices with their start and end apart: 51 -> 51, of which waited for: 21 -> 22; matrix products, arithmetic and copies ran while one was open for 21% -> 21% of each run, Pallas kernels for 18% -> 18%
where the time goes in v4:
time: 929 us; the launch traced here: 917 us
  waiting for transfers between devices  321 us (35%)
  Pallas kernels  278 us (30%)
  other arithmetic  141 us (15%)
  local copies, waits for them, and re-layouts  79 us (9%)
  starting transfers between devices  54.3 us (6%)
  between operations  23.8 us (3%)
  blocking collectives  10.4 us (1%)
  matrix products  10.1 us (1%)
    ppermute x8, waiting for transfers between devices, pair_swap(): return lax.ppermute(value, 'dp', [(i, i ^ 1) for i in range(groups)])  124 us
    pallas_call x2, Pallas kernels, head_stats(): pl.pallas_call(lambda *refs: head_body(vocab, *refs), grid=(tiles,), in_s...  76.8 us
    ppermute x19, waiting for transfers between devices, tensor_swap(): lax.ppermute(value, 'tensor', [(i, i ^ bit) for i in range(lax.axis_size(...  66.7 us
    all_gather x5, waiting for transfers between devices, gather_ring(): return lax.all_gather(piece, 'dp', axis_index_groups=ring_groups())  55.2 us
    unnamed x192, local copies, waits for them, and re-layouts  50.1 us
    pallas_call x1, Pallas kernels, head_pull(): pl.pallas_call(lambda *refs: head_pull_body(vocab, tiles, *refs), grid=(t...  36.8 us
    all_to_all x2, waiting for transfers between devices, borrow_rows(): lax.all_to_all(jnp.take(spread, order, axis=0), 'dp', split_axis=0, conca...  29.9 us
    pallas_call x7, Pallas kernels, grad_blocks(): pl.pallas_call(lambda low_ref, *refs: grad_body(*refs), grid_spec=pltpu.P...  29.7 us
  transfers between devices with their start and end apart: 51, of which 22 were waited for; matrix products, arithmetic and copies ran while one was open for 21% of the time, Pallas kernels for 18%

profile of v4, /device:TPU:0, one launch (start us, length us, event | category | flops | bytes accessed | tf_op | source)
XLA Modules:
  0.0 917.2 jit_solution(792285088953583452)
XLA Ops:
  8.7 3.3 fusion.63
  12.9 7.3 all-to-all-start
  20.7 28.1 %all-to-all-done = bf16[8,2,8,2048]{3,2,1,0:T(8,128)(2,1)S(1)} async-done(((bf16[8,2,8,2048]{3,2,1,0:T(8,128)(2,1)}), bf16[8,2,8,2048]{3,2,1,0:T(8,128)(2,1)S(1)}, u32[]{:S(2)}, u32[]{:S(2)}) %all-to-all-start) | async-done | bytes 524320 | tf_op jit(solution)/shard_map/all_to_all | solution.py:654
  50.3 3.6 all-to-all-start.1
  56.1 27.0 %all-to-all-done.1 = bf16[8,2,8,2048]{3,2,1,0:T(8,128)(2,1)S(1)} async-done(((bf16[8,2,8,2048]{3,2,1,0:T(8,128)(2,1)}), bf16[8,2,8,2048]{3,2,1,0:T(8,128)(2,1)S(1)}, u32[]{:S(2)}, u32[]{:S(2)}) %all-to-all-start.1) | async-done | bytes 524320 | tf_op jit(solution)/shard_map/all_to_all | solution.py:655
  88.9 7.3 collective-permute-done
  113.0 2.9 slice_bitcast_fusion.1
  120.2 3.4 fusion
  124.2 13.0 %attend.2 = (bf16[512,512]{1,0:T(8,128)(2,1)S(1)}, bf16[512,512]{1,0:T(8,128)(2,1)}, bf16[768,512]{1,0:T(8,128)(2,1)}, bf16[768,512]{1,0:T(8,128)(2,1)}) custom-call(bf16[768,2048]{1,0:T(8,128)(2,1)} %get-tuple-element.78.refs_0_, bf16[3,2048,512]{2,1,0:T(8,128)(2,1)} %refs_1_.1, f32[3,768,128]{2,1,0:T(8,128)S(1)} %pad_maximum_fusion.8.refs_2_.refs_4_), custom_call_target="tpu_custom_call" | custom-call | flops 1 | bytes 1 | tf_op jit(solution)/shard_map/attend/pallas_call | solution.py:267
  137.2 8.9 hidden.2
  146.1 7.5 fusion.70
  156.3 22.1 %all-gather.17.cloned.1.call-done = bf16[1024,2048]{1,0:T(8,128)(2,1)} async-done(((bf16[256,2048]{1,0:T(8,128)(2,1)}), bf16[1024,2048]{1,0:T(8,128)(2,1)}) %all-gather.17.cloned.1.call-update) | async-done | bytes 4194320 | tf_op jit(solution)/shard_map/all_gather | solution.py:66
  178.3 6.8 collective-permute-done.6.refs_1_
  191.6 7.4 subtract_multiply_fusion
  200.1 5.4 maximum_select_fusion
  206.1 3.2 copy.234
  209.3 15.0 %attend.3 = (bf16[768,512]{1,0:T(8,128)(2,1)S(1)}, bf16[768,512]{1,0:T(8,128)(2,1)S(1)}, bf16[768,512]{1,0:T(8,128)(2,1)S(1)}, bf16[768,512]{1,0:T(8,128)(2,1)S(1)}) custom-call(bf16[768,2048]{1,0:T(8,128)(2,1)} %get-tuple-element.295.refs_0_, bf16[3,2048,512]{2,1,0:T(8,128)(2,1)} %bitcast.202, f32[3,768,128]{2,1,0:T(8,128)S(1)} %pad_maximum_fusion.8.refs_2_.refs_4_), custom_call_target="tpu_custom_call" | custom-call | flops 1 | bytes 1 | tf_op jit(solution)/shard_map/attend/pallas_call | solution.py:267
  226.1 33.1 %all-gather.19.cloned.1.call-done = bf16[8192,256]{1,0:T(8,128)(2,1)} async-done(((bf16[2048,256]{1,0:T(8,128)(2,1)}), bf16[8192,256]{1,0:T(8,128)(2,1)}) %all-gather.19.cloned.1.call-update) | async-done | bytes 4194320 | tf_op jit(solution)/shard_map/all_gather | solution.py:66
  259.3 16.6 %collective-permute-done.10.refs_1_ = bf16[4,256,2048]{2,1,0:T(8,128)(2,1)} collective-permute-done((bf16[4,256,2048]{2,1,0:T(8,128)(2,1)}, bf16[4,256,2048]{2,1,0:T(8,128)(2,1)}, u32[]{:S(2)}, u32[]{:S(2)}) %collective-permute-start.10) | collective-permute-done | bytes 4194336 | tf_op jit(solution)/shard_map/ppermute | solution.py:47
  281.1 19.2 %collective-permute-done.8 = bf16[256,2048]{1,0:T(8,128)(2,1)} collective-permute-done((bf16[256,2048]{1,0:T(8,128)(2,1)S(1)}, bf16[256,2048]{1,0:T(8,128)(2,1)}, u32[]{:S(2)}, u32[]{:S(2)}) %collective-permute-start.8) | collective-permute-done | bytes 1048608 | tf_op jit(solution)/shard_map/ppermute | solution.py:57
  305.6 3.1 pad_maximum_fusion.4.x_ref
  308.7 5.6 out_rows.2
  314.3 37.6 %head.2 = f32[8,512]{1,0:T(8,128)S(1)} custom-call(bf16[512,2048]{1,0:T(8,128)(2,1)S(1)} %get-tuple-element.90.refs_0_, bf16[12576,2048]{1,0:T(8,128)(2,1)} %bitcast.192, s32[512,1]{1,0:T(8,128)S(1)} %and_select_fusion.refs_2_.refs_3_), custom_call_target="tpu_custom_call" | custom-call | flops 1 | bytes 1 | tf_op jit(solution)/shard_map/head/pallas_call | solution.py:719
  351.9 5.2 all-gather.7
  357.2 13.3 %hidden.3 = (bf16[768,2048]{1,0:T(8,128)(2,1)S(1)}, f32[512,2048]{1,0:T(8,128)}) custom-call(s32[1]{0:T(128)} %bitcast.16.low_ref, bf16[768,2048]{1,0:T(8,128)(2,1)} %get-tuple-element.91.x_ref, bf16[4,256,2048]{2,1,0:T(8,128)(2,1)} %bitcast.209, bf16[4,256,2048]{2,1,0:T(8,128)(2,1)} %collective-permute-done.10.refs_1_), custom_call_target="tpu_custom_call" | custom-call | flops 1 | bytes 1 | tf_op jit(solution)/shard_map/hidden/pallas_call | solution.py:387
  374.6 11.3 %branch.2 = bf16[512,2048]{1,0:T(8,128)(2,1)S(1)} custom-call(s32[1]{0:T(128)} %bitcast.16.low_ref, bf16[768,2048]{1,0:T(8,128)(2,1)} %copy-done.2, bf16[768,512]{1,0:T(8,128)(2,1)S(1)} %get-tuple-element.94.refs_1_.refs_3_, bf16[768,2048]{1,0:T(8,128)(2,1)} %copy-done.2, bf16[768,512]{1,0:T(8,128)(2,1)S(1)} %get-tuple-element.94.refs_1_.refs_3_, ...), custom_call_target="tpu_custom_call" | custom-call | flops 1 | bytes 1 | tf_op jit(solution)/shard_map/branch/pallas_call | solution.py:513
  390.7 23.9 %collective-permute-done.13 = bf16[256,2048]{1,0:T(8,128)(2,1)S(1)} collective-permute-done((bf16[256,2048]{1,0:T(8,128)(2,1)S(1)}, bf16[256,2048]{1,0:T(8,128)(2,1)S(1)}, u32[]{:S(2)}, u32[]{:S(2)}) %collective-permute-start.13) | collective-permute-done | bytes 1048608 | tf_op jit(solution)/shard_map/ppermute | solution.py:57
  418.3 3.1 pad_maximum_fusion.5.x_ref
  421.4 5.1 out_rows.3
  426.6 39.2 %head.3 = (f32[512,12576]{1,0:T(8,128)}, f32[8,512]{1,0:T(8,128)S(1)}) custom-call(bf16[512,2048]{1,0:T(8,128)(2,1)S(1)} %get-tuple-element.96.refs_0_, bf16[12576,2048]{1,0:T(8,128)(2,1)} %bitcast.193, s32[512,1]{1,0:T(8,128)S(1)} %and_select_fusion.refs_2_.refs_3_), custom_call_target="tpu_custom_call" | custom-call | flops 1 | bytes 1 | tf_op jit(solution)/shard_map/head/pallas_call | solution.py:719
  465.7 5.2 all-gather.8
  471.2 36.8 %head_pull.1 = bf16[512,2048]{1,0:T(8,128)(2,1)S(1)} custom-call(f32[512,12576]{1,0:T(8,128)} %get-tuple-element.97.refs_0_, bf16[12576,2048]{1,0:T(8,128)(2,1)} %bitcast.194, f32[512,2]{1,0:T(8,128)S(1)} %copy.237.refs_2_, s32[512,1]{1,0:T(8,128)S(1)} %and_select_fusion.refs_2_.refs_3_), custom_call_target="tpu_custom_call" | custom-call | flops 1 | bytes 1 | tf_op jit(solution)/shard_map/head_pull/pallas_call | solution.py:778
  515.9 3.1 collective-permute-done.17
  533.2 6.3 collective-permute-done.16
  548.7 6.7 pull_rows.1
  557.9 6.7 grad_blocks.8
  566.9 10.7 %pull_units.2 = bf16[512,2048]{1,0:T(8,128)(2,1)S(1)} custom-call(s32[1]{0:T(128)} %bitcast.16.low_ref, bf16[512,2048]{1,0:T(8,128)(2,1)S(1)} %get-tuple-element.109.refs_0_.x_ref, bf16[4,2048,256]{2,1,0:T(8,128)(2,1)} %bitcast.199, bf16[4,2048,256]{2,1,0:T(8,128)(2,1)} %collective-permute-done.11.refs_5_.refs_1_.refs_3_, f32[512,2048]{1,0:T(8,128)} %get-tuple-element.107.refs_2_), custom_call_target="tpu_custom_call" | custom-call | flops 1 | bytes 1 | tf_op jit(solution)/shard_map/pull_units/pallas_call | solution.py:419
  577.6 4.4 grad_blocks.9
  584.5 38.7 %collective-permute-done.21 = bf16[4,1,1,256,1280]{4,3,2,1,0:T(8,128)(2,1)S(1)} collective-permute-done((bf16[4,1,1,256,1280]{4,3,2,1,0:T(8,128)(2,1)}, bf16[4,1,1,256,1280]{4,3,2,1,0:T(8,128)(2,1)S(1)}, u32[]{:S(2)}, u32[]{:S(2)}) %collective-permute-start.21) | collective-permute-done | bytes 2621472 | tf_op jit(solution)/shard_map/ppermute | solution.py:47
  630.3 9.4 %attend_back.1.refs_1_.x_ref = bf16[3,768,512]{2,1,0:T(8,128)(2,1)} custom-call(bf16[512,512]{1,0:T(8,128)(2,1)S(1)} %pull_units.3.refs_0_, bf16[768,512]{1,0:T(8,128)(2,1)S(1)} %copy-done.28, bf16[768,512]{1,0:T(8,128)(2,1)S(1)} %copy-done.30, bf16[768,512]{1,0:T(8,128)(2,1)S(1)} %copy-done.32, f32[3,768,128]{2,1,0:T(8,128)S(1)} %copy-done.10), custom_call_target="tpu_custom_call" | custom-call | flops 1 | bytes 1 | tf_op jit(solution)/shard_map/attend_back/pallas_call | solution.py:321
  641.4 11.8 %shard_terms.2 = f32[768,2048]{1,0:T(8,128)} custom-call(s32[1]{0:T(128)} %bitcast.16.low_ref, bf16[3,768,512]{2,1,0:T(8,128)(2,1)S(1)} %copy-done.4, bf16[4,3,256,512]{3,2,1,0:T(8,128)(2,1)} %bitcast.14.refs_0_, bf16[4,3,256,512]{3,2,1,0:T(8,128)(2,1)} %collective-permute-done.6.refs_1_), custom_call_target="tpu_custom_call" | custom-call | flops 1 | bytes 1 | tf_op jit(solution)/shard_map/shard_terms/pallas_call | solution.py:555
  653.2 11.6 %shard_terms.3 = f32[512,2048]{1,0:T(8,128)} custom-call(s32[1]{0:T(128)} %bitcast.16.low_ref, bf16[1,512,2048]{2,1,0:T(8,128)(2,1)S(1)} %bitcast.184, bf16[4,1,256,2048]{3,2,1,0:T(8,128)(2,1)} %bitcast.210, bf16[4,1,256,2048]{3,2,1,0:T(8,128)(2,1)} %bitcast.69.refs_1_), custom_call_target="tpu_custom_call" | custom-call | flops 1 | bytes 1 | tf_op jit(solution)/shard_map/shard_terms/pallas_call | solution.py:555
  664.8 3.9 fusion.8
  674.6 4.6 grad_blocks.11
  681.0 3.2 add_convert_fusion.9
  687.4 4.5 grad_blocks.12
  691.9 25.1 %collective-permute-done.23 = bf16[4,1,1,256,2048]{4,3,2,1,0:T(8,128)(2,1)} collective-permute-done((bf16[4,1,1,256,2048]{4,3,2,1,0:T(8,128)(2,1)}, bf16[4,1,1,256,2048]{4,3,2,1,0:T(8,128)(2,1)}, u32[]{:S(2)}, u32[]{:S(2)}) %collective-permute-start.23) | collective-permute-done | bytes 4194336 | tf_op jit(solution)/shard_map/ppermute | solution.py:47
  717.0 7.8 fusion.7
  742.6 5.1 fusion.53
  751.0 4.6 grad_blocks.13
  756.5 36.6 %collective-permute-done.24 = bf16[4,1,3,256,512]{4,3,2,1,0:T(8,128)(2,1)} collective-permute-done((bf16[4,1,3,256,512]{4,3,2,1,0:T(8,128)(2,1)}, bf16[4,1,3,256,512]{4,3,2,1,0:T(8,128)(2,1)}, u32[]{:S(2)}, u32[]{:S(2)}) %collective-permute-start.24) | collective-permute-done | bytes 3145760 | tf_op jit(solution)/shard_map/ppermute | solution.py:47
  793.1 4.5 fusion.11
  797.6 3.1 reduce-scatter.7.cloned.1.call-done
  804.6 9.8 %branch.3 = bf16[256,2048]{1,0:T(8,128)(2,1)S(1)} custom-call(s32[1]{0:T(128)} %bitcast.16.low_ref, bf16[768,2048]{1,0:T(8,128)(2,1)} %copy-done.2, bf16[768,512]{1,0:T(8,128)(2,1)S(1)} %copy-done.16, bf16[4,2048,256]{2,1,0:T(8,128)(2,1)} %bitcast.200, bf16[4,2048,256]{2,1,0:T(8,128)(2,1)} %collective-permute-done.11.refs_5_.refs_1_.refs_3_, ...), custom_call_target="tpu_custom_call" | custom-call | flops 1 | bytes 1 | tf_op jit(solution)/shard_map/branch/pallas_call | solution.py:513
  814.8 5.3 multiply_subtract_fusion
  823.3 3.6 multiply_subtract_fusion.1
  826.9 7.5 collective-permute-done.27
  835.5 7.6 multiply_reduce_fusion
  843.7 11.1 %fusion.5 = f32[768,2048]{1,0:T(8,128)S(1)} fusion(f32[512,2048]{1,0:T(8,128)S(1)} %copy-done.53, f32[768]{0:T(1024)S(1)} %broadcast_multiply_fusion.1, f32[768]{0:T(1024)S(1)} %broadcast_multiply_fusion.2, f32[768]{0:T(1024)S(1)} %copy-done.72, f32[768]{0:T(1024)S(1)} %copy-done.70, bf16[384,2048]{1,0:T(8,128)(2,1)S(1)} %add_convert_fusion.8, ...), kind=kLoop, calls=%fused_computation.14 | loop fusion | flops 33030144 | bytes 16789504 | tf_op jit(solution)/shard_map/add | solution.py:1027
  860.0 4.5 all-to-all-start.2
  872.1 3.0 copy.262
  880.0 3.6 all-to-all-start.3
  886.4 3.0 collective-permute-start.37
  900.4 5.3 multiply_subtract_fusion.2
  (410 shorter events, 185.8 us)
Async XLA Ops:
  7.2 146.4 %copy-start = (bf16[512,2048]{1,0:T(8,128)(2,1)S(1)}, bf16[512,2048]{1,0:T(8,128)(2,1)}, u32[]{:S(2)}) copy-start(bf16[512,2048]{1,0:T(8,128)(2,1)} %param.60) | copy-start | bytes 6291460
  7.2 105.8 %all-gather.15.cloned.1.call-start = ((), (), s32[]{:S(2)}) async-start(), calls=%async_computation.12 | async-start | bytes 3932160 | tf_op jit(solution)/shard_map/all_gather | solution.py:66
  7.9 170.4 %all-gather.17.cloned.1.call-start = ((), (), s32[]{:S(2)}) async-start(), calls=%async_computation.13 | async-start | bytes 5242880 | tf_op jit(solution)/shard_map/all_gather | solution.py:66
  12.9 36.0 %all-to-all-start = ((bf16[8,2,8,2048]{3,2,1,0:T(8,128)(2,1)}), bf16[8,2,8,2048]{3,2,1,0:T(8,128)(2,1)S(1)}, u32[]{:S(2)}, u32[]{:S(2)}) async-start(bf16[8,2,8,2048]{3,2,1,0:T(8,128)(2,1)} %copy_bitcast_fusion.1), calls=%async_computation | async-start | bytes 1048576 | tf_op jit(solution)/shard_map/all_to_all | solution.py:654
  50.3 32.9 %all-to-all-start.1 = ((bf16[8,2,8,2048]{3,2,1,0:T(8,128)(2,1)}), bf16[8,2,8,2048]{3,2,1,0:T(8,128)(2,1)S(1)}, u32[]{:S(2)}, u32[]{:S(2)}) async-start(bf16[8,2,8,2048]{3,2,1,0:T(8,128)(2,1)} %broadcast_select_fusion), calls=%async_computation.1 | async-start | bytes 1048576 | tf_op jit(solution)/shard_map/all_to_all | solution.py:655
  53.9 205.4 %all-gather.19.cloned.1.call-start = ((), (), s32[]{:S(2)}) async-start(), calls=%async_computation.14 | async-start | bytes 5242880 | tf_op jit(solution)/shard_map/all_gather | solution.py:66
  53.9 44.8 %collective-permute-start.2 = (bf16[1,4,256]{2,1,0:T(4,128)(2,1)}, bf16[1,4,256]{2,1,0:T(4,128)(2,1)}, u32[]{:S(2)}, u32[]{:S(2)}) collective-permute-start(bf16[1,4,256]{2,1,0:T(4,128)(2,1)} %bitcast.22), channel_id=1, source_target_pairs={{0,4},{4,0},{8,12},{12,8},{16,20},{20,16},{24,28},{28,24},{1,5},{5... | collective-permute-start | bytes 6152 | tf_op jit(solution)/shard_map/ppermute | solution.py:100
  55.9 51.9 %collective-permute-start.5 = (bf16[512,256]{1,0:T(8,128)(2,1)}, bf16[512,256]{1,0:T(8,128)(2,1)}, u32[]{:S(2)}, u32[]{:S(2)}) collective-permute-start(bf16[512,256]{1,0:T(8,128)(2,1)} %param.40), channel_id=1, source_target_pairs={{0,4},{4,0},{8,12},{12,8},{16,20},{20,16},{24,28},{28,24},{1,5},{5... | collective-permute-start | bytes 786440 | tf_op jit(solution)/shard_map/ppermute | solution.py:47
  56.1 316.0 %all-gather.21.cloned.1.call-start = ((), (), s32[]{:S(2)}) async-start(), calls=%async_computation.15 | async-start | bytes 1310720 | tf_op jit(solution)/shard_map/all_gather | solution.py:66
  83.2 15.4 %copy-start.52 = (bf16[2,64,2048]{2,1,0:T(8,128)(2,1)}, bf16[2,64,2048]{2,1,0:T(8,128)(2,1)S(1)}, u32[]{:S(2)}) copy-start(bf16[2,64,2048]{2,1,0:T(8,128)(2,1)S(1)} %copy_bitcast_fusion) | copy-start | bytes 1572868
  83.2 13.0 %collective-permute-start = (bf16[2,64,2048]{2,1,0:T(8,128)(2,1)S(1)}, bf16[2,64,2048]{2,1,0:T(8,128)(2,1)S(1)}, u32[]{:S(2)}, u32[]{:S(2)}) collective-permute-start(bf16[2,64,2048]{2,1,0:T(8,128)(2,1)S(1)} %copy_bitcast_fusion), channel_id=1, source_target_pairs={{0,2},{1,3},{2,0},{3,1},{4,6},{5,7},{6,4},{7,5},{8,10},{9,11},{10,... | collective-permute-start | bytes 1572872 | tf_op jit(solution)/shard_map/ppermute | solution.py:57
  97.4 12.1 %collective-permute-start.1 = (bf16[2,2,64,2048]{3,2,1,0:T(8,128)(2,1)}, bf16[2,2,64,2048]{3,2,1,0:T(8,128)(2,1)}, u32[]{:S(2)}, u32[]{:S(2)}) collective-permute-start(bf16[2,2,64,2048]{3,2,1,0:T(8,128)(2,1)} %maximum_select_fusion.4), channel_id=1, source_target_pairs={{0,1},{1,0},{2,3},{3,2},{4,5},{5,4},{6,7},{7,6},{8,9},{9,8},{10,11... | collective-permute-start | bytes 3145736 | tf_op jit(solution)/shard_map/ppermute | solution.py:57
  99.5 3.7 collective-permute-start.3
  103.2 4.6 collective-permute-start.4
  104.9 104.4 %copy-start.9 = (f32[3,768,128]{2,1,0:T(8,128)}, f32[3,768,128]{2,1,0:T(8,128)S(1)}, u32[]{:S(2)}) copy-start(f32[3,768,128]{2,1,0:T(8,128)S(1)} %pad_maximum_fusion.8.refs_2_.refs_4_) | copy-start | bytes 3538948
  116.5 68.7 %collective-permute-start.6 = (bf16[4,3,256,512]{3,2,1,0:T(8,128)(2,1)}, bf16[4,3,256,512]{3,2,1,0:T(8,128)(2,1)}, u32[]{:S(2)}, u32[]{:S(2)}) collective-permute-start(bf16[4,3,256,512]{3,2,1,0:T(8,128)(2,1)} %bitcast.14.refs_0_), channel_id=1, source_target_pairs={{0,4},{4,0},{8,12},{12,8},{16,20},{20,16},{24,28},{28,24},{1,5},{5... | collective-permute-start | bytes 9437192 | tf_op jit(solution)/shard_map/ppermute | solution.py:47
  156.3 33.2 %copy-start.35 = (bf16[512,2048]{1,0:T(8,128)(2,1)S(1)}, bf16[512,2048]{1,0:T(8,128)(2,1)}, u32[]{:S(2)}) copy-start(bf16[512,2048]{1,0:T(8,128)(2,1)} %param.32) | copy-start | bytes 6291460
  185.2 90.7 %collective-permute-start.10 = (bf16[4,256,2048]{2,1,0:T(8,128)(2,1)}, bf16[4,256,2048]{2,1,0:T(8,128)(2,1)}, u32[]{:S(2)}, u32[]{:S(2)}) collective-permute-start(bf16[4,256,2048]{2,1,0:T(8,128)(2,1)} %bitcast.208), channel_id=1, source_target_pairs={{0,4},{4,0},{8,12},{12,8},{16,20},{20,16},{24,28},{28,24},{1,5},{5... | collective-permute-start | bytes 12582920 | tf_op jit(solution)/shard_map/ppermute | solution.py:47
  200.1 77.5 %collective-permute-start.7 = (bf16[256,2048]{1,0:T(8,128)(2,1)}, bf16[256,2048]{1,0:T(8,128)(2,1)}, u32[]{:S(2)}, u32[]{:S(2)}) collective-permute-start(bf16[256,2048]{1,0:T(8,128)(2,1)} %constant_dynamic-slice_fusion.7), channel_id=1, source_target_pairs={{0,1},{1,0},{2,3},{3,2},{4,5},{5,4},{6,7},{7,6},{8,9},{9,8},{10,11... | collective-permute-start | bytes 3145736 | tf_op jit(solution)/shard_map/ppermute | solution.py:57
  226.1 55.0 %copy-start.27 = (bf16[768,512]{1,0:T(8,128)(2,1)}, bf16[768,512]{1,0:T(8,128)(2,1)S(1)}, u32[]{:S(2)}) copy-start(bf16[768,512]{1,0:T(8,128)(2,1)S(1)} %get-tuple-element.110.refs_1_) | copy-start | bytes 2359300
  226.1 146.0 %copy-start.14 = (bf16[768,512]{1,0:T(8,128)(2,1)}, bf16[768,512]{1,0:T(8,128)(2,1)S(1)}, u32[]{:S(2)}) copy-start(bf16[768,512]{1,0:T(8,128)(2,1)S(1)} %get-tuple-element.94.refs_1_.refs_3_) | copy-start | bytes 2359300
  275.9 96.2 %collective-permute-start.11 = (bf16[4,2048,256]{2,1,0:T(8,128)(2,1)}, bf16[4,2048,256]{2,1,0:T(8,128)(2,1)}, u32[]{:S(2)}, u32[]{:S(2)}) collective-permute-start(bf16[4,2048,256]{2,1,0:T(8,128)(2,1)} %bitcast.197), channel_id=1, source_target_pairs={{0,4},{4,0},{8,12},{12,8},{16,20},{20,16},{24,28},{28,24},{1,5},{5... | collective-permute-start | bytes 12582920 | tf_op jit(solution)/shard_map/ppermute | solution.py:47
  277.5 94.6 %all-gather.23.cloned.1.call-start = ((), (), s32[]{:S(2)}) async-start(), calls=%async_computation.16 | async-start | bytes 1310720 | tf_op jit(solution)/shard_map/all_gather | solution.py:66
  277.5 24.5 %copy-start.82 = (s32[8]{0:T(128)S(1)}, s32[8]{0:T(128)}, u32[]{:S(2)}) copy-start(s32[8]{0:T(128)} %param.37) | copy-start | bytes 100
  279.5 20.8 %collective-permute-start.8 = (bf16[256,2048]{1,0:T(8,128)(2,1)S(1)}, bf16[256,2048]{1,0:T(8,128)(2,1)}, u32[]{:S(2)}, u32[]{:S(2)}) collective-permute-start(bf16[256,2048]{1,0:T(8,128)(2,1)S(1)} %add_convert_fusion.15), channel_id=1, source_target_pairs={{0,2},{1,3},{2,0},{3,1},{4,6},{5,7},{6,4},{7,5},{8,10},{9,11},{10,... | collective-permute-start | bytes 3145736 | tf_op jit(solution)/shard_map/ppermute | solution.py:57
  281.1 403.1 %reduce-scatter.5.cloned.1.call-start = ((), (), s32[]{:S(2)}) async-start(), calls=%async_computation.8 | async-start | bytes 6553600 | tf_op jit(solution)/shard_map/reduce_scatter | solution.py:70
  302.0 6.7 collective-permute-start.9
  386.0 29.1 %copy-start.78 = (s32[8]{0:T(128)S(1)}, s32[8]{0:T(128)}, u32[]{:S(2)}) copy-start(s32[8]{0:T(128)} %param.36) | copy-start | bytes 100
  386.0 2.7 collective-permute-start.12
  389.2 25.4 %collective-permute-start.13 = (bf16[256,2048]{1,0:T(8,128)(2,1)S(1)}, bf16[256,2048]{1,0:T(8,128)(2,1)S(1)}, u32[]{:S(2)}, u32[]{:S(2)}) collective-permute-start(bf16[256,2048]{1,0:T(8,128)(2,1)S(1)} %add_convert_fusion.13), channel_id=1, source_target_pairs={{0,2},{1,3},{2,0},{3,1},{4,6},{5,7},{6,4},{7,5},{8,10},{9,11},{10,... | collective-permute-start | bytes 3145736 | tf_op jit(solution)/shard_map/ppermute | solution.py:57
  415.0 6.4 collective-permute-start.14
  426.6 39.2 %copy-start.33 = (f32[512,1]{1,0:T(8,128)}, f32[512,1]{1,0:T(8,128)S(1)}, u32[]{:S(2)}) copy-start(f32[512,1]{1,0:T(8,128)S(1)} %get-tuple-element.103.scale_ref) | copy-start | bytes 6148
  508.0 20.7 %copy-start.79 = (s32[8]{0:T(128)S(1)}, s32[8]{0:T(128)}, u32[]{:S(2)}) copy-start(s32[8]{0:T(128)} %param.35) | copy-start | bytes 100
  508.2 4.4 collective-permute-start.15
  512.6 29.9 %copy-start.3 = (bf16[768,2048]{1,0:T(8,128)(2,1)S(1)}, bf16[768,2048]{1,0:T(8,128)(2,1)}, u32[]{:S(2)}) copy-start(bf16[768,2048]{1,0:T(8,128)(2,1)} %copy-done.2) | copy-start | bytes 9437188
  513.9 25.6 %collective-permute-start.16 = (bf16[256,2048]{1,0:T(8,128)(2,1)}, bf16[256,2048]{1,0:T(8,128)(2,1)}, u32[]{:S(2)}, u32[]{:S(2)}) collective-permute-start(bf16[256,2048]{1,0:T(8,128)(2,1)} %add_convert_fusion.11), channel_id=1, source_target_pairs={{0,2},{1,3},{2,0},{3,1},{4,6},{5,7},{6,4},{7,5},{8,10},{9,11},{10,... | collective-permute-start | bytes 3145736 | tf_op jit(solution)/shard_map/ppermute | solution.py:57
  515.4 3.5 collective-permute-start.17
  519.0 3.6 collective-permute-start.18
  522.6 4.5 collective-permute-start.19
  542.4 4.4 collective-permute-start.20
  564.6 184.2 %reduce-scatter.11.cloned.1.call-start = ((), (), s32[]{:S(2)}) async-start(), calls=%async_computation.11 | async-start | bytes 3276800 | tf_op jit(solution)/shard_map/reduce_scatter | solution.py:70
  564.6 58.6 %collective-permute-start.21 = (bf16[4,1,1,256,1280]{4,3,2,1,0:T(8,128)(2,1)}, bf16[4,1,1,256,1280]{4,3,2,1,0:T(8,128)(2,1)S(1)}, u32[]{:S(2)}, u32[]{:S(2)}) collective-permute-start(bf16[4,1,1,256,1280]{4,3,2,1,0:T(8,128)(2,1)} %copy-done.25), channel_id=1, source_target_pairs={{0,4},{4,0},{8,12},{12,8},{16,20},{20,16},{24,28},{28,24},{1,5},{5... | collective-permute-start | bytes 7864328 | tf_op jit(solution)/shard_map/ppermute | solution.py:47
  625.4 175.3 %reduce-scatter.7.cloned.1.call-start = ((), (), s32[]{:S(2)}) async-start(), calls=%async_computation.9 | async-start | bytes 5242880 | tf_op jit(solution)/shard_map/reduce_scatter | solution.py:70
  625.4 91.6 %collective-permute-start.23 = (bf16[4,1,1,256,2048]{4,3,2,1,0:T(8,128)(2,1)}, bf16[4,1,1,256,2048]{4,3,2,1,0:T(8,128)(2,1)}, u32[]{:S(2)}, u32[]{:S(2)}) collective-permute-start(bf16[4,1,1,256,2048]{4,3,2,1,0:T(8,128)(2,1)} %grad_blocks.9), channel_id=1, source_target_pairs={{0,4},{4,0},{8,12},{12,8},{16,20},{20,16},{24,28},{28,24},{1,5},{5... | collective-permute-start | bytes 12582920 | tf_op jit(solution)/shard_map/ppermute | solution.py:47
  630.3 34.5 %slice-start.4 = ((s8[6291456]{0:T(1024)(128)(4,1)}), s8[2097152]{0:T(1024)(128)(4,1)S(1)}, s32[]{:S(2)}) async-start(s8[6291456]{0:T(1024)(128)(4,1)} %bitcast.206), calls=%async_computation.21 | async-start | bytes 4194304
  641.4 23.4 %slice-start.5 = ((s8[6291456]{0:T(1024)(128)(4,1)}), s8[4194304]{0:T(1024)(128)(4,1)S(1)}, s32[]{:S(2)}) async-start(s8[6291456]{0:T(1024)(128)(4,1)} %bitcast.206), calls=%async_computation.22 | async-start | bytes 8388608
  673.6 7.4 collective-permute-start.22
  724.8 167.4 %reduce-scatter.9.cloned.1.call-start = ((), (), s32[]{:S(2)}) async-start(), calls=%async_computation.10 | async-start | bytes 3932160 | tf_op jit(solution)/shard_map/reduce_scatter | solution.py:70
  724.9 68.2 %collective-permute-start.24 = (bf16[4,1,3,256,512]{4,3,2,1,0:T(8,128)(2,1)}, bf16[4,1,3,256,512]{4,3,2,1,0:T(8,128)(2,1)}, u32[]{:S(2)}, u32[]{:S(2)}) collective-permute-start(bf16[4,1,3,256,512]{4,3,2,1,0:T(8,128)(2,1)} %copy-done.24), channel_id=1, source_target_pairs={{0,4},{4,0},{8,12},{12,8},{16,20},{20,16},{24,28},{28,24},{1,5},{5... | collective-permute-start | bytes 9437192 | tf_op jit(solution)/shard_map/ppermute | solution.py:47
  741.0 56.6 %collective-permute-start.25 = (bf16[384,2048]{1,0:T(8,128)(2,1)}, bf16[384,2048]{1,0:T(8,128)(2,1)}, u32[]{:S(2)}, u32[]{:S(2)}) collective-permute-start(bf16[384,2048]{1,0:T(8,128)(2,1)} %add_convert_fusion.9), channel_id=1, source_target_pairs={{0,2},{1,3},{2,0},{3,1},{4,6},{5,7},{6,4},{7,5},{8,10},{9,11},{10,... | collective-permute-start | bytes 4718600 | tf_op jit(solution)/shard_map/ppermute | solution.py:57
  803.0 32.4 %collective-permute-start.29 = (bf16[384,2048]{1,0:T(8,128)(2,1)S(1)}, bf16[384,2048]{1,0:T(8,128)(2,1)}, u32[]{:S(2)}, u32[]{:S(2)}) collective-permute-start(bf16[384,2048]{1,0:T(8,128)(2,1)S(1)} %add_convert_fusion.8), channel_id=1, source_target_pairs={{0,1},{1,0},{2,3},{3,2},{4,5},{5,4},{6,7},{7,6},{8,9},{9,8},{10,11... | collective-permute-start | bytes 4718600 | tf_op jit(solution)/shard_map/ppermute | solution.py:57
  803.1 18.8 %collective-permute-start.32 = (bf16[256,1280]{1,0:T(8,128)(2,1)}, bf16[256,1280]{1,0:T(8,128)(2,1)}, u32[]{:S(2)}, u32[]{:S(2)}) collective-permute-start(bf16[256,1280]{1,0:T(8,128)(2,1)} %slice_bitcast_fusion.3), channel_id=1, source_target_pairs={{0,4},{4,0},{8,12},{12,8},{16,20},{20,16},{24,28},{28,24},{1,5},{5... | collective-permute-start | bytes 1966088 | tf_op jit(solution)/shard_map/ppermute | solution.py:47
  814.5 5.5 collective-permute-start.26
  820.2 14.2 %collective-permute-start.27 = (bf16[128,2048]{1,0:T(8,128)(2,1)S(1)}, bf16[128,2048]{1,0:T(8,128)(2,1)S(1)}, u32[]{:S(2)}, u32[]{:S(2)}) collective-permute-start(bf16[128,2048]{1,0:T(8,128)(2,1)S(1)} %add_convert_fusion.17), channel_id=1, source_target_pairs={{0,2},{1,3},{2,0},{3,1},{4,6},{5,7},{6,4},{7,5},{8,10},{9,11},{10,... | collective-permute-start | bytes 1572872 | tf_op jit(solution)/shard_map/ppermute | solution.py:57
  835.4 48.3 %collective-permute-start.28 = (bf16[128,2048]{1,0:T(8,128)(2,1)}, bf16[128,2048]{1,0:T(8,128)(2,1)}, u32[]{:S(2)}, u32[]{:S(2)}) collective-permute-start(bf16[128,2048]{1,0:T(8,128)(2,1)} %add_convert_fusion.16), channel_id=1, source_target_pairs={{0,1},{1,0},{2,3},{3,2},{4,5},{5,4},{6,7},{7,6},{8,9},{9,8},{10,11... | collective-permute-start | bytes 1572872 | tf_op jit(solution)/shard_map/ppermute | solution.py:57
  843.1 14.4 %collective-permute-start.33 = (f32[4,2048]{1,0:T(4,128)S(1)}, f32[4,2048]{1,0:T(4,128)S(1)}, u32[]{:S(2)}, u32[]{:S(2)}) collective-permute-start(f32[4,2048]{1,0:T(4,128)S(1)} %pad_maximum_fusion.9), channel_id=1, source_target_pairs={{0,1},{1,0},{2,3},{3,2},{4,5},{5,4},{6,7},{7,6},{8,9},{9,8},{10,11... | collective-permute-start | bytes 98312 | tf_op jit(solution)/shard_map/ppermute | solution.py:128
  857.6 6.9 collective-permute-start.34
  860.0 18.6 %all-to-all-start.2 = ((bf16[8,1,8,2048]{3,2,1,0:T(8,128)(2,1)}), bf16[8,1,8,2048]{3,2,1,0:T(8,128)(2,1)S(1)}, u32[]{:S(2)}, u32[]{:S(2)}) async-start(bf16[8,1,8,2048]{3,2,1,0:T(8,128)(2,1)} %fusion.25), calls=%async_computation.4 | async-start | bytes 524288 | tf_op jit(solution)/shard_map/all_to_all | solution.py:654
  864.5 12.6 %collective-permute-start.35 = (f32[4,2048]{1,0:T(4,128)S(1)}, f32[4,2048]{1,0:T(4,128)S(1)}, u32[]{:S(2)}, u32[]{:S(2)}) collective-permute-start(f32[4,2048]{1,0:T(4,128)S(1)} %fusion.75), channel_id=1, source_target_pairs={{0,4},{4,0},{8,12},{12,8},{16,20},{20,16},{24,28},{28,24},{1,5},{5... | collective-permute-start | bytes 98312 | tf_op jit(solution)/shard_map/ppermute | solution.py:128
  877.1 9.2 %collective-permute-start.36 = (f32[4,2048]{1,0:T(4,128)S(1)}, f32[4,2048]{1,0:T(4,128)S(1)}, u32[]{:S(2)}, u32[]{:S(2)}) collective-permute-start(f32[4,2048]{1,0:T(4,128)S(1)} %add.383), channel_id=1, source_target_pairs={{0,8},{4,12},{8,0},{12,4},{16,24},{20,28},{24,16},{28,20},{1,9},{5... | collective-permute-start | bytes 98312 | tf_op jit(solution)/shard_map/ppermute | solution.py:128
  880.0 12.2 %all-to-all-start.3 = ((bf16[8,1,8,2048]{3,2,1,0:T(8,128)(2,1)}), bf16[8,1,8,2048]{3,2,1,0:T(8,128)(2,1)S(1)}, u32[]{:S(2)}, u32[]{:S(2)}) async-start(bf16[8,1,8,2048]{3,2,1,0:T(8,128)(2,1)} %fusion.26), calls=%async_computation.5 | async-start | bytes 524288 | tf_op jit(solution)/shard_map/all_to_all | solution.py:655
  886.4 9.2 collective-permute-start.37
  892.2 6.8 collective-permute-start.30
  900.3 6.5 collective-permute-start.31
  (76 other events, 414.3 us)
Sparse Core Ops, SparseCore 0:
  9.6 87.2 all-gather.14
  98.5 79.7 all-gather.16
  179.9 79.2 all-gather.18
  277.6 26.4 all-gather.20
  305.5 27.4 all-gather.22
  564.7 92.7 reduce-scatter.4
  659.8 52.6 reduce-scatter.10
  724.9 75.7 reduce-scatter.6
  803.1 60.7 reduce-scatter.8
